TPU v7x, 512 devices: a whole 4x4x16 slice. The times are simulated.
512 devices in a mesh: seq: 16 (over y, x), exp: 32 (over z, core).
Axes of the slice: x: 4, y: 4, z: 16, core: 2. Of those that a mesh axis runs over, the one named last changes fastest.
Arguments:
- queries: bfloat16 [2048, 64, 128], P('seq', 'exp'), may hold values from -18 to 18
- cache: bfloat16 [4096, 4, 2, 128], P('seq'), may hold values from -4 to 4
- new_key_value: bfloat16 [2048, 4, 2, 128], P('seq'), may hold values from -4 to 4
- out_proj: bfloat16 [8192, 4096], P('exp', 'seq'), may hold values from -0.0625 to 0.0625
- residual: bfloat16 [2048, 4096], P('seq', 'exp'), may hold values from -3 to 3
- norm_gain: float32 [4096], replicated, may hold values from 0.1 to 1.9
- expert_ids: int32 [2048, 8], P('seq'), may hold values from 0 to 63, all different within a row; in each aligned block of 128 rows (0 to 127, 128 to 255, ...) at most 20 rows name the same one
- gates: float32 [2048, 8], P('seq'), may hold values from 0.05 to 0.5
- w_gate_up: bfloat16 [64, 4096, 1536], P('exp', 'seq'), may hold values from -0.09375 to 0.09375
- w_down: bfloat16 [64, 768, 4096], P('exp', None, 'seq'), may hold values from -0.21875 to 0.21875
Outputs:
- mixed: bfloat16 [2048, 4096], P(('seq', 'exp'))
Inputs may be any that keep to these rules, and one draw needn't show every extreme that they name: `expert_ids`: within each row of 128 consecutive new tokens, at most 20 tokens name one expert, a bound that some row reaches; each token names 8 different experts.
All inputs are finite; a program needn't handle non-finite values.
Results may differ from a plain program's by a relative error of at most 0.039.
Values may be sent and summed in bfloat16 or wider, within the bound.
No kernel may reach another device: no remote copies, remote signals or barrier semaphores. Data moves between devices by JAX's collectives and lax.ppermute only.
A program may use at most 64 MiB of HBM per device.

v0:
```python
import math

import jax
import jax.numpy as jnp
from jax import lax
from jax.sharding import PartitionSpec as P

QUERY_HEADS = 64
KEY_VALUE_HEADS = 4


floor_score = -1e30


def key_positions(global_rows, span_rows, cache_rows, query_count):
    shard_number = global_rows // span_rows
    within_shard = global_rows % span_rows
    return jnp.where(
        within_shard < cache_rows, -1, shard_number * query_count + within_shard - cache_rows
    )


def softmax_update(query_rows, key_block, value_block, visible, state_in, scale_factor):
    running_top, running_sum, running_acc = state_in
    scores = jnp.dot(query_rows, key_block.T, preferred_element_type=jnp.float32) * scale_factor
    scores = jnp.where(visible, scores, floor_score)
    new_top = jnp.maximum(running_top, jnp.max(scores, axis=1))
    shrink = jnp.exp(running_top - new_top)
    probs = jnp.where(visible, jnp.exp(scores - new_top[:, None]), 0.0)
    running_sum = running_sum * shrink + jnp.sum(probs, axis=1)
    running_acc = running_acc * shrink[:, None] + jnp.dot(
        probs.astype(jnp.bfloat16), value_block, preferred_element_type=jnp.float32
    )
    return (new_top, running_sum, running_acc)


def empty_state(row_count, head_width):
    return (
        jnp.full((row_count,), floor_score, jnp.float32),
        jnp.zeros((row_count,), jnp.float32),
        jnp.zeros((row_count, head_width), jnp.float32),
    )


def local(
    queries,
    cache,
    new_key_value,
    out_proj,
    residual,
    norm_gain,
    expert_ids,
    gates,
    w_gate_up,
    w_down,
):
    exp_count = lax.axis_size("exp")
    seq_index = lax.axis_index("seq")
    expert_index = lax.axis_index("exp")
    query_count, head_total, head_width = queries.shape
    cache_rows = cache.shape[0]
    scale_factor = 1.0 / math.sqrt(head_width)
    key_value_group = expert_index * head_total // (QUERY_HEADS // KEY_VALUE_HEADS)
    own_cache = lax.dynamic_index_in_dim(cache, key_value_group, 1, keepdims=False)
    own_fresh = lax.dynamic_index_in_dim(new_key_value, key_value_group, 1, keepdims=False)
    local_kv = jnp.concatenate([own_cache, own_fresh], axis=0)
    span_rows = cache_rows + query_count
    row_count = query_count * head_total
    query_rows = queries.reshape(row_count, head_width)
    head_of_row = jnp.arange(row_count, dtype=jnp.int32) // head_total
    own_query_pos = seq_index * query_count + head_of_row
    shard_piece = lax.all_gather(local_kv, "seq", axis=0, tiled=True)
    piece_rows = shard_piece.shape[0]
    block_rows = 512

    def one_block(inner_state, offset_row):
        kv_block = lax.dynamic_slice_in_dim(shard_piece, offset_row, block_rows, 0)
        key_pos = key_positions(
            offset_row + jnp.arange(block_rows, dtype=jnp.int32), span_rows, cache_rows, query_count
        )
        visible = key_pos[None, :] <= own_query_pos[:, None]
        return (
            softmax_update(
                query_rows, kv_block[:, 0], kv_block[:, 1], visible, inner_state, scale_factor
            ),
            None,
        )

    offsets = jnp.arange(piece_rows // block_rows, dtype=jnp.int32) * block_rows
    state_out, _ = lax.scan(one_block, empty_state(row_count, head_width), offsets)
    running_top, running_sum, running_acc = state_out
    attended = (running_acc / running_sum[:, None]).astype(jnp.bfloat16)
    flat_heads = attended.reshape(query_count, head_total * head_width)
    head_part = jnp.dot(
        flat_heads,
        lax.all_gather(out_proj, "seq", axis=1, tiled=True),
        preferred_element_type=jnp.float32,
    )
    model_width = head_part.shape[1]
    head_sum = lax.psum(head_part.astype(jnp.bfloat16), "exp").astype(jnp.float32)
    full_residual = lax.all_gather(residual, "exp", axis=1, tiled=True)
    hidden_state = (full_residual.astype(jnp.float32) + head_sum).astype(jnp.bfloat16)
    state_f = hidden_state.astype(jnp.float32)
    mean_square = jnp.mean(state_f * state_f, axis=1, keepdims=True)
    normed = (state_f * lax.rsqrt(mean_square + 1e-06) * norm_gain).astype(jnp.bfloat16)
    local_experts = w_gate_up.shape[0]
    hidden_units = w_down.shape[1]
    top_k = expert_ids.shape[1]
    capacity = 5 * query_count * top_k // (4 * local_experts * exp_count)
    slot_range = jnp.arange(capacity, dtype=jnp.int32)
    select_tables = []
    token_weights = []
    dispatched = []
    for member in range(local_experts):
        expert = expert_index * local_experts + member
        chosen = expert_ids == expert
        taken = jnp.sum(chosen.astype(jnp.int32), axis=1)
        weight = jnp.sum(jnp.where(chosen, gates, 0.0), axis=1)
        slot = jnp.cumsum(taken) - taken
        select = ((slot[None, :] == slot_range[:, None]) & (taken[None, :] > 0)).astype(
            jnp.bfloat16
        )
        select_tables.append(select)
        token_weights.append(weight)
        dispatched.append(
            jnp.dot(select, normed, preferred_element_type=jnp.float32).astype(jnp.bfloat16)
        )
    outgoing = jnp.stack(dispatched, axis=1)
    incoming = lax.all_to_all(outgoing, "seq", split_axis=2, concat_axis=0, tiled=True)
    gate_up = lax.psum(
        jnp.einsum("rlk,lkf->rlf", incoming, w_gate_up, preferred_element_type=jnp.float32).astype(
            jnp.bfloat16
        ),
        "seq",
    ).astype(jnp.float32)
    activation = (jax.nn.silu(gate_up[..., :hidden_units]) * gate_up[..., hidden_units:]).astype(
        jnp.bfloat16
    )
    expert_out = jnp.einsum(
        "rlf,lfk->rlk", activation, w_down, preferred_element_type=jnp.float32
    ).astype(jnp.bfloat16)
    returned = lax.all_to_all(expert_out, "seq", split_axis=0, concat_axis=2, tiled=True)
    combined = jnp.zeros((query_count, model_width), jnp.float32)
    for member in range(local_experts):
        picked = jnp.einsum(
            "cq,cd->qd",
            select_tables[member],
            returned[:, member],
            preferred_element_type=jnp.float32,
        )
        combined = combined + token_weights[member][:, None] * picked
    token_part = lax.psum_scatter(
        combined.astype(jnp.bfloat16), "exp", scatter_dimension=0, tiled=True
    ).astype(jnp.float32)
    own_count = token_part.shape[0]
    own_rows = lax.dynamic_slice_in_dim(hidden_state, expert_index * own_count, own_count, 0)
    return (own_rows.astype(jnp.float32) + token_part).astype(jnp.bfloat16)


def solution(mesh):
    in_specs = (
        P("seq", "exp", None),
        P("seq", None, None, None),
        P("seq", None, None, None),
        P("exp", "seq"),
        P("seq", "exp"),
        P(),
        P("seq", None),
        P("seq", None),
        P("exp", "seq", None),
        P("exp", None, "seq"),
    )
    out_specs = P(("seq", "exp"), None)
    return jax.shard_map(local, mesh=mesh, in_specs=in_specs, out_specs=out_specs, check_vma=False)
```

profile of v0, /device:TPU:1, one launch (start us, length us, event | category | flops | bytes accessed | tf_op | source)
XLA Modules:
  0.0 818.5 jit_solution(13226865057687671086)
XLA Ops:
  10.9 67.8 %all-gather.6.cloned.1.call-done = bf16[6144,2,128]{2,0,1:T(8,128)(2,1)} async-done(((bf16[384,2,128]{2,0,1:T(8,128)(2,1)}), bf16[6144,2,128]{2,0,1:T(8,128)(2,1)}) %all-gather.6.cloned.1.call-update) | async-done | bytes 3145744 | tf_op jit(solution)/shard_map/all_gather | solution.py:72
  78.7 67.7 %while.17 = (s32[]{:T(128)}, f32[256]{0:T(256)S(1)}, f32[256]{0:T(256)S(1)}, f32[256,128]{1,0:T(8,128)S(1)}, s32[12]{0:T(128)S(1)}, /*index=5*/bf16[6144,2,128]{...) while((s32[]{:T(128)}, f32[256]{0:T(256)S(1)}, ...), condition=%wide.region_3.4_spmd.clone, body=%wide.region_0.3_spmd.clone.sunk | while | flops 68792832 | bytes 2191575 | solution.py:90
  94.2 1.3 convolution_add_fusion.2
  105.5 1.3 convolution_add_fusion.2
  116.8 1.3 convolution_add_fusion.2
  133.7 1.3 convolution_add_fusion.2
  139.4 1.3 convolution_add_fusion.2
  146.5 3.1 convolution_convert_fusion
  150.5 65.5 %all-gather.4.cloned.1.call-done = bf16[128,4096]{1,0:T(8,128)(2,1)} async-done(((bf16[128,128]{1,0:T(8,128)(2,1)}), bf16[128,4096]{1,0:T(8,128)(2,1)}) %all-gather.4.cloned.1.call-update) | async-done | bytes 1048592 | tf_op jit(solution)/shard_map/all_gather | solution.py:101
  216.0 207.7 %all-reduce.5.cloned.1.call-done = bf16[128,4096]{1,0:T(8,128)(2,1)} async-done(((bf16[128,4096]{1,0:T(8,128)(2,1)}), bf16[128,4096]{1,0:T(8,128)(2,1)}) %all-reduce.5.cloned.1.call-update) | async-done | bytes 1048592 | tf_op jit(solution)/shard_map/psum | solution.py:100
  423.7 2.0 fusion.27
  426.7 3.9 copy.27
  430.6 6.8 reshape.119
  437.4 15.1 %all_to_all.36 = bf16[16,2,5120]{2,1,0:T(2,128)(2,1)S(1)} all-to-all(bf16[16,2,5120]{2,1,0:T(2,128)(2,1)S(1)} %reshape.119), channel_id=1, replica_groups=mesh['seq'=16,'exp'=32] {'seq'}, dimensions={0} | all-to-all | bytes 655360 | tf_op jit(solution)/shard_map/all_to_all | solution.py:129
  452.5 6.2 reshape.120
  458.7 3.3 copy.33
  462.3 2.0 fusion.26
  464.3 115.4 %all-reduce.7.cloned.1.call-done = bf16[320,2,1536]{2,0,1:T(8,128)(2,1)} async-done(((bf16[320,2,1536]{2,0,1:T(8,128)(2,1)}), bf16[320,2,1536]{2,0,1:T(8,128)(2,1)}) %all-reduce.7.cloned.1.call-update) | async-done | bytes 1966096 | tf_op jit(solution)/shard_map/psum | solution.py:130
  579.7 2.1 convert_element_type.85
  583.6 4.5 all-to-all-start.1
  588.1 7.8 all-to-all-done.1
  597.5 1.5 fusion.23
  601.0 209.2 %all-reduce.9.cloned.1.call-done = bf16[128,4096]{1,0:T(8,128)(2,1)} async-done(((bf16[128,4096]{1,0:T(8,128)(2,1)}), bf16[128,4096]{1,0:T(8,128)(2,1)}) %all-reduce.9.cloned.1.call-update) | async-done | bytes 1048592
  810.1 1.5 add_convert_fusion.1
  (159 shorter events, 50.8 us)
Async XLA Ops:
  6.5 455.8 %copy-start = (bf16[2,256,1536]{2,1,0:T(8,128)(2,1)S(1)}, bf16[2,256,1536]{2,1,0:T(8,128)(2,1)}, u32[]{:S(2)}) copy-start(bf16[2,256,1536]{2,1,0:T(8,128)(2,1)} %param.20) | copy-start | bytes 4718596
  6.5 72.1 %all-gather.6.cloned.1.call-start = ((), (), s32[]{:S(2)}) async-start(), calls=%async_computation.3 | async-start | bytes 3342336 | tf_op jit(solution)/shard_map/all_gather | solution.py:72
  9.3 137.2 %all-gather.8.cloned.1.call-start = ((), (), s32[]{:S(2)}) async-start(), calls=%async_computation.4 | async-start | bytes 2228224 | tf_op jit(solution)/shard_map/all_gather | solution.py:96
  10.1 206.0 %all-gather.4.cloned.1.call-start = ((), (), s32[]{:S(2)}) async-start(), calls=%async_computation.2 | async-start | bytes 1081344 | tf_op jit(solution)/shard_map/all_gather | solution.py:101
  10.8 412.9 %all-reduce.5.cloned.1.call-start = ((), (), s32[]{:S(2)}) async-start(), calls=%async_computation.5 | async-start | bytes 2097152 | tf_op jit(solution)/shard_map/psum | solution.py:100
  146.5 3.2 copy-start.2
  149.6 276.1 %copy-start.4 = (f32[4096]{0:T(1024)S(1)}, f32[4096]{0:T(1024)}, u32[]{:S(2)}) copy-start(f32[4096]{0:T(1024)} %param.17) | copy-start | bytes 49156
  149.6 430.1 %all-reduce.7.cloned.1.call-start = ((), (), s32[]{:S(2)}) async-start(), calls=%async_computation.6 | async-start | bytes 3932160 | tf_op jit(solution)/shard_map/psum | solution.py:130
  579.7 2.1 copy-start.3
  581.8 6.3 copy-start.1
  583.6 12.4 %all-to-all-start.1 = ((bf16[320,2,256]{2,1,0:T(2,128)(2,1)}), bf16[320,2,256]{2,1,0:T(2,128)(2,1)S(1)}, u32[]{:S(2)}, u32[]{:S(2)}) async-start(bf16[320,2,256]{2,1,0:T(2,128)(2,1)} %copy.31), calls=%async_computation.1 | async-start | bytes 655360 | tf_op jit(solution)/shard_map/all_to_all | solution.py:142
  588.0 222.1 %all-reduce.9.cloned.1.call-start = ((), (), s32[]{:S(2)}) async-start(), calls=%async_computation.7 | async-start | bytes 2097152
Sparse Core Ops, SparseCore 0:
  10.4 68.2 all-gather.5
  81.6 61.2 all-gather.7
  145.0 70.9 all-gather.3
  218.2 205.4 all-reduce.4
  464.4 115.2 all-reduce.6
  599.2 210.9 all-reduce.8
where the time goes:
time: 820 us; the launch traced here: 818 us
  waiting for transfers between devices  675 us (82%)
  matrix products  38.6 us (5%)
  local copies, waits for them, and re-layouts  33.2 us (4%)
  loops' own time  21.3 us (3%)
  other arithmetic  16.4 us (2%)
  blocking collectives  15.1 us (2%)
  between operations  14.4 us (2%)
    unnamed x7, waiting for transfers between devices  211 us
    psum x1, waiting for transfers between devices, local(): lax.psum(head_part.astype(jnp.bfloat16), 'exp').astype(jnp.float32)  208 us
    psum x1, waiting for transfers between devices, local(): lax.psum(jnp.einsum('rlk,lkf->rlf', incoming, w_gate_up, preferred_elemen...  115 us
    all_gather x1, waiting for transfers between devices, local(): shard_piece = lax.all_gather(local_kv, 'seq', axis=0, tiled=True)  67.8 us
    all_gather x1, waiting for transfers between devices, local(): full_residual = lax.all_gather(residual, 'exp', axis=1, tiled=True)  65.5 us
    another operation x1, loops' own time, local(): lax.scan(one_block, empty_state(row_count, head_width), offsets)  21.3 us
  transfers between devices with their start and end apart: 7, of which 6 were waited for; matrix products, arithmetic and copies ran while one was open for 6% of the time, Pallas kernels for 0%

commit v1 on v0

v1 whole, which is shorter than its diff:
```python
import functools
import math

import jax
import jax.numpy as jnp
from jax import lax
from jax.experimental import pallas as pl
from jax.experimental.pallas import tpu as pltpu
from jax.sharding import PartitionSpec as P

QUERY_HEADS = 64
KEY_VALUE_HEADS = 4
FLOOR = -1e30
VMEM_BYTES = 56 * 1024 * 1024
f32 = jnp.float32
bf16 = jnp.bfloat16


def run(body, out_shape, *operands, place=None, flops=0, moved=0, scratch=(), name=None):
    vmem = pl.BlockSpec(memory_space=pltpu.VMEM)
    smem = pl.BlockSpec(memory_space=pltpu.SMEM)
    placed = [] if place is None else [place]
    return pl.pallas_call(
        body,
        out_shape=out_shape,
        in_specs=[smem] * len(placed) + [vmem] * len(operands),
        out_specs=jax.tree.map(lambda _: vmem, out_shape),
        scratch_shapes=list(scratch),
        compiler_params=pltpu.CompilerParams(vmem_limit_bytes=VMEM_BYTES),
        cost_estimate=pl.CostEstimate(flops=flops, bytes_accessed=moved, transcendentals=0),
        name=name,
    )(*placed, *operands)


def shape(dims, dtype=bf16):
    return jax.ShapeDtypeStruct(dims, dtype)


def attend_half(place_ref, q_ref, kv_ref, *refs, first, rows, cached, fresh, scale):
    if first:
        top_ref, sum_ref, acc_ref, s_ref = refs
    else:
        top_in, sum_in, acc_in, extra_ref, out_ref, s_ref = refs
    shards, _, span, width = kv_ref.shape
    heads = q_ref.shape[0]
    seq_index, half = place_ref[0], place_ref[1]
    total = heads * rows
    q = q_ref[...].reshape(total, width)
    per = 4
    wide = per * span
    lane = lax.broadcasted_iota(jnp.int32, (1, wide), 1)
    query_pos = seq_index * rows + lax.broadcasted_iota(jnp.int32, (total, 1), 0) % rows
    top = jnp.full((total, 128), FLOOR, f32)
    for part in range(shards // per):
        keys = kv_ref[part * per : (part + 1) * per, 0].reshape(wide, width)
        s = lax.dot_general(q, keys, (((1,), (1,)), ((), ())), preferred_element_type=f32)
        within = lane % span
        pos = (part * per + lane // span) * rows + half * fresh + within - cached
        pos = jnp.where(within < cached, -1, pos)
        s = jnp.where(pos <= query_pos, s, FLOOR)
        s_ref[:, part * wide : (part + 1) * wide] = s
        for k in range(wide // 128):
            top = jnp.maximum(top, s[:, k * 128 : (k + 1) * 128])
    top = jnp.max(top, axis=1, keepdims=True)
    factor = scale * math.log2(math.e)
    if first:
        new_top = top
    else:
        old_top = top_in[:, 0:1]
        new_top = jnp.maximum(top, old_top)
    acc = jnp.zeros((total, width), f32)
    sums = jnp.zeros((total, 128), f32)
    for part in range(shards // per):
        values = kv_ref[part * per : (part + 1) * per, 1].reshape(wide, width)
        p = jnp.exp2((s_ref[:, part * wide : (part + 1) * wide] - new_top) * factor)
        for k in range(wide // 128):
            sums = sums + p[:, k * 128 : (k + 1) * 128]
        acc = acc + jnp.dot(p.astype(bf16), values, preferred_element_type=f32)
    row_sum = jnp.sum(sums, axis=1, keepdims=True)
    if first:
        top_ref[...] = jnp.broadcast_to(new_top, (total, 128))
        sum_ref[...] = jnp.broadcast_to(row_sum, (total, 128))
        acc_ref[...] = acc
    else:
        shrink = jnp.exp2((old_top - new_top) * factor)
        row_sum = row_sum + sum_in[:, 0:1] * shrink
        acc = acc + acc_in[...] * shrink
        attended = (acc / row_sum).astype(bf16)
        extra = extra_ref[...]
        for k in range(out_ref.shape[0]):
            for h in range(heads):
                out_ref[k, 0:rows, h * width : (h + 1) * width] = attended[h * rows : (h + 1) * rows]
            out_ref[k, rows:, :] = extra


def project(place_ref, got_ref, w_ref, keep_ref, send_ref, table_ref, *, rows):
    shards = got_ref.shape[0]
    half = place_ref[1]
    w = w_ref[...]
    width = w.shape[1] // 2
    group = 4
    for g in range(shards // group):
        x = got_ref[g * group : (g + 1) * group, 0:rows, :].reshape(group * rows, w.shape[0])
        y = jnp.dot(x, w, preferred_element_type=f32)
        low, high = y[:, :width], y[:, width:]
        keep = jnp.where(half == 0, low, high).astype(bf16)
        send = jnp.where(half == 0, high, low).astype(bf16)
        keep_ref[g * group : (g + 1) * group] = keep.reshape(group, rows, width)
        send_ref[g * group : (g + 1) * group] = send.reshape(group, rows, width)
    for j in range(shards // 2):
        table_ref[j] = got_ref[2 * j, rows:, :].astype(f32) + got_ref[2 * j + 1, rows:, :].astype(f32)


def add_state(got_ref, residual_ref, out_ref):
    total = residual_ref[...].astype(f32)
    for k in range(got_ref.shape[0]):
        total = total + got_ref[k].astype(f32)
    out_ref[...] = total.astype(bf16)


def dispatch(place_ref, own_ref, other_ref, ids_ref, state_ref, out_ref, *, capacity):
    half = place_ref[1]
    own, other = own_ref[...], other_ref[...]
    low = jnp.where(half == 0, own.astype(f32), other.astype(f32)).astype(bf16)
    high = jnp.where(half == 0, other.astype(f32), own.astype(f32)).astype(bf16)
    state = jnp.concatenate([low, high], axis=1)
    state_ref[...] = state
    tokens = own.shape[0]
    chips = out_ref.shape[0] // (2 * capacity)
    ids = ids_ref[...].astype(f32).astype(jnp.int32)
    before = (
        lax.broadcasted_iota(jnp.int32, (tokens, tokens), 0)
        < lax.broadcasted_iota(jnp.int32, (tokens, tokens), 1)
    ).astype(f32).astype(bf16)
    codes = []
    for member in range(2):
        expert = lax.broadcasted_iota(jnp.int32, (chips, tokens), 0) * 4 + 2 * half + member
        taken = jnp.zeros((chips, tokens), f32)
        for k in range(ids.shape[0]):
            taken = taken + (expert == ids[k : k + 1, :]).astype(f32)
        slot = jnp.dot(taken.astype(bf16), before, preferred_element_type=f32)
        codes.append(jnp.where(taken > 0, slot.astype(jnp.int32) + member * capacity, -1))
    slots = lax.broadcasted_iota(jnp.int32, (chips, 2 * capacity, tokens), 1)
    chosen = (codes[0][:, None, :] == slots) | (codes[1][:, None, :] == slots)
    select = chosen.astype(f32).reshape(chips * 2 * capacity, tokens).astype(bf16)
    out_ref[...] = jnp.dot(select, state, preferred_element_type=f32).astype(bf16)


def gate_up(x_ref, gain_ref, w_ref, out_ref, *, capacity):
    slots = x_ref.shape[0]
    columns = w_ref.shape[2]
    x = x_ref[...].astype(f32)
    squares = jnp.sum(x * x, axis=1, keepdims=True)
    scaled = (x * gain_ref[...]).astype(bf16)
    second = lax.broadcasted_iota(jnp.int32, (slots, 1), 0) % (2 * capacity) >= capacity
    step = 256
    for k in range(columns // step):
        cut = slice(k * step, (k + 1) * step)
        a = jnp.dot(scaled, w_ref[0, :, cut], preferred_element_type=f32)
        b = jnp.dot(scaled, w_ref[1, :, cut], preferred_element_type=f32)
        out_ref[:, cut] = jnp.where(second, b, a).astype(bf16)
    high = squares.astype(bf16).astype(f32)
    lane = lax.broadcasted_iota(jnp.int32, (slots, 128), 1)
    out_ref[:, columns:] = jnp.where(lane < 64, high, squares - high).astype(bf16)


def activate(got_ref, out_ref, *, features):
    blocks, slots, columns = got_ref.shape
    hidden = (columns - 128) // 2

    def total(start, size):
        value = got_ref[0, :, start : start + size].astype(f32)
        for k in range(1, blocks):
            value = value + got_ref[k, :, start : start + size].astype(f32)
        return value

    pieces = total(2 * hidden, 128)
    squares = pieces[:, 0:1] + pieces[:, 64:65]
    norm = lax.rsqrt(squares / features + 1e-6)
    for start in range(0, hidden, 128):
        gate = total(start, 128) * norm
        up = total(hidden + start, 128) * norm
        value = (gate / (1.0 + jnp.exp(-gate)) * up).astype(bf16)
        for k in range(out_ref.shape[0]):
            out_ref[k, :, start : start + 128] = value


def combine(place_ref, x_ref, w_ref, table_ref, state_ref, keep_ref, send_ref, *, capacity):
    half, chip = place_ref[1], place_ref[2]
    pairs = table_ref.shape[0]
    slots = 2 * 2 * capacity
    tokens = state_ref.shape[0]
    width = w_ref.shape[2]
    chips = keep_ref.shape[0]
    size = 2 * tokens
    x = x_ref[...]
    second = lax.broadcasted_iota(jnp.int32, (x.shape[0], 1), 0) % (2 * capacity) >= capacity
    y = jnp.where(
        second,
        jnp.dot(x, w_ref[1], preferred_element_type=f32),
        jnp.dot(x, w_ref[0], preferred_element_type=f32),
    )
    place = lax.broadcasted_iota(jnp.int32, (size, tokens), 0)
    token = (place % tokens // 8) * 8 + place // tokens * 4 + place % 4
    mine = ((place % 8 // 4) == chip % 2) & (place // tokens == half)
    column = lax.broadcasted_iota(jnp.int32, (size, tokens), 1)
    own = jnp.dot(
        ((token == column) & mine).astype(f32).astype(bf16), state_ref[...], preferred_element_type=f32
    )
    slot = lax.broadcasted_iota(jnp.int32, (slots, size), 0) + 1
    for j in range(pairs):
        table = table_ref[j]
        code = table.astype(jnp.int32)
        hit_a = slot == code[0:1, :]
        hit_b = slot == code[1:2, :]
        weight_a = table[2:3, :] + table[3:4, :] + table[4:5, :]
        weight_b = table[5:6, :] + table[6:7, :] + table[7:8, :]
        weight = jnp.where(hit_a, weight_a, 0.0) + jnp.where(hit_b, weight_b, 0.0)
        weight = jnp.sum(weight, axis=1, keepdims=True)
        rows = (y[j * slots : (j + 1) * slots] * weight).astype(bf16)
        select = (hit_a | hit_b).astype(f32).astype(bf16)
        part = lax.dot_general(select, rows, (((0,), (0,)), ((), ())), preferred_element_type=f32)
        part = part + jnp.where(j == chip // 2, own, 0.0)
        low, high = part[:tokens], part[tokens:]
        keep = jnp.where(half == 0, low, high).astype(bf16)
        send = jnp.where(half == 0, high, low).astype(bf16)
        keep_ref[:, j * 8 : (j + 1) * 8, :] = keep.reshape(chips, 8, width)
        send_ref[:, j * 8 : (j + 1) * 8, :] = send.reshape(chips, 8, width)


def local(
    queries,
    cache,
    new_key_value,
    out_proj,
    residual,
    norm_gain,
    expert_ids,
    gates,
    w_gate_up,
    w_down,
):
    n_seq, n_exp = lax.axis_size("seq"), lax.axis_size("exp")
    n_chip = n_exp // 2
    seq_index, exp_index = lax.axis_index("seq"), lax.axis_index("exp")
    core, chip = exp_index % 2, exp_index // 2
    place = jnp.stack([seq_index, core, chip]).astype(jnp.int32)
    other_place = jnp.stack([seq_index, 1 - core, chip]).astype(jnp.int32)
    rows, heads, width = queries.shape
    top_k = expert_ids.shape[1]
    features = norm_gain.shape[0]
    members, feature_block, gate_columns = w_gate_up.shape
    hidden_units = w_down.shape[1]
    capacity = 5 * rows * top_k // (4 * members * n_exp)
    swap = [(i, i ^ 1) for i in range(n_exp)]
    chips = [[2 * z + c for z in range(n_chip)] for c in range(2)]
    turn = [
        (s * n_exp + e, (e // 2) * n_exp + 2 * s + e % 2) for s in range(n_seq) for e in range(n_exp)
    ]

    def over_chips(value):
        return lax.all_to_all(value, "exp", 0, 0, tiled=True, axis_index_groups=chips)

    def over_seq(value):
        return lax.all_to_all(value, "seq", 0, 0, tiled=True)

    with jax.named_scope("turn_residual"):
        packed = jnp.concatenate([residual, expert_ids.T.astype(bf16)], axis=0)
        turned = lax.ppermute(packed, ("seq", "exp"), turn)

    with jax.named_scope("key_values"):
        group = exp_index * heads // (QUERY_HEADS // KEY_VALUE_HEADS)
        cached, fresh = cache.shape[0] // 2, rows // 2
        own_cache = lax.dynamic_slice(
            cache, (core * cached, group, 0, 0), (cached, 1, 2, width)
        ).reshape(cached, 2, width)
        own_fresh = lax.dynamic_slice(
            new_key_value, (core * fresh, group, 0, 0), (fresh, 1, 2, width)
        ).reshape(fresh, 2, width)
        own_kv = jnp.concatenate([own_cache, own_fresh], axis=0).transpose(1, 0, 2)
        half_kv = over_seq(jnp.broadcast_to(own_kv[None], (n_seq,) + own_kv.shape))
        other_kv = lax.ppermute(half_kv, "exp", swap)

    with jax.named_scope("tables"):
        lines = []
        weights = []
        for member in range(2):
            chosen = expert_ids == exp_index * 2 + member
            taken = jnp.sum(chosen.astype(jnp.int32), axis=1)
            slot = jnp.cumsum(taken) - taken
            code = slot + member * capacity + (seq_index % 2) * 2 * capacity + 1
            lines.append(jnp.where(taken > 0, code, 0).astype(f32))
            weight = jnp.sum(jnp.where(chosen, gates, 0.0), axis=1)
            first = lax.reduce_precision(weight, 8, 7)
            second = lax.reduce_precision(weight - first, 8, 7)
            weights += [first, second, weight - first - second]
        table = jnp.stack(lines + weights).reshape(8, n_chip, 2, 1, 4).transpose(0, 2, 1, 3, 4)
        spot = (jnp.arange(2) == seq_index % 2).astype(f32).reshape(1, 1, 1, 2, 1)
        extra = (table * spot).reshape(8, 2 * rows).astype(bf16)

    with jax.named_scope("attention"):
        q = queries.transpose(1, 0, 2)
        total = rows * heads
        span = cached + fresh
        half_attend = functools.partial(
            attend_half, rows=rows, cached=cached, fresh=fresh, scale=1.0 / math.sqrt(width)
        )
        flops = 4 * total * n_seq * span * width
        scores = pltpu.VMEM((total, n_seq * span), f32)
        state = run(
            functools.partial(half_attend, first=True),
            [shape((total, 128), f32), shape((total, 128), f32), shape((total, width), f32)],
            q,
            half_kv,
            place=place,
            flops=flops,
            moved=half_kv.size * 2,
            scratch=[scores],
            name="attend_first",
        )
        attended = run(
            functools.partial(half_attend, first=False),
            shape((n_seq, rows + 8, heads * width)),
            q,
            other_kv,
            *state,
            extra,
            place=other_place,
            flops=flops,
            moved=half_kv.size * 2,
            scratch=[scores],
            name="attend_second",
        )

    with jax.named_scope("projection"):
        got = over_seq(attended)
        columns = shape((n_seq, rows, feature_block // 2))
        keep, send, tables = run(
            functools.partial(project, rows=rows),
            [columns, columns, shape((n_seq // 2, 8, 2 * rows), f32)],
            got,
            out_proj,
            place=place,
            name="project",
        )
        paired = (keep.astype(f32) + lax.ppermute(send, "exp", swap).astype(f32)).astype(bf16)
        own_state = run(
            add_state,
            shape((rows, feature_block // 2)),
            over_chips(paired),
            turned[:rows],
            name="add_state",
        )
        other_state = lax.ppermute(own_state, "exp", swap)

    with jax.named_scope("gate_up"):
        slots = 2 * capacity
        state, outgoing = run(
            functools.partial(dispatch, capacity=capacity),
            [shape((rows, feature_block)), shape((n_chip * slots, feature_block))],
            own_state,
            other_state,
            turned[rows:],
            place=place,
            name="dispatch",
        )
        incoming = over_chips(outgoing.reshape(n_chip, slots, feature_block))
        gain = lax.dynamic_slice(norm_gain, (seq_index * feature_block,), (feature_block,))
        partial = run(
            functools.partial(gate_up, capacity=capacity),
            shape((n_seq * slots, gate_columns + 128)),
            incoming.reshape(n_seq * slots, feature_block),
            gain.reshape(1, -1),
            w_gate_up,
            name="gate_up",
        )
        sums = over_seq(partial.reshape(n_seq, slots, gate_columns + 128))

    with jax.named_scope("down"):
        active = run(
            functools.partial(activate, features=features),
            shape((n_seq, slots, hidden_units)),
            sums,
            name="activate",
        )
        line = shape((n_chip, n_seq * 4, feature_block))
        keep, send = run(
            functools.partial(combine, capacity=capacity),
            [line, line],
            over_seq(active).reshape(n_seq * slots, hidden_units),
            w_down,
            tables,
            state,
            place=place,
            name="combine",
        )

    with jax.named_scope("output"):
        paired = (keep.astype(f32) + lax.ppermute(send, "exp", swap).astype(f32)).astype(bf16)
        mixed = jnp.sum(over_chips(paired).astype(f32), axis=0).astype(bf16)
        mixed = over_seq(mixed.reshape(n_seq, 4, feature_block))
        return mixed.transpose(1, 0, 2).reshape(4, features)


def solution(mesh):
    in_specs = (
        P("seq", "exp", None),
        P("seq", None, None, None),
        P("seq", None, None, None),
        P("exp", "seq"),
        P("seq", "exp"),
        P(),
        P("seq", None),
        P("seq", None),
        P("exp", "seq", None),
        P("exp", None, "seq"),
    )
    out_specs = P(("seq", "exp"), None)
    return jax.shard_map(local, mesh=mesh, in_specs=in_specs, out_specs=out_specs, check_vma=False)
```

time: 820 us -> 286 us (0.35)
  the two profiles are of different devices: /device:TPU:1 before, /device:TPU:32 now
where the time goes in v1:
time: 286 us; the launch traced here: 285 us
  blocking collectives  129 us (45%)
  waiting for transfers between devices  75.7 us (26%)
  starting transfers between devices  39.1 us (14%)
  Pallas kernels  25.1 us (9%)
  local copies, waits for them, and re-layouts  10.4 us (4%)
  other arithmetic  5.79 us (2%)
    all_to_all x4, blocking collectives, over_seq(): return lax.all_to_all(value, 'seq', 0, 0, tiled=True)  91.4 us
    all_to_all x1, blocking collectives, over_chips(): lax.all_to_all(value, 'exp', 0, 0, tiled=True, axis_index_groups=chips)  37.5 us
    pallas_call x8, Pallas kernels, run(): pl.pallas_call(body, out_shape=out_shape, in_specs=[smem] * len(placed) +...  25.1 us
    all_to_all x1, waiting for transfers between devices, over_seq(): return lax.all_to_all(value, 'seq', 0, 0, tiled=True)  24.2 us
    all_to_all x2, waiting for transfers between devices, over_chips(): lax.all_to_all(value, 'exp', 0, 0, tiled=True, axis_index_groups=chips)  23.7 us
    ppermute x1, waiting for transfers between devices, local(): turned = lax.ppermute(packed, ('seq', 'exp'), turn)  22.8 us
    all_to_all x2, starting transfers between devices, over_chips(): lax.all_to_all(value, 'exp', 0, 0, tiled=True, axis_index_groups=chips)  22.1 us
    all_to_all x1, starting transfers between devices, over_seq(): return lax.all_to_all(value, 'seq', 0, 0, tiled=True)  7.17 us
  transfers between devices with their start and end apart: 8, of which 7 were waited for; matrix products, arithmetic and copies ran while one was open for 3% of the time, Pallas kernels for 1%

profile of v1, /device:TPU:32, one launch (start us, length us, event | category | flops | bytes accessed | tf_op | source)
XLA Modules:
  0.0 285.2 jit_solution(1904147634517584222)
XLA Ops:
  2.7 7.2 %all-to-all-start = ((bf16[16,2,192,128]{3,2,1,0:T(8,128)(2,1)}), bf16[16,2,192,128]{3,2,1,0:T(8,128)(2,1)S(1)}, u32[]{:S(2)}, u32[]{:S(2)}) async-start(bf16[16,2,192,128]{3,2,1,0:T(8,128)(2,1)} %broadcast_in_dim.14), calls=%async_computation | async-start | bytes 3145728 | tf_op jit(solution)/shard_map/key_values/all_to_all | solution.py:265
  10.1 24.2 %all-to-all-done.kv_ref = bf16[16,2,192,128]{3,2,1,0:T(8,128)(2,1)S(1)} async-done(((bf16[16,2,192,128]{3,2,1,0:T(8,128)(2,1)}), bf16[16,2,192,128]{3,2,1,0:T(8,128)(2,1)S(1)}, u32[]{:S(2)}, u32[]{:S(2)}) %all-to-all-start) | async-done | bytes 1572896 | tf_op jit(solution)/shard_map/key_values/all_to_all | solution.py:265
  34.3 1.9 collective-permute-start
  41.2 3.7 %attend_first.1 = (f32[256,128]{1,0:T(8,128)}, f32[256,128]{1,0:T(8,128)}, f32[256,128]{1,0:T(8,128)}) custom-call(s32[3]{0:T(128)} %add_add_fusion.place_ref, bf16[2,128,128]{2,1,0:T(8,128)(2,1)} %bitcast.42, bf16[16,2,192,128]{3,2,1,0:T(8,128)(2,1)} %copy-done.1), custom_call_target="tpu_custom_call" | custom-call | flops 402653184 | bytes 1572864 | tf_op jit(solution)/shard_map/attention/attend_first/pallas_call | solution.py:23
  45.0 4.3 %attend_second.1 = bf16[16,136,256]{2,1,0:T(8,128)(2,1)} custom-call(s32[3]{0:T(128)} %add_add_fusion.1.place_ref, bf16[2,128,128]{2,1,0:T(8,128)(2,1)} %bitcast.43, bf16[16,2,192,128]{3,2,1,0:T(8,128)(2,1)} %collective-permute-done.kv_ref, f32[256,128]{1,0:T(8,128)} %get-tuple-element.15.refs_0_, f32[256,128]{1,0:T(8,128)} %get-tuple-element.16.refs_1_, ...), custom_call_target="tpu_custom_call" | custom-call | flops 402653184 | bytes 1572864 | tf_op jit(solution)/shard_map/attention/attend_second/pallas_call | solution.py:23
  49.2 23.2 %all_to_all.40.got_ref = bf16[16,136,256]{2,1,0:T(8,128)(2,1)} all-to-all(bf16[16,136,256]{2,1,0:T(8,128)(2,1)} %attend_second.1), channel_id=1, replica_groups=mesh['seq'=16,'exp'=32] {'seq'}, dimensions={0} | all-to-all | bytes 2228224 | tf_op jit(solution)/shard_map/projection/all_to_all | solution.py:265
  72.4 2.7 project.1
  75.2 2.0 collective-permute-start.1
  77.2 2.1 collective-permute-done.1
  79.3 2.0 add_convert_fusion.1
  81.3 15.2 %all-to-all-start.2 = ((bf16[16,128,128]{2,1,0:T(8,128)(2,1)}), bf16[16,128,128]{2,1,0:T(8,128)(2,1)S(1)}, u32[]{:S(2)}, u32[]{:S(2)}) async-start(bf16[16,128,128]{2,1,0:T(8,128)(2,1)} %add_convert_fusion.1), calls=%async_computation.2 | async-start | bytes 1048576 | tf_op jit(solution)/shard_map/projection/all_to_all | solution.py:262
  96.5 2.0 collective-permute-start.2
  98.6 22.8 %collective-permute-done.2 = bf16[136,128]{1,0:T(8,128)(2,1)S(1)} collective-permute-done((bf16[136,128]{1,0:T(8,128)(2,1)S(1)}, bf16[136,128]{1,0:T(8,128)(2,1)S(1)}, u32[]{:S(2)}, u32[]{:S(2)}) %collective-permute-start.2) | collective-permute-done | bytes 34848 | tf_op jit(solution)/shard_map/turn_residual/ppermute | solution.py:269
  121.9 4.5 %all-to-all-done.2.got_ref = bf16[16,128,128]{2,1,0:T(8,128)(2,1)S(1)} async-done(((bf16[16,128,128]{2,1,0:T(8,128)(2,1)}), bf16[16,128,128]{2,1,0:T(8,128)(2,1)S(1)}, u32[]{:S(2)}, u32[]{:S(2)}) %all-to-all-start.2) | async-done | bytes 524320 | tf_op jit(solution)/shard_map/projection/all_to_all | solution.py:262
  134.7 6.9 %all-to-all-start.3 = ((bf16[16,40,256]{2,1,0:T(8,128)(2,1)}), bf16[16,40,256]{2,1,0:T(8,128)(2,1)S(1)}, u32[]{:S(2)}, u32[]{:S(2)}) async-start(bf16[16,40,256]{2,1,0:T(8,128)(2,1)} %bitcast.45), calls=%async_computation.3 | async-start | bytes 655360 | tf_op jit(solution)/shard_map/gate_up/all_to_all | solution.py:262
  143.0 19.2 %all-to-all-done.3 = bf16[16,40,256]{2,1,0:T(8,128)(2,1)S(1)} async-done(((bf16[16,40,256]{2,1,0:T(8,128)(2,1)}), bf16[16,40,256]{2,1,0:T(8,128)(2,1)S(1)}, u32[]{:S(2)}, u32[]{:S(2)}) %all-to-all-start.3) | async-done | bytes 327712 | tf_op jit(solution)/shard_map/gate_up/all_to_all | solution.py:262
  162.9 4.1 %gate_up.1 = bf16[640,1664]{1,0:T(8,128)(2,1)} custom-call(bf16[640,256]{1,0:T(8,128)(2,1)} %bitcast.41, f32[1,256]{1,0:T(1,128)} %bitcast.60, bf16[2,256,1536]{2,1,0:T(8,128)(2,1)} %w_ref.4), custom_call_target="tpu_custom_call" | custom-call | tf_op jit(solution)/shard_map/gate_up/gate_up/pallas_call | solution.py:23
  167.0 39.0 %all_to_all.41.got_ref = bf16[16,40,1664]{2,1,0:T(8,128)(2,1)} all-to-all(bf16[16,40,1664]{2,1,0:T(8,128)(2,1)} %bitcast.39), channel_id=1, replica_groups=mesh['seq'=16,'exp'=32] {'seq'}, dimensions={0} | all-to-all | bytes 4259840 | tf_op jit(solution)/shard_map/gate_up/all_to_all | solution.py:265
  206.0 3.0 %activate.1 = bf16[16,40,768]{2,1,0:T(8,128)(2,1)} custom-call(bf16[16,40,1664]{2,1,0:T(8,128)(2,1)} %all_to_all.41.got_ref), custom_call_target="tpu_custom_call" | custom-call | tf_op jit(solution)/shard_map/down/activate/pallas_call | solution.py:23
  209.0 18.7 %all_to_all.42 = bf16[16,40,768]{2,1,0:T(8,128)(2,1)} all-to-all(bf16[16,40,768]{2,1,0:T(8,128)(2,1)} %activate.1), channel_id=1, replica_groups=mesh['seq'=16,'exp'=32] {'seq'}, dimensions={0} | all-to-all | bytes 1966080 | tf_op jit(solution)/shard_map/down/all_to_all | solution.py:265
  227.7 3.7 %combine.1 = (bf16[16,64,256]{2,1,0:T(8,128)(2,1)}, bf16[16,64,256]{2,1,0:T(8,128)(2,1)}) custom-call(s32[3]{0:T(128)} %add_add_fusion.place_ref, bf16[640,768]{1,0:T(8,128)(2,1)} %bitcast.40, bf16[2,768,256]{2,1,0:T(8,128)(2,1)} %w_ref.5, f32[8,8,256]{2,1,0:T(8,128)} %get-tuple-element.21.table_ref, bf16[128,256]{1,0:T(8,128)(2,1)} %get-tuple-element.22.state_ref), custom_call_target="tpu_custom_call" | custom-call | tf_op jit(solution)/shard_map/down/combine/pallas_call | solution.py:23
  233.3 2.1 collective-permute-done.4
  236.6 37.5 %all_to_all.43 = bf16[16,64,256]{2,1,0:T(8,128)(2,1)S(1)} all-to-all(bf16[16,64,256]{2,1,0:T(8,128)(2,1)S(1)} %add_convert_fusion), channel_id=1, replica_groups={{0,2,4,6,8,10,12,14,16,18,20,22,24,26,28,30},{1,3,5,7,9,11,13,15,17,19,..., dimensions={0} | all-to-all | bytes 1048576 | tf_op jit(solution)/shard_map/output/all_to_all | solution.py:262
  274.2 10.4 %all_to_all.44 = bf16[16,4,256]{2,1,0:T(4,128)(2,1)S(1)} all-to-all(bf16[16,4,256]{2,1,0:T(4,128)(2,1)S(1)} %reshape.230), channel_id=1, replica_groups=mesh['seq'=16,'exp'=32] {'seq'}, dimensions={0} | all-to-all | bytes 65536 | tf_op jit(solution)/shard_map/output/all_to_all | solution.py:265
  (74 shorter events, 22.5 us)
Async XLA Ops:
  0.0 1.1 copy-start
  2.7 7.2 %copy-start.7 = (s32[128,8]{0,1:T(8,128)S(1)}, s32[128,8]{0,1:T(8,128)}, u32[]{:S(2)}) copy-start(s32[128,8]{0,1:T(8,128)} %param.16) | copy-start | bytes 12292
  2.7 7.2 %copy-start.8 = (f32[128,8]{0,1:T(8,128)S(1)}, f32[128,8]{0,1:T(8,128)}, u32[]{:S(2)}) copy-start(f32[128,8]{0,1:T(8,128)} %param.17) | copy-start | bytes 12292
  2.7 36.0 %copy-start.4 = (bf16[128,2,128]{2,1,0:T(2,128)(2,1)S(1)}, bf16[128,2,128]{2,1,0:T(2,128)(2,1)}, u32[]{:S(2)}) copy-start(bf16[128,2,128]{2,1,0:T(2,128)(2,1)} %param.10) | copy-start | bytes 196612
  2.7 31.6 %all-to-all-start = ((bf16[16,2,192,128]{3,2,1,0:T(8,128)(2,1)}), bf16[16,2,192,128]{3,2,1,0:T(8,128)(2,1)S(1)}, u32[]{:S(2)}, u32[]{:S(2)}) async-start(bf16[16,2,192,128]{3,2,1,0:T(8,128)(2,1)} %broadcast_in_dim.14), calls=%async_computation | async-start | bytes 3145728 | tf_op jit(solution)/shard_map/key_values/all_to_all | solution.py:265
  34.3 6.9 %copy-start.1 = (bf16[16,2,192,128]{3,2,1,0:T(8,128)(2,1)}, bf16[16,2,192,128]{3,2,1,0:T(8,128)(2,1)S(1)}, u32[]{:S(2)}) copy-start(bf16[16,2,192,128]{3,2,1,0:T(8,128)(2,1)S(1)} %all-to-all-done.kv_ref) | copy-start | bytes 4718596
  34.3 10.6 %collective-permute-start = (bf16[16,2,192,128]{3,2,1,0:T(8,128)(2,1)S(1)}, bf16[16,2,192,128]{3,2,1,0:T(8,128)(2,1)}, u32[]{:S(2)}, u32[]{:S(2)}) collective-permute-start(bf16[16,2,192,128]{3,2,1,0:T(8,128)(2,1)S(1)} %all-to-all-done.kv_ref), channel_id=1, source_target_pairs={{0,1},{1,0},{2,3},{3,2},{4,5},{5,4},{6,7},{7,6},{8,9},{9,8},{10,11... | collective-permute-start | bytes 4718600 | tf_op jit(solution)/shard_map/key_values/ppermute | solution.py:282
  75.2 21.3 %copy-start.5 = (bf16[128,128]{1,0:T(8,128)(2,1)S(1)}, bf16[128,128]{1,0:T(8,128)(2,1)}, u32[]{:S(2)}) copy-start(bf16[128,128]{1,0:T(8,128)(2,1)} %param.14) | copy-start | bytes 98308
  75.2 4.1 %collective-permute-start.1 = (bf16[16,128,128]{2,1,0:T(8,128)(2,1)}, bf16[16,128,128]{2,1,0:T(8,128)(2,1)S(1)}, u32[]{:S(2)}, u32[]{:S(2)}) collective-permute-start(bf16[16,128,128]{2,1,0:T(8,128)(2,1)} %get-tuple-element.19), channel_id=1, source_target_pairs={{0,1},{1,0},{2,3},{3,2},{4,5},{5,4},{6,7},{7,6},{8,9},{9,8},{10,11... | collective-permute-start | bytes 1572872 | tf_op jit(solution)/shard_map/projection/ppermute | solution.py:346
  81.3 45.1 %all-to-all-start.2 = ((bf16[16,128,128]{2,1,0:T(8,128)(2,1)}), bf16[16,128,128]{2,1,0:T(8,128)(2,1)S(1)}, u32[]{:S(2)}, u32[]{:S(2)}) async-start(bf16[16,128,128]{2,1,0:T(8,128)(2,1)} %add_convert_fusion.1), calls=%async_computation.2 | async-start | bytes 1048576 | tf_op jit(solution)/shard_map/projection/all_to_all | solution.py:262
  96.5 24.8 %collective-permute-start.2 = (bf16[136,128]{1,0:T(8,128)(2,1)S(1)}, bf16[136,128]{1,0:T(8,128)(2,1)S(1)}, u32[]{:S(2)}, u32[]{:S(2)}) collective-permute-start(bf16[136,128]{1,0:T(8,128)(2,1)S(1)} %pad_maximum_fusion), channel_id=1, source_target_pairs={{0,0},{1,1},{2,32},{3,33},{4,64},{5,65},{6,96},{7,97},{8,128},{9,1... | collective-permute-start | bytes 104456 | tf_op jit(solution)/shard_map/turn_residual/ppermute | solution.py:269
  126.4 0.8 copy-start.2
  128.9 3.3 %collective-permute-start.3 = (bf16[128,128]{1,0:T(8,128)(2,1)}, bf16[128,128]{1,0:T(8,128)(2,1)S(1)}, u32[]{:S(2)}, u32[]{:S(2)}) collective-permute-start(bf16[128,128]{1,0:T(8,128)(2,1)} %add_state.1.own_ref), channel_id=1, source_target_pairs={{0,1},{1,0},{2,3},{3,2},{4,5},{5,4},{6,7},{7,6},{8,9},{9,8},{10,11... | collective-permute-start | bytes 98312 | tf_op jit(solution)/shard_map/projection/ppermute | solution.py:354
  132.2 0.6 copy-start.6
  134.7 27.4 %all-to-all-start.3 = ((bf16[16,40,256]{2,1,0:T(8,128)(2,1)}), bf16[16,40,256]{2,1,0:T(8,128)(2,1)S(1)}, u32[]{:S(2)}, u32[]{:S(2)}) async-start(bf16[16,40,256]{2,1,0:T(8,128)(2,1)} %bitcast.45), calls=%async_computation.3 | async-start | bytes 655360 | tf_op jit(solution)/shard_map/gate_up/all_to_all | solution.py:262
  162.2 0.7 copy-start.3
  231.4 4.0 %collective-permute-start.4 = (bf16[16,64,256]{2,1,0:T(8,128)(2,1)}, bf16[16,64,256]{2,1,0:T(8,128)(2,1)S(1)}, u32[]{:S(2)}, u32[]{:S(2)}) collective-permute-start(bf16[16,64,256]{2,1,0:T(8,128)(2,1)} %get-tuple-element.24), channel_id=1, source_target_pairs={{0,1},{1,0},{2,3},{3,2},{4,5},{5,4},{6,7},{7,6},{8,9},{9,8},{10,11... | collective-permute-start | bytes 1572872 | tf_op jit(solution)/shard_map/output/ppermute | solution.py:399

commit v2 on v1

v2 whole, which is shorter than its diff:
```python
import functools
import math

import jax
import jax.numpy as jnp
import numpy as np
from jax import lax
from jax.experimental import pallas as pl
from jax.experimental.pallas import tpu as pltpu
from jax.sharding import PartitionSpec as P

QUERY_HEADS = 64
KEY_VALUE_HEADS = 4
FLOOR = -1e30
VMEM_BYTES = 56 * 1024 * 1024
f32 = jnp.float32
bf16 = jnp.bfloat16


def run(body, out_shape, *operands, place=None, flops=0, moved=0, scratch=(), name=None):
    vmem = pl.BlockSpec(memory_space=pltpu.VMEM)
    smem = pl.BlockSpec(memory_space=pltpu.SMEM)
    placed = [] if place is None else [place]
    return pl.pallas_call(
        body,
        out_shape=out_shape,
        in_specs=[smem] * len(placed) + [vmem] * len(operands),
        out_specs=jax.tree.map(lambda _: vmem, out_shape),
        scratch_shapes=list(scratch),
        compiler_params=pltpu.CompilerParams(vmem_limit_bytes=VMEM_BYTES),
        cost_estimate=pl.CostEstimate(flops=flops, bytes_accessed=moved, transcendentals=0),
        name=name,
    )(*placed, *operands)


def shape(dims, dtype=bf16):
    return jax.ShapeDtypeStruct(dims, dtype)


def attend(place_ref, q_ref, kv_ref, out_ref, s_ref, *, rows, cached, scale):
    sides, _, span, width = kv_ref.shape
    blocks = q_ref.shape[0]
    seq_index = place_ref[0]
    near, far = seq_index // sides, seq_index % sides
    heads = blocks // sides
    total = heads * rows
    wide = sides * span
    lane = lax.broadcasted_iota(jnp.int32, (1, wide), 1)
    within = lane % span
    pos = ((lane // span) * sides + far) * rows + within - cached
    pos = jnp.where(within < cached, -1, pos)
    token = lax.broadcasted_iota(jnp.int32, (total, 1), 0) % rows
    column = lax.broadcasted_iota(jnp.int32, (rows, 128), 1)
    factor = scale * math.log2(math.e)
    logs = jnp.zeros((rows, 128), f32)
    for b in range(sides):
        q = q_ref[b * heads : (b + 1) * heads].reshape(total, width)
        query_pos = (near * sides + b) * rows + token
        top = jnp.full((total, 128), FLOOR, f32)
        for part in range(sides):
            cut = slice(part * span, (part + 1) * span)
            s = lax.dot_general(
                q, kv_ref[part, 0], (((1,), (1,)), ((), ())), preferred_element_type=f32
            )
            s = jnp.where(pos[:, cut] <= query_pos, s, FLOOR)
            s_ref[b % 2, :, cut] = s
            for k in range(span // 128):
                top = jnp.maximum(top, s[:, k * 128 : (k + 1) * 128])
        top = jnp.max(top, axis=1, keepdims=True)
        acc = jnp.zeros((total, width), f32)
        sums = jnp.zeros((total, 128), f32)
        for part in range(sides):
            cut = slice(part * span, (part + 1) * span)
            p = jnp.exp2((s_ref[b % 2, :, cut] - top) * factor)
            for k in range(span // 128):
                sums = sums + p[:, k * 128 : (k + 1) * 128]
            acc = acc + jnp.dot(p.astype(bf16), kv_ref[part, 1], preferred_element_type=f32)
        row_sum = jnp.sum(sums, axis=1, keepdims=True)
        part_out = (acc / row_sum).astype(bf16)
        row_log = top * factor + jnp.log2(row_sum)
        for h in range(heads):
            logs = jnp.where(column == b * heads + h, row_log[h * rows : (h + 1) * rows], logs)
        for k in range(out_ref.shape[0]):
            out_ref[k, b * total : (b + 1) * total, :] = part_out
    logs = logs.T[:blocks]
    first = logs.astype(bf16).astype(f32)
    second = (logs - first).astype(bf16).astype(f32)
    third = logs - first - second
    pieces = jnp.concatenate([first, second, third, jnp.zeros_like(first)], axis=0).astype(bf16)
    for k in range(out_ref.shape[0]):
        out_ref[k, blocks * rows :, :] = pieces


def project(place_ref, got_ref, w_ref, keep_ref, send_ref, *, rows):
    sides, _, width = got_ref.shape
    half = place_ref[1]
    depth = w_ref.shape[0] // sides
    heads = depth // width
    blocks = sides * heads
    base = blocks * rows
    logs = []
    for x in range(sides):
        pieces = got_ref[x, base:, :].astype(f32)
        logs.append(pieces[:blocks] + pieces[blocks : 2 * blocks] + pieces[2 * blocks : 3 * blocks])
    top = functools.reduce(jnp.maximum, logs)
    shares = [jnp.exp2(v - top) for v in logs]
    whole = functools.reduce(jnp.add, shares)
    shares = jnp.concatenate([v / whole for v in shares], axis=0).T
    joined = []
    for b in range(sides):
        line = []
        for h in range(heads):
            k = b * heads + h
            value = jnp.zeros((rows, width), f32)
            for x in range(sides):
                share = shares[:, x * blocks + k : x * blocks + k + 1]
                value = value + share * got_ref[x, k * rows : (k + 1) * rows, :].astype(f32)
            line.append(value.astype(bf16))
        joined.append(jnp.concatenate(line, axis=1))
    x = jnp.concatenate(joined, axis=0)
    for a in range(sides):
        y = jnp.dot(x, w_ref[a * depth : (a + 1) * depth, :], preferred_element_type=f32)
        part = y.shape[1] // 2
        low, high = y[:, :part], y[:, part:]
        keep = jnp.where(half == 0, low, high).astype(bf16)
        send = jnp.where(half == 0, high, low).astype(bf16)
        keep_ref[a * sides : (a + 1) * sides] = keep.reshape(sides, rows, part)
        send_ref[a * sides : (a + 1) * sides] = send.reshape(sides, rows, part)


def add_state(got_ref, packed_ref, out_ref):
    rows = got_ref.shape[1]
    total = packed_ref[0:rows, :].astype(f32)
    for k in range(got_ref.shape[0]):
        total = total + got_ref[k].astype(f32)
    out_ref[0:rows, :] = total.astype(bf16)
    out_ref[rows:, :] = packed_ref[rows:, :]


def dispatch(place_ref, own_ref, other_ref, out_ref, *, capacity):
    half = place_ref[1]
    tokens = own_ref.shape[1]
    own, other = own_ref[0:tokens, :], other_ref[0:tokens, :]
    low = jnp.where(half == 0, own.astype(f32), other.astype(f32)).astype(bf16)
    high = jnp.where(half == 0, other.astype(f32), own.astype(f32)).astype(bf16)
    state = jnp.concatenate([low, high], axis=1)
    chips = out_ref.shape[0] // (2 * capacity)
    ids = own_ref[tokens:, :].astype(f32).astype(jnp.int32)
    before = (
        lax.broadcasted_iota(jnp.int32, (tokens, tokens), 0)
        < lax.broadcasted_iota(jnp.int32, (tokens, tokens), 1)
    ).astype(f32).astype(bf16)
    codes = []
    for member in range(2):
        expert = lax.broadcasted_iota(jnp.int32, (chips, tokens), 0) * 4 + 2 * half + member
        taken = jnp.zeros((chips, tokens), f32)
        for k in range(ids.shape[0]):
            taken = taken + (expert == ids[k : k + 1, :]).astype(f32)
        slot = jnp.dot(taken.astype(bf16), before, preferred_element_type=f32)
        codes.append(jnp.where(taken > 0, slot.astype(jnp.int32) + member * capacity, -1))
    slots = lax.broadcasted_iota(jnp.int32, (chips, 2 * capacity, tokens), 1)
    chosen = (codes[0][:, None, :] == slots) | (codes[1][:, None, :] == slots)
    select = chosen.astype(f32).reshape(chips * 2 * capacity, tokens).astype(bf16)
    out_ref[...] = jnp.dot(select, state, preferred_element_type=f32).astype(bf16)


def gate_up(place_ref, x_ref, gain_ref, *refs, capacity):
    *w_refs, out_ref = refs
    sides, _, slots, depth = x_ref.shape
    near = place_ref[0] // sides
    total = sides * slots
    columns = w_refs[0].shape[-1]
    sums = [jnp.zeros((total, columns), f32)] * 2
    squares = jnp.zeros((total, 1), f32)
    for k in range(sides):
        block = lax.rem(near + sides - k, sides)
        x = x_ref[:, block].reshape(total, depth).astype(f32)
        squares = squares + jnp.sum(x * x, axis=1, keepdims=True)
        scaled = (x * gain_ref[block]).astype(bf16)
        for m in range(2):
            sums[m] = sums[m] + jnp.dot(scaled, w_refs[k][m], preferred_element_type=f32)
    second = lax.broadcasted_iota(jnp.int32, (total, 1), 0) % (2 * capacity) >= capacity
    out_ref[:, :columns] = jnp.where(second, sums[1], sums[0]).astype(bf16)
    high = squares.astype(bf16).astype(f32)
    lane = lax.broadcasted_iota(jnp.int32, (total, 128), 1)
    out_ref[:, columns:] = jnp.where(lane < 64, high, squares - high).astype(bf16)


def activate(got_ref, extra_ref, out_ref, *, features):
    blocks, slots, _ = got_ref.shape

    def total(k):
        value = got_ref[0, :, k * 128 : (k + 1) * 128].astype(f32)
        for j in range(1, blocks):
            value = value + got_ref[j, :, k * 128 : (k + 1) * 128].astype(f32)
        return value

    pieces = total(3)
    squares = pieces[:, 0:1] + pieces[:, 64:65]
    norm = lax.rsqrt(squares / features + 1e-6)
    values = []
    for k in range(3):
        both = total(k) * norm
        values.append(both / (1.0 + jnp.exp(-both)) * pltpu.roll(both, 64, 1))
    part = slots // 2
    left = lax.broadcasted_iota(jnp.int32, (slots, 128), 1) < 64
    full = jnp.where(left, values[0], pltpu.roll(values[1], 64, 1)).astype(bf16)
    rest = jnp.where(left[:part], values[2][:part], pltpu.roll(values[2][part:], 64, 1)).astype(bf16)
    extra = extra_ref[...]
    for k in range(out_ref.shape[0]):
        out_ref[k, 0:slots, :] = full
        out_ref[k, slots : slots + part, :] = rest
        out_ref[k, slots + part :, :] = extra


def combine(place_ref, got_ref, w_in_ref, state_ref, keep_ref, send_ref, x_ref, w_ref, *, capacity):
    half, chip = place_ref[1], place_ref[2]
    pairs = got_ref.shape[0] // 2
    slots = 2 * 2 * capacity
    tokens = state_ref.shape[0]
    width = w_ref.shape[2]
    chips = keep_ref.shape[0]
    size = 2 * tokens
    sides = math.isqrt(got_ref.shape[0])
    part = x_ref.shape[0] // sides
    rest = part // 2
    left = lax.broadcasted_iota(jnp.int32, (rest, 128), 1) < 64
    for y in range(sides):
        w_ref[:, y * 128 : (y + 1) * 128] = w_in_ref[:, y * 192 : y * 192 + 128]
        start = sides * 128 + y * 64
        w_ref[:, start : start + 64] = w_in_ref[:, y * 192 + 128 : (y + 1) * 192]
        for x in range(sides):
            x_ref[x * part : (x + 1) * part, y * 128 : (y + 1) * 128] = got_ref[y * sides + x, :part]
    for x in range(sides):
        for y in range(0, sides, 2):
            a, b = (got_ref[k * sides + x, part : part + rest].astype(f32) for k in (y, y + 1))
            cut = slice((sides + y // 2) * 128, (sides + y // 2 + 1) * 128)
            one = jnp.where(left, a, pltpu.roll(b, 64, 1)).astype(bf16)
            two = jnp.where(left, pltpu.roll(a, 64, 1), b).astype(bf16)
            x_ref[x * part : x * part + rest, cut] = one
            x_ref[x * part + rest : (x + 1) * part, cut] = two
    x = x_ref[...]
    second = lax.broadcasted_iota(jnp.int32, (x.shape[0], 1), 0) % (2 * capacity) >= capacity
    y = jnp.where(
        second,
        jnp.dot(x, w_ref[1], preferred_element_type=f32),
        jnp.dot(x, w_ref[0], preferred_element_type=f32),
    )
    place = lax.broadcasted_iota(jnp.int32, (size, tokens), 0)
    token = (place % tokens // 8) * 8 + place // tokens * 4 + place % 4
    mine = (place % 8 // 4) == chip % 2
    column = lax.broadcasted_iota(jnp.int32, (size, tokens), 1)
    own = jnp.dot(
        ((token == column) & mine).astype(f32).astype(bf16), state_ref[...], preferred_element_type=f32
    )
    slot = lax.broadcasted_iota(jnp.int32, (slots, size), 0) + 1
    for j in range(pairs):
        table = got_ref[2 * j, part + rest :].astype(f32) + got_ref[2 * j + 1, part + rest :].astype(f32)
        table = jnp.concatenate([table[:8], table[8:]], axis=1)
        code = table.astype(jnp.int32)
        hit_a = slot == code[0:1, :]
        hit_b = slot == code[1:2, :]
        weight_a = table[2:3, :] + table[3:4, :] + table[4:5, :]
        weight_b = table[5:6, :] + table[6:7, :] + table[7:8, :]
        weight = jnp.where(hit_a, weight_a, 0.0) + jnp.where(hit_b, weight_b, 0.0)
        weight = jnp.sum(weight, axis=1, keepdims=True)
        rows = (y[j * slots : (j + 1) * slots] * weight).astype(bf16)
        select = (hit_a | hit_b).astype(f32).astype(bf16)
        found = lax.dot_general(select, rows, (((0,), (0,)), ((), ())), preferred_element_type=f32)
        mine = jnp.where(j == chip // 2, own, 0.0)
        found = found + jnp.concatenate(
            [jnp.where(half == 0, mine, 0.0), jnp.where(half == 0, 0.0, mine)], axis=1
        )
        low, high = found[:tokens], found[tokens:]
        keep = jnp.where(half == 0, low, high).astype(bf16)
        send = jnp.where(half == 0, high, low).astype(bf16)
        keep_ref[:, j * 8 : (j + 1) * 8, :] = keep.reshape(chips, 8, width)
        send_ref[:, j * 8 : (j + 1) * 8, :] = send.reshape(chips, 8, width)


def local(
    queries,
    cache,
    new_key_value,
    out_proj,
    residual,
    norm_gain,
    expert_ids,
    gates,
    w_gate_up,
    w_down,
):
    n_seq, n_exp = lax.axis_size("seq"), lax.axis_size("exp")
    n_chip = n_exp // 2
    seq_index, exp_index = lax.axis_index("seq"), lax.axis_index("exp")
    core, chip = exp_index % 2, exp_index // 2
    place = jnp.stack([seq_index, core, chip]).astype(jnp.int32)
    rows, heads, width = queries.shape
    top_k = expert_ids.shape[1]
    features = norm_gain.shape[0]
    members, feature_block, gate_columns = w_gate_up.shape
    hidden_units = w_down.shape[1]
    capacity = 5 * rows * top_k // (4 * members * n_exp)
    swap = [(i, i ^ 1) for i in range(n_exp)]
    chips = [[2 * z + c for z in range(n_chip)] for c in range(2)]
    sides = math.isqrt(n_seq)
    along_x = [[sides * y + x for x in range(sides)] for y in range(sides)]
    along_y = [[sides * y + x for y in range(sides)] for x in range(sides)]

    def spots():
        return np.ndindex(sides, sides, sides, sides, 2)

    def flat(y, x, a, b, c):
        return (sides * y + x) * n_exp + 2 * (sides * a + b) + c

    swap_x = [(flat(y, b, a, x, c), flat(y, x, a, b, c)) for y, x, a, b, c in spots()]
    swap_y = [(flat(y, x, a, b, c), flat(a, x, y, b, c)) for y, x, a, b, c in spots()]

    def over_chips(value):
        return lax.all_to_all(value, "exp", 0, 0, tiled=True, axis_index_groups=chips)

    def over_seq(value, groups=None):
        return lax.all_to_all(value, "seq", 0, 0, tiled=True, axis_index_groups=groups)

    with jax.named_scope("turn_residual"):
        packed = jnp.concatenate([residual, expert_ids.T.astype(bf16)], axis=0)
        turned = lax.ppermute(packed, ("seq", "exp"), swap_x)

    with jax.named_scope("key_values"):
        group = exp_index * heads // (QUERY_HEADS // KEY_VALUE_HEADS)
        own_cache = lax.dynamic_index_in_dim(cache, group, 1, keepdims=False)
        own_fresh = lax.dynamic_index_in_dim(new_key_value, group, 1, keepdims=False)
        own_kv = jnp.concatenate([own_cache, own_fresh], axis=0).transpose(1, 0, 2)
        kv = over_seq(jnp.broadcast_to(own_kv[None], (sides,) + own_kv.shape), along_y)
        q = lax.all_gather(
            queries.transpose(1, 0, 2), "seq", axis=0, tiled=True, axis_index_groups=along_x
        )

    with jax.named_scope("tables"):
        lines = []
        weights = []
        for member in range(2):
            chosen = expert_ids == exp_index * 2 + member
            taken = jnp.sum(chosen.astype(jnp.int32), axis=1)
            slot = jnp.cumsum(taken) - taken
            code = slot + member * capacity + (seq_index % 2) * 2 * capacity + 1
            lines.append(jnp.where(taken > 0, code, 0).astype(f32))
            weight = jnp.sum(jnp.where(chosen, gates, 0.0), axis=1)
            first = lax.reduce_precision(weight, 8, 7)
            second = lax.reduce_precision(weight - first, 8, 7)
            weights += [first, second, weight - first - second]
        table = jnp.stack(lines + weights).reshape(8, n_chip, 2, 1, 4).transpose(0, 2, 1, 3, 4)
        spot = (jnp.arange(2) == seq_index % 2).astype(f32).reshape(1, 1, 1, 2, 1)
        extra = (table * spot).reshape(8, 2 * rows).astype(bf16)
        extra = jnp.concatenate([extra[:, :rows], extra[:, rows:]], axis=0)

    with jax.named_scope("attention"):
        cached = cache.shape[0]
        span = cached + rows
        attended = run(
            functools.partial(attend, rows=rows, cached=cached, scale=1.0 / math.sqrt(width)),
            shape((sides, (sides * heads) * rows + 4 * sides * heads, width)),
            q,
            kv,
            place=place,
            flops=4 * q.size * span * sides,
            moved=kv.size * 2,
            scratch=[pltpu.VMEM((2, heads * rows, sides * span), f32)],
            name="attend",
        )
        columns = lax.all_gather(
            lax.optimization_barrier((out_proj, kv))[0],
            "seq",
            axis=0,
            tiled=True,
            axis_index_groups=along_y,
        )

    with jax.named_scope("projection"):
        part = shape((n_chip, rows, feature_block // 2))
        keep, send = run(
            functools.partial(project, rows=rows),
            [part, part],
            over_seq(attended, along_x),
            columns,
            place=place,
            name="project",
        )
        paired = (keep.astype(f32) + lax.ppermute(send, "exp", swap).astype(f32)).astype(bf16)
        weights = lax.optimization_barrier((w_gate_up, paired))[0]
        weights = weights.reshape(members, feature_block, 2, sides, -1, 64)
        weights = weights.transpose(3, 0, 1, 4, 2, 5).reshape(sides, members, feature_block, -1)
        blocks = []
        for k in range(sides):
            block = lax.dynamic_index_in_dim(weights, (seq_index // sides + k) % sides, 0, False)
            if k:
                ring = [
                    (sides * y + x, sides * ((y + k) % sides) + x)
                    for y in range(sides)
                    for x in range(sides)
                ]
                block = lax.ppermute(block, "seq", ring)
            blocks.append(block)
        gathered, blocks = lax.optimization_barrier((over_chips(paired), blocks))
        own_state = run(
            add_state,
            shape(turned.shape),
            gathered,
            turned,
            name="add_state",
        )
        other_state = lax.ppermute(own_state, "exp", swap)

    with jax.named_scope("gate_up"):
        slots = 2 * capacity
        outgoing = run(
            functools.partial(dispatch, capacity=capacity),
            shape((n_chip * slots, feature_block)),
            own_state,
            other_state,
            place=place,
            name="dispatch",
        )
        incoming = over_chips(outgoing.reshape(n_chip, slots, feature_block))
        incoming = incoming.reshape(1, sides, sides * slots, feature_block)
        incoming = over_seq(jnp.broadcast_to(incoming, (sides,) + incoming.shape[1:]), along_y)
        state = lax.ppermute(own_state[:rows], ("seq", "exp"), swap_y)
        gain = lax.dynamic_index_in_dim(
            norm_gain.reshape(sides, sides, 1, feature_block), seq_index % sides, 1, False
        )
        width = blocks[0].shape[-1] + 128
        partial = run(
            functools.partial(gate_up, capacity=capacity),
            shape((n_seq * slots, width)),
            incoming,
            gain,
            *blocks,
            place=place,
            name="gate_up",
        )
        sums = over_seq(partial.reshape(sides, sides * slots, width), along_x)

    with jax.named_scope("down"):
        quarter = sides * slots
        active = run(
            functools.partial(activate, features=features),
            shape((n_seq, quarter + quarter // 2 + extra.shape[0], 128)),
            sums,
            extra,
            name="activate",
        )
        line = shape((n_chip, n_seq * 4, feature_block))
        keep, send = run(
            functools.partial(combine, capacity=capacity),
            [line, line],
            over_seq(active),
            w_down,
            state,
            place=place,
            scratch=[
                pltpu.VMEM((n_seq * slots, hidden_units), bf16),
                pltpu.VMEM((members, hidden_units, feature_block), bf16),
            ],
            name="combine",
        )

    with jax.named_scope("output"):
        paired = (keep.astype(f32) + lax.ppermute(send, "exp", swap).astype(f32)).astype(bf16)
        mixed = jnp.sum(over_chips(paired).astype(f32), axis=0).astype(bf16)
        mixed = over_seq(mixed.reshape(n_seq, 4, feature_block))
        return mixed.transpose(1, 0, 2).reshape(4, features)


def solution(mesh):
    in_specs = (
        P("seq", "exp", None),
        P("seq", None, None, None),
        P("seq", None, None, None),
        P("exp", "seq"),
        P("seq", "exp"),
        P(),
        P("seq", None),
        P("seq", None),
        P("exp", "seq", None),
        P("exp", None, "seq"),
    )
    out_specs = P(("seq", "exp"), None)
    return jax.shard_map(local, mesh=mesh, in_specs=in_specs, out_specs=out_specs, check_vma=False)
```

time: 286 us -> 272 us (0.951)
  blocking collectives: 129 us -> 83.6 us
  starting transfers between devices: 39.1 us -> 67.2 us
  local copies, waits for them, and re-layouts: 10.4 us -> 19.3 us
  waiting for transfers between devices: 75.7 us -> 71.9 us
    all_to_all x4 -> x1, blocking collectives: 91.4 us -> 14.2 us  [over_seq(): lax.all_to_all(value, 'seq', 0, 0, tiled=True, axis_index_groups=groups)]
    all_gather x0 -> x2, blocking collectives: none -> 27.8 us  [the longest x1 14.4 us: local(): lax.all_gather(lax.optimization_barrier((out_proj, kv))[0], 'seq', axis=0...]
    all_to_all x1 -> x5, starting transfers between devices: 7.17 us -> 20.8 us  [over_seq(): lax.all_to_all(value, 'seq', 0, 0, tiled=True, axis_index_groups=groups)]
    ppermute x2 -> x5, waiting for transfers between devices: 22.8 us -> 10.3 us  [the longest x3 10.3 us: local(): block = lax.ppermute(block, 'seq', ring)]
    all_to_all x1 -> x5, waiting for transfers between devices: 24.2 us -> 35.8 us  [over_seq(): lax.all_to_all(value, 'seq', 0, 0, tiled=True, axis_index_groups=groups)]
    ppermute x2 -> x5, starting transfers between devices: 3.93 us -> 14 us  [the longest x3 10.2 us: local(): block = lax.ppermute(block, 'seq', ring)]
    unnamed x22 -> x44, local copies, waits for them, and re-layouts: 3.6 us -> 8.59 us
    all_to_all x2, starting transfers between devices: 22.1 us -> 26.7 us  [over_chips(): lax.all_to_all(value, 'exp', 0, 0, tiled=True, axis_index_groups=chips)]
  transfers between devices with their start and end apart: 8 -> 15, of which waited for: 7 -> 10; matrix products, arithmetic and copies ran while one was open for 3% -> 3% of each run, Pallas kernels for 1% -> 0%
where the time goes in v2:
time: 272 us; the launch traced here: 271 us
  blocking collectives  83.6 us (31%)
  waiting for transfers between devices  71.9 us (26%)
  starting transfers between devices  67.2 us (25%)
  Pallas kernels  22.9 us (8%)
  local copies, waits for them, and re-layouts  19.3 us (7%)
  other arithmetic  5.13 us (2%)
    all_to_all x1, blocking collectives, over_chips(): lax.all_to_all(value, 'exp', 0, 0, tiled=True, axis_index_groups=chips)  41.7 us
    all_to_all x5, waiting for transfers between devices, over_seq(): lax.all_to_all(value, 'seq', 0, 0, tiled=True, axis_index_groups=groups)  35.8 us
    all_to_all x2, starting transfers between devices, over_chips(): lax.all_to_all(value, 'exp', 0, 0, tiled=True, axis_index_groups=chips)  26.7 us
    pallas_call x7, Pallas kernels, run(): pl.pallas_call(body, out_shape=out_shape, in_specs=[smem] * len(placed) +...  22.9 us
    all_to_all x5, starting transfers between devices, over_seq(): lax.all_to_all(value, 'seq', 0, 0, tiled=True, axis_index_groups=groups)  20.8 us
    all_to_all x2, waiting for transfers between devices, over_chips(): lax.all_to_all(value, 'exp', 0, 0, tiled=True, axis_index_groups=chips)  20.3 us
    all_gather x1, blocking collectives, local(): lax.all_gather(lax.optimization_barrier((out_proj, kv))[0], 'seq', axis=0...  14.4 us
    all_to_all x1, blocking collectives, over_seq(): lax.all_to_all(value, 'seq', 0, 0, tiled=True, axis_index_groups=groups)  14.2 us
  transfers between devices with their start and end apart: 15, of which 10 were waited for; matrix products, arithmetic and copies ran while one was open for 3% of the time, Pallas kernels for 0%

profile of v2, /device:TPU:32, one launch (start us, length us, event | category | flops | bytes accessed | tf_op | source)
XLA Modules:
  0.0 270.6 jit_solution(15178279720653230347)
XLA Ops:
  3.1 4.5 %all-to-all-start = ((bf16[4,2,384,128]{3,2,1,0:T(8,128)(2,1)}), bf16[4,2,384,128]{3,2,1,0:T(8,128)(2,1)S(1)}, u32[]{:S(2)}, u32[]{:S(2)}) async-start(bf16[4,2,384,128]{3,2,1,0:T(8,128)(2,1)} %broadcast_in_dim.21), calls=%async_computation | async-start | bytes 1572864 | tf_op jit(solution)/shard_map/key_values/all_to_all | solution.py:323
  7.6 13.3 %all_gather.6.q_ref = bf16[8,128,128]{2,1,0:T(8,128)(2,1)} all-gather(bf16[2,128,128]{2,1,0:T(8,128)(2,1)S(1)} %bitcast.55), channel_id=1, replica_groups={{0,32,64,96},{128,160,192,224},{256,288,320,352},{384,416,448,480},{1,3..., dimensions={0}, use_global_device_ids=true | all-gather | bytes 327680 | tf_op jit(solution)/shard_map/key_values/all_gather | solution.py:335
  22.5 5.4 %attend.1 = bf16[4,1056,128]{2,1,0:T(8,128)(2,1)} custom-call(s32[3]{0:T(128)} %pad_add_fusion.place_ref, bf16[8,128,128]{2,1,0:T(8,128)(2,1)} %all_gather.6.q_ref, bf16[4,2,384,128]{3,2,1,0:T(8,128)(2,1)} %copy-done.6), custom_call_target="tpu_custom_call" | custom-call | flops 805306368 | bytes 786432 | tf_op jit(solution)/shard_map/attention/attend/pallas_call | solution.py:24
  27.9 4.0 %all-to-all-start.1 = ((bf16[4,1056,128]{2,1,0:T(8,128)(2,1)}), bf16[4,1056,128]{2,1,0:T(8,128)(2,1)S(1)}, u32[]{:S(2)}, u32[]{:S(2)}) async-start(bf16[4,1056,128]{2,1,0:T(8,128)(2,1)} %attend.1), calls=%async_computation.1 | async-start | bytes 2162688 | tf_op jit(solution)/shard_map/projection/all_to_all | solution.py:323
  31.8 14.4 %all_gather.7.w_ref = bf16[1024,256]{1,0:T(8,128)(2,1)} all-gather(bf16[256,256]{1,0:T(8,128)(2,1)S(1)} %copy-done.11), channel_id=1, replica_groups={{0,128,256,384},{32,160,288,416},{64,192,320,448},{96,224,352,480},{1,1..., dimensions={0}, use_global_device_ids=true | all-gather | bytes 655360 | tf_op jit(solution)/shard_map/attention/all_gather | solution.py:371
  47.3 3.6 %project.1 = (bf16[16,128,128]{2,1,0:T(8,128)(2,1)}, bf16[16,128,128]{2,1,0:T(8,128)(2,1)}) custom-call(s32[3]{0:T(128)} %pad_add_fusion.place_ref, bf16[4,1056,128]{2,1,0:T(8,128)(2,1)} %copy-done.2, bf16[1024,256]{1,0:T(8,128)(2,1)} %all_gather.7.w_ref), custom_call_target="tpu_custom_call" | custom-call | tf_op jit(solution)/shard_map/projection/project/pallas_call | solution.py:24
  56.8 15.2 %all-to-all-start.2 = ((bf16[16,128,128]{2,1,0:T(8,128)(2,1)}), bf16[16,128,128]{2,1,0:T(8,128)(2,1)S(1)}, u32[]{:S(2)}, u32[]{:S(2)}) async-start(bf16[16,128,128]{2,1,0:T(8,128)(2,1)} %add_convert_fusion.1), calls=%async_computation.2 | async-start | bytes 1048576 | tf_op jit(solution)/shard_map/projection/all_to_all | solution.py:320
  75.0 2.9 %collective-permute-start.1 = (bf16[2,256,384]{2,1,0:T(8,128)(2,1)}, bf16[2,256,384]{2,1,0:T(8,128)(2,1)S(1)}, u32[]{:S(2)}, u32[]{:S(2)}) collective-permute-start(bf16[2,256,384]{2,1,0:T(8,128)(2,1)} %bitcast.11), channel_id=1, source_target_pairs={{0,128},{32,160},{64,192},{96,224},{128,256},{160,288},{192,320},{... | collective-permute-start | bytes 1179656 | tf_op jit(solution)/shard_map/projection/ppermute | solution.py:402
  78.8 4.6 %collective-permute-start.2 = (bf16[2,256,384]{2,1,0:T(8,128)(2,1)}, bf16[2,256,384]{2,1,0:T(8,128)(2,1)S(1)}, u32[]{:S(2)}, u32[]{:S(2)}) collective-permute-start(bf16[2,256,384]{2,1,0:T(8,128)(2,1)} %bitcast.12), channel_id=1, source_target_pairs={{0,256},{32,288},{64,320},{96,352},{128,384},{160,416},{192,448},{... | collective-permute-start | bytes 1179656 | tf_op jit(solution)/shard_map/projection/ppermute | solution.py:402
  86.4 3.1 %collective-permute-start.4 = (bf16[136,128]{1,0:T(8,128)(2,1)S(1)}, bf16[136,128]{1,0:T(8,128)(2,1)S(1)}, u32[]{:S(2)}, u32[]{:S(2)}) collective-permute-start(bf16[136,128]{1,0:T(8,128)(2,1)S(1)} %pad_maximum_fusion), channel_id=1, source_target_pairs={{0,0},{1,1},{32,2},{33,3},{64,4},{65,5},{96,6},{97,7},{8,8},{9,9},... | collective-permute-start | bytes 104456 | tf_op jit(solution)/shard_map/turn_residual/ppermute | solution.py:327
  90.5 7.3 %collective-permute-done.2.refs_2_ = bf16[2,256,384]{2,1,0:T(8,128)(2,1)S(1)} collective-permute-done((bf16[2,256,384]{2,1,0:T(8,128)(2,1)}, bf16[2,256,384]{2,1,0:T(8,128)(2,1)S(1)}, u32[]{:S(2)}, u32[]{:S(2)}) %collective-permute-start.2) | collective-permute-done | bytes 393248 | tf_op jit(solution)/shard_map/projection/ppermute | solution.py:402
  97.8 3.0 %collective-permute-done.3.refs_3_ = bf16[2,256,384]{2,1,0:T(8,128)(2,1)S(1)} collective-permute-done((bf16[2,256,384]{2,1,0:T(8,128)(2,1)S(1)}, bf16[2,256,384]{2,1,0:T(8,128)(2,1)S(1)}, u32[]{:S(2)}, u32[]{:S(2)}) %collective-permute-start.3) | collective-permute-done | bytes 393248 | tf_op jit(solution)/shard_map/projection/ppermute | solution.py:402
  110.3 11.5 %all-to-all-start.3 = ((bf16[16,40,256]{2,1,0:T(8,128)(2,1)}), bf16[16,40,256]{2,1,0:T(8,128)(2,1)S(1)}, u32[]{:S(2)}, u32[]{:S(2)}) async-start(bf16[16,40,256]{2,1,0:T(8,128)(2,1)} %bitcast.50), calls=%async_computation.3 | async-start | bytes 655360 | tf_op jit(solution)/shard_map/gate_up/all_to_all | solution.py:320
  122.7 19.7 %all-to-all-done.3 = bf16[16,40,256]{2,1,0:T(8,128)(2,1)S(1)} async-done(((bf16[16,40,256]{2,1,0:T(8,128)(2,1)}), bf16[16,40,256]{2,1,0:T(8,128)(2,1)S(1)}, u32[]{:S(2)}, u32[]{:S(2)}) %all-to-all-start.3) | async-done | bytes 327712 | tf_op jit(solution)/shard_map/gate_up/all_to_all | solution.py:320
  143.5 4.0 %all-to-all-start.4 = ((bf16[4,4,160,256]{3,2,1,0:T(8,128)(2,1)}), bf16[4,4,160,256]{3,2,1,0:T(8,128)(2,1)S(1)}, u32[]{:S(2)}, u32[]{:S(2)}) async-start(bf16[4,4,160,256]{3,2,1,0:T(8,128)(2,1)} %broadcast_in_dim.23), calls=%async_computation.4 | async-start | bytes 2621440 | tf_op jit(solution)/shard_map/gate_up/all_to_all | solution.py:323
  150.0 14.1 %all-to-all-done.4.x_ref = bf16[4,4,160,256]{3,2,1,0:T(8,128)(2,1)S(1)} async-done(((bf16[4,4,160,256]{3,2,1,0:T(8,128)(2,1)}), bf16[4,4,160,256]{3,2,1,0:T(8,128)(2,1)S(1)}, u32[]{:S(2)}, u32[]{:S(2)}) %all-to-all-start.4) | async-done | bytes 1310752 | tf_op jit(solution)/shard_map/gate_up/all_to_all | solution.py:323
  165.2 4.2 %gate_up.1 = bf16[640,512]{1,0:T(8,128)(2,1)} custom-call(s32[3]{0:T(128)} %pad_add_fusion.place_ref, bf16[4,4,160,256]{3,2,1,0:T(8,128)(2,1)} %copy-done.1, f32[4,1,256]{2,1,0:T(1,128)} %dynamic-slice_bitcast_fusion.gain_ref, bf16[2,256,384]{2,1,0:T(8,128)(2,1)} %bitcast.49, bf16[2,256,384]{2,1,0:T(8,128)(2,1)} %copy-done.7, ...), custom_call_target="tpu_custom_call" | custom-call | tf_op jit(solution)/shard_map/gate_up/gate_up/pallas_call | solution.py:24
  169.4 4.7 %all-to-all-start.5 = ((bf16[4,160,512]{2,1,0:T(8,128)(2,1)}), bf16[4,160,512]{2,1,0:T(8,128)(2,1)S(1)}, u32[]{:S(2)}, u32[]{:S(2)}) async-start(bf16[4,160,512]{2,1,0:T(8,128)(2,1)} %bitcast.48), calls=%async_computation.5 | async-start | bytes 1310720 | tf_op jit(solution)/shard_map/gate_up/all_to_all | solution.py:323
  174.7 8.2 %all-to-all-done.5.got_ref = bf16[4,160,512]{2,1,0:T(8,128)(2,1)S(1)} async-done(((bf16[4,160,512]{2,1,0:T(8,128)(2,1)}), bf16[4,160,512]{2,1,0:T(8,128)(2,1)S(1)}, u32[]{:S(2)}, u32[]{:S(2)}) %all-to-all-start.5) | async-done | bytes 655392 | tf_op jit(solution)/shard_map/gate_up/all_to_all | solution.py:323
  186.2 3.7 %all-to-all-start.6 = ((bf16[16,256,128]{2,1,0:T(8,128)(2,1)}), bf16[16,256,128]{2,1,0:T(8,128)(2,1)S(1)}, u32[]{:S(2)}, u32[]{:S(2)}) async-start(bf16[16,256,128]{2,1,0:T(8,128)(2,1)} %activate.1), calls=%async_computation.6 | async-start | bytes 2097152 | tf_op jit(solution)/shard_map/down/all_to_all | solution.py:323
  190.6 13.5 %all-to-all-done.6.got_ref = bf16[16,256,128]{2,1,0:T(8,128)(2,1)S(1)} async-done(((bf16[16,256,128]{2,1,0:T(8,128)(2,1)}), bf16[16,256,128]{2,1,0:T(8,128)(2,1)S(1)}, u32[]{:S(2)}, u32[]{:S(2)}) %all-to-all-start.6) | async-done | bytes 1048608 | tf_op jit(solution)/shard_map/down/all_to_all | solution.py:323
  205.1 3.7 %combine.1 = (bf16[16,64,256]{2,1,0:T(8,128)(2,1)}, bf16[16,64,256]{2,1,0:T(8,128)(2,1)}) custom-call(s32[3]{0:T(128)} %pad_add_fusion.place_ref, bf16[16,256,128]{2,1,0:T(8,128)(2,1)} %copy-done.3, bf16[2,768,256]{2,1,0:T(8,128)(2,1)} %w_in_ref.1, bf16[128,128]{1,0:T(8,128)(2,1)} %copy-done.15), custom_call_target="tpu_custom_call" | custom-call | tf_op jit(solution)/shard_map/down/combine/pallas_call | solution.py:24
  214.0 41.7 %all_to_all.45 = bf16[16,64,256]{2,1,0:T(8,128)(2,1)S(1)} all-to-all(bf16[16,64,256]{2,1,0:T(8,128)(2,1)S(1)} %add_convert_fusion), channel_id=1, replica_groups={{0,2,4,6,8,10,12,14,16,18,20,22,24,26,28,30},{1,3,5,7,9,11,13,15,17,19,..., dimensions={0} | all-to-all | bytes 1048576 | tf_op jit(solution)/shard_map/output/all_to_all | solution.py:320
  255.8 14.2 %all_to_all.46 = bf16[16,4,256]{2,1,0:T(4,128)(2,1)S(1)} all-to-all(bf16[16,4,256]{2,1,0:T(4,128)(2,1)S(1)} %reshape.224), channel_id=1, replica_groups=mesh['seq'=16,'exp'=32] {'seq'}, dimensions={0} | all-to-all | bytes 65536 | tf_op jit(solution)/shard_map/output/all_to_all | solution.py:323
  (117 shorter events, 45.8 us)
Async XLA Ops:
  2.1 5.5 %copy-start.12 = (bf16[128,2,128]{2,1,0:T(2,128)(2,1)S(1)}, bf16[128,2,128]{2,1,0:T(2,128)(2,1)}, u32[]{:S(2)}) copy-start(bf16[128,2,128]{2,1,0:T(2,128)(2,1)} %param.10) | copy-start | bytes 196612
  3.1 18.5 %all-to-all-start = ((bf16[4,2,384,128]{3,2,1,0:T(8,128)(2,1)}), bf16[4,2,384,128]{3,2,1,0:T(8,128)(2,1)S(1)}, u32[]{:S(2)}, u32[]{:S(2)}) async-start(bf16[4,2,384,128]{3,2,1,0:T(8,128)(2,1)} %broadcast_in_dim.21), calls=%async_computation | async-start | bytes 1572864 | tf_op jit(solution)/shard_map/key_values/all_to_all | solution.py:323
  27.9 18.4 %all-to-all-start.1 = ((bf16[4,1056,128]{2,1,0:T(8,128)(2,1)}), bf16[4,1056,128]{2,1,0:T(8,128)(2,1)S(1)}, u32[]{:S(2)}, u32[]{:S(2)}) async-start(bf16[4,1056,128]{2,1,0:T(8,128)(2,1)} %attend.1), calls=%async_computation.1 | async-start | bytes 2162688 | tf_op jit(solution)/shard_map/projection/all_to_all | solution.py:323
  50.9 4.0 %collective-permute-start = (bf16[16,128,128]{2,1,0:T(8,128)(2,1)}, bf16[16,128,128]{2,1,0:T(8,128)(2,1)S(1)}, u32[]{:S(2)}, u32[]{:S(2)}) collective-permute-start(bf16[16,128,128]{2,1,0:T(8,128)(2,1)} %get-tuple-element.18), channel_id=1, source_target_pairs={{0,1},{1,0},{2,3},{3,2},{4,5},{5,4},{6,7},{7,6},{8,9},{9,8},{10,11... | collective-permute-start | bytes 1572872 | tf_op jit(solution)/shard_map/projection/ppermute | solution.py:389
  56.8 44.5 %all-to-all-start.2 = ((bf16[16,128,128]{2,1,0:T(8,128)(2,1)}), bf16[16,128,128]{2,1,0:T(8,128)(2,1)S(1)}, u32[]{:S(2)}, u32[]{:S(2)}) async-start(bf16[16,128,128]{2,1,0:T(8,128)(2,1)} %add_convert_fusion.1), calls=%async_computation.2 | async-start | bytes 1048576 | tf_op jit(solution)/shard_map/projection/all_to_all | solution.py:320
  74.1 12.3 %copy-start.17 = (s32[128,8]{0,1:T(8,128)S(1)}, s32[128,8]{0,1:T(8,128)}, u32[]{:S(2)}) copy-start(s32[128,8]{0,1:T(8,128)} %param.16) | copy-start | bytes 12292
  74.1 12.3 %copy-start.16 = (bf16[128,128]{1,0:T(8,128)(2,1)S(1)}, bf16[128,128]{1,0:T(8,128)(2,1)}, u32[]{:S(2)}) copy-start(bf16[128,128]{1,0:T(8,128)(2,1)} %param.14) | copy-start | bytes 98308
  75.0 15.5 %collective-permute-start.1 = (bf16[2,256,384]{2,1,0:T(8,128)(2,1)}, bf16[2,256,384]{2,1,0:T(8,128)(2,1)S(1)}, u32[]{:S(2)}, u32[]{:S(2)}) collective-permute-start(bf16[2,256,384]{2,1,0:T(8,128)(2,1)} %bitcast.11), channel_id=1, source_target_pairs={{0,128},{32,160},{64,192},{96,224},{128,256},{160,288},{192,320},{... | collective-permute-start | bytes 1179656 | tf_op jit(solution)/shard_map/projection/ppermute | solution.py:402
  78.8 18.9 %collective-permute-start.2 = (bf16[2,256,384]{2,1,0:T(8,128)(2,1)}, bf16[2,256,384]{2,1,0:T(8,128)(2,1)S(1)}, u32[]{:S(2)}, u32[]{:S(2)}) collective-permute-start(bf16[2,256,384]{2,1,0:T(8,128)(2,1)} %bitcast.12), channel_id=1, source_target_pairs={{0,256},{32,288},{64,320},{96,352},{128,384},{160,416},{192,448},{... | collective-permute-start | bytes 1179656 | tf_op jit(solution)/shard_map/projection/ppermute | solution.py:402
  83.4 38.4 %copy-start.19 = (f32[128,8]{0,1:T(8,128)S(1)}, f32[128,8]{0,1:T(8,128)}, u32[]{:S(2)}) copy-start(f32[128,8]{0,1:T(8,128)} %param.17) | copy-start | bytes 12292
  83.6 17.1 %collective-permute-start.3 = (bf16[2,256,384]{2,1,0:T(8,128)(2,1)S(1)}, bf16[2,256,384]{2,1,0:T(8,128)(2,1)S(1)}, u32[]{:S(2)}, u32[]{:S(2)}) collective-permute-start(bf16[2,256,384]{2,1,0:T(8,128)(2,1)S(1)} %bitcast.54), channel_id=1, source_target_pairs={{0,384},{32,416},{64,448},{96,480},{128,0},{160,32},{192,64},{224,... | collective-permute-start | bytes 1179656 | tf_op jit(solution)/shard_map/projection/ppermute | solution.py:402
  86.4 15.0 %collective-permute-start.4 = (bf16[136,128]{1,0:T(8,128)(2,1)S(1)}, bf16[136,128]{1,0:T(8,128)(2,1)S(1)}, u32[]{:S(2)}, u32[]{:S(2)}) collective-permute-start(bf16[136,128]{1,0:T(8,128)(2,1)S(1)} %pad_maximum_fusion), channel_id=1, source_target_pairs={{0,0},{1,1},{32,2},{33,3},{64,4},{65,5},{96,6},{97,7},{8,8},{9,9},... | collective-permute-start | bytes 104456 | tf_op jit(solution)/shard_map/turn_residual/ppermute | solution.py:327
  90.5 73.7 %copy-start.7 = (bf16[2,256,384]{2,1,0:T(8,128)(2,1)}, bf16[2,256,384]{2,1,0:T(8,128)(2,1)S(1)}, u32[]{:S(2)}) copy-start(bf16[2,256,384]{2,1,0:T(8,128)(2,1)S(1)} %collective-permute-done.1.refs_1_) | copy-start | bytes 1179652
  97.8 66.4 %copy-start.8 = (bf16[2,256,384]{2,1,0:T(8,128)(2,1)}, bf16[2,256,384]{2,1,0:T(8,128)(2,1)S(1)}, u32[]{:S(2)}) copy-start(bf16[2,256,384]{2,1,0:T(8,128)(2,1)S(1)} %collective-permute-done.2.refs_2_) | copy-start | bytes 1179652
  100.8 63.3 %copy-start.9 = (bf16[2,256,384]{2,1,0:T(8,128)(2,1)}, bf16[2,256,384]{2,1,0:T(8,128)(2,1)S(1)}, u32[]{:S(2)}) copy-start(bf16[2,256,384]{2,1,0:T(8,128)(2,1)S(1)} %collective-permute-done.3.refs_3_) | copy-start | bytes 1179652
  104.5 3.3 %collective-permute-start.5 = (bf16[136,128]{1,0:T(8,128)(2,1)}, bf16[136,128]{1,0:T(8,128)(2,1)S(1)}, u32[]{:S(2)}, u32[]{:S(2)}) collective-permute-start(bf16[136,128]{1,0:T(8,128)(2,1)} %add_state.1.own_ref), channel_id=1, source_target_pairs={{0,1},{1,0},{2,3},{3,2},{4,5},{5,4},{6,7},{7,6},{8,9},{9,8},{10,11... | collective-permute-start | bytes 104456 | tf_op jit(solution)/shard_map/projection/ppermute | solution.py:412
  110.3 32.0 %all-to-all-start.3 = ((bf16[16,40,256]{2,1,0:T(8,128)(2,1)}), bf16[16,40,256]{2,1,0:T(8,128)(2,1)S(1)}, u32[]{:S(2)}, u32[]{:S(2)}) async-start(bf16[16,40,256]{2,1,0:T(8,128)(2,1)} %bitcast.50), calls=%async_computation.3 | async-start | bytes 655360 | tf_op jit(solution)/shard_map/gate_up/all_to_all | solution.py:320
  143.5 20.6 %all-to-all-start.4 = ((bf16[4,4,160,256]{3,2,1,0:T(8,128)(2,1)}), bf16[4,4,160,256]{3,2,1,0:T(8,128)(2,1)S(1)}, u32[]{:S(2)}, u32[]{:S(2)}) async-start(bf16[4,4,160,256]{3,2,1,0:T(8,128)(2,1)} %broadcast_in_dim.23), calls=%async_computation.4 | async-start | bytes 2621440 | tf_op jit(solution)/shard_map/gate_up/all_to_all | solution.py:323
  169.4 13.5 %all-to-all-start.5 = ((bf16[4,160,512]{2,1,0:T(8,128)(2,1)}), bf16[4,160,512]{2,1,0:T(8,128)(2,1)S(1)}, u32[]{:S(2)}, u32[]{:S(2)}) async-start(bf16[4,160,512]{2,1,0:T(8,128)(2,1)} %bitcast.48), calls=%async_computation.5 | async-start | bytes 1310720 | tf_op jit(solution)/shard_map/gate_up/all_to_all | solution.py:323
  174.7 15.2 %copy-start.10 = (bf16[136,128]{1,0:T(8,128)(2,1)S(1)}, bf16[136,128]{1,0:T(8,128)(2,1)}, u32[]{:S(2)}) copy-start(bf16[136,128]{1,0:T(8,128)(2,1)} %add_state.1.own_ref) | copy-start | bytes 104452
  186.2 17.8 %all-to-all-start.6 = ((bf16[16,256,128]{2,1,0:T(8,128)(2,1)}), bf16[16,256,128]{2,1,0:T(8,128)(2,1)S(1)}, u32[]{:S(2)}, u32[]{:S(2)}) async-start(bf16[16,256,128]{2,1,0:T(8,128)(2,1)} %activate.1), calls=%async_computation.6 | async-start | bytes 2097152 | tf_op jit(solution)/shard_map/down/all_to_all | solution.py:323
  189.9 0.7 collective-permute-start.6
  190.6 13.5 %copy-start.15 = (bf16[128,128]{1,0:T(8,128)(2,1)}, bf16[128,128]{1,0:T(8,128)(2,1)S(1)}, u32[]{:S(2)}) copy-start(bf16[128,128]{1,0:T(8,128)(2,1)S(1)} %collective-permute-done.6.state_ref) | copy-start | bytes 98308
  208.8 4.0 %collective-permute-start.7 = (bf16[16,64,256]{2,1,0:T(8,128)(2,1)}, bf16[16,64,256]{2,1,0:T(8,128)(2,1)S(1)}, u32[]{:S(2)}, u32[]{:S(2)}) collective-permute-start(bf16[16,64,256]{2,1,0:T(8,128)(2,1)} %get-tuple-element.26), channel_id=1, source_target_pairs={{0,1},{1,0},{2,3},{3,2},{4,5},{5,4},{6,7},{7,6},{8,9},{9,8},{10,11... | collective-permute-start | bytes 1572872 | tf_op jit(solution)/shard_map/output/ppermute | solution.py:468
  (11 other events, 15.9 us)

commit v3 on v2

--- a/solution.py
+++ b/solution.py
@@ -144,7 +144,7 @@
     low = jnp.where(half == 0, own.astype(f32), other.astype(f32)).astype(bf16)
     high = jnp.where(half == 0, other.astype(f32), own.astype(f32)).astype(bf16)
     state = jnp.concatenate([low, high], axis=1)
-    chips = out_ref.shape[0] // (2 * capacity)
+    chips, size, _ = out_ref.shape
     ids = own_ref[tokens:, :].astype(f32).astype(jnp.int32)
     before = (
         lax.broadcasted_iota(jnp.int32, (tokens, tokens), 0)
@@ -158,18 +158,52 @@
             taken = taken + (expert == ids[k : k + 1, :]).astype(f32)
         slot = jnp.dot(taken.astype(bf16), before, preferred_element_type=f32)
         codes.append(jnp.where(taken > 0, slot.astype(jnp.int32) + member * capacity, -1))
-    slots = lax.broadcasted_iota(jnp.int32, (chips, 2 * capacity, tokens), 1)
+    slots = lax.broadcasted_iota(jnp.int32, (chips, size, tokens), 1)
     chosen = (codes[0][:, None, :] == slots) | (codes[1][:, None, :] == slots)
-    select = chosen.astype(f32).reshape(chips * 2 * capacity, tokens).astype(bf16)
-    out_ref[...] = jnp.dot(select, state, preferred_element_type=f32).astype(bf16)
-
-
-def gate_up(place_ref, x_ref, gain_ref, *refs, capacity):
-    *w_refs, out_ref = refs
+    place = lax.broadcasted_iota(jnp.int32, (chips, size, tokens), 0) * 8 + 4 * half
+    own = slots - 2 * capacity
+    token = lax.broadcasted_iota(jnp.int32, (chips, size, tokens), 2)
+    chosen = chosen | ((own >= 0) & (own < 4) & (token == place + own))
+    select = chosen.astype(f32).reshape(chips * size, tokens).astype(bf16)
+    rows = jnp.dot(select, state, preferred_element_type=f32)
+    out_ref[...] = rows.astype(bf16).reshape(out_ref.shape)
+
+
+def split_columns(place_ref, w_ref, own_ref, next_ref, prev_ref, all_ref):
+    sides = all_ref.shape[0]
+    near = place_ref[0] // sides
+    members, depth, columns = w_ref.shape
+    left = lax.broadcasted_iota(jnp.int32, (depth, 128), 1) < 64
+    for m in range(members):
+        for q in range(columns // 128):
+            cut = slice(q // 2 * 128, (q // 2 + 1) * 128)
+            gate = w_ref[m, :, cut].astype(f32)
+            up = w_ref[m, :, columns // 2 + cut.start : columns // 2 + cut.stop].astype(f32)
+            if q % 2:
+                gate = pltpu.roll(gate, 64, 1)
+            else:
+                up = pltpu.roll(up, 64, 1)
+            per = columns // 128 // sides
+            out = slice(q % per * 128, (q % per + 1) * 128)
+            all_ref[q // per, m, :, out] = jnp.where(left, gate, up).astype(bf16)
+    far = lax.rem(near + 2, sides)
+    own_ref[...] = all_ref[near]
+    for ref, step, m in ((next_ref, 1, 0), (prev_ref, sides - 1, 1)):
+        ref[0:2] = all_ref[lax.rem(near + step, sides)]
+        ref[2] = all_ref[far, m]
+
+
+def gate_up(place_ref, x_ref, state_ref, gain_ref, own_ref, prev_ref, next_ref, opp_ref, opp2_ref, out_ref, *, capacity):
+    w_refs = (
+        (own_ref.at[0], own_ref.at[1]),
+        (prev_ref.at[0], prev_ref.at[1]),
+        (opp_ref, opp2_ref),
+        (next_ref.at[0], next_ref.at[1]),
+    )
     sides, _, slots, depth = x_ref.shape
     near = place_ref[0] // sides
     total = sides * slots
-    columns = w_refs[0].shape[-1]
+    columns = own_ref.shape[-1]
     sums = [jnp.zeros((total, columns), f32)] * 2
     squares = jnp.zeros((total, 1), f32)
     for k in range(sides):
@@ -178,22 +212,38 @@
         squares = squares + jnp.sum(x * x, axis=1, keepdims=True)
         scaled = (x * gain_ref[block]).astype(bf16)
         for m in range(2):
-            sums[m] = sums[m] + jnp.dot(scaled, w_refs[k][m], preferred_element_type=f32)
+            sums[m] = sums[m] + jnp.dot(scaled, w_refs[k][m][...], preferred_element_type=f32)
     second = lax.broadcasted_iota(jnp.int32, (total, 1), 0) % (2 * capacity) >= capacity
-    out_ref[:, :columns] = jnp.where(second, sums[1], sums[0]).astype(bf16)
+    partial = jnp.where(second, sums[1], sums[0])
     high = squares.astype(bf16).astype(f32)
     lane = lax.broadcasted_iota(jnp.int32, (total, 128), 1)
-    out_ref[:, columns:] = jnp.where(lane < 64, high, squares - high).astype(bf16)
-
-
-def activate(got_ref, extra_ref, out_ref, *, features):
-    blocks, slots, _ = got_ref.shape
+    pieces = jnp.where(lane < 64, high, squares - high)
+    size = 2 * capacity
+    for a in range(sides):
+        for b in range(sides):
+            cut = slice((a * sides + b) * size, (a * sides + b + 1) * size)
+            state = state_ref[a, b].astype(f32)
+            slot_rows = jnp.concatenate([partial[cut], pieces[cut]], axis=1)
+            state = jnp.concatenate([state, jnp.zeros_like(state)], axis=1)
+            out_ref[b, a] = jnp.concatenate([slot_rows, state], axis=0).astype(bf16)
+
+
+def activate(got_ref, extra_ref, out_ref, state_ref, *, features):
+    blocks, lines, size, _ = got_ref.shape
+    extra_rows = 8
+    slots = lines * (size - extra_rows)
+    width = state_ref.shape[1] // (blocks * lines)
+    for a in range(lines):
+        for x in range(blocks):
+            start = (a * blocks + x) * width
+            state = got_ref[x, a, :, :width].astype(f32)[size - extra_rows :]
+            state_ref[:, start : start + width] = state
 
     def total(k):
-        value = got_ref[0, :, k * 128 : (k + 1) * 128].astype(f32)
+        value = got_ref[0, :, :, k * 128 : (k + 1) * 128].astype(f32)
         for j in range(1, blocks):
-            value = value + got_ref[j, :, k * 128 : (k + 1) * 128].astype(f32)
-        return value
+            value = value + got_ref[j, :, :, k * 128 : (k + 1) * 128].astype(f32)
+        return value[:, : size - extra_rows].reshape(slots, 128)
 
     pieces = total(3)
     squares = pieces[:, 0:1] + pieces[:, 64:65]
@@ -213,69 +263,72 @@
         out_ref[k, slots + part :, :] = extra
 
 
-def combine(place_ref, got_ref, w_in_ref, state_ref, keep_ref, send_ref, x_ref, w_ref, *, capacity):
-    half, chip = place_ref[1], place_ref[2]
-    pairs = got_ref.shape[0] // 2
-    slots = 2 * 2 * capacity
-    tokens = state_ref.shape[0]
+def combine(
+    place_ref,
+    got_ref,
+    own_ref,
+    prev_ref,
+    next_ref,
+    opp_ref,
+    opp2_ref,
+    out_ref,
+    x_ref,
+    w_ref,
+    *,
+    capacity,
+):
+    w_refs = (
+        (own_ref.at[0], own_ref.at[1]),
+        (prev_ref.at[0], prev_ref.at[1]),
+        (opp_ref, opp2_ref),
+        (next_ref.at[0], next_ref.at[1]),
+    )
+    sides = got_ref.shape[0]
+    far = place_ref[0] % sides
+    slots = x_ref.shape[0]
+    rest = slots // 2
     width = w_ref.shape[2]
-    chips = keep_ref.shape[0]
-    size = 2 * tokens
-    sides = math.isqrt(got_ref.shape[0])
-    part = x_ref.shape[0] // sides
-    rest = part // 2
+    size = got_ref.shape[2] * sides
     left = lax.broadcasted_iota(jnp.int32, (rest, 128), 1) < 64
     for y in range(sides):
-        w_ref[:, y * 128 : (y + 1) * 128] = w_in_ref[:, y * 192 : y * 192 + 128]
-        start = sides * 128 + y * 64
-        w_ref[:, start : start + 64] = w_in_ref[:, y * 192 + 128 : (y + 1) * 192]
-        for x in range(sides):
-            x_ref[x * part : (x + 1) * part, y * 128 : (y + 1) * 128] = got_ref[y * sides + x, :part]
-    for x in range(sides):
-        for y in range(0, sides, 2):
-            a, b = (got_ref[k * sides + x, part : part + rest].astype(f32) for k in (y, y + 1))
-            cut = slice((sides + y // 2) * 128, (sides + y // 2 + 1) * 128)
-            one = jnp.where(left, a, pltpu.roll(b, 64, 1)).astype(bf16)
-            two = jnp.where(left, pltpu.roll(a, 64, 1), b).astype(bf16)
-            x_ref[x * part : x * part + rest, cut] = one
-            x_ref[x * part + rest : (x + 1) * part, cut] = two
+        x_ref[:, y * 128 : (y + 1) * 128] = got_ref[y, :slots]
+    for y in range(0, sides, 2):
+        a, b = (got_ref[k, slots : slots + rest].astype(f32) for k in (y, y + 1))
+        cut = slice((sides + y // 2) * 128, (sides + y // 2 + 1) * 128)
+        x_ref[:rest, cut] = jnp.where(left, a, pltpu.roll(b, 64, 1)).astype(bf16)
+        x_ref[rest:, cut] = jnp.where(left, pltpu.roll(a, 64, 1), b).astype(bf16)
     x = x_ref[...]
-    second = lax.broadcasted_iota(jnp.int32, (x.shape[0], 1), 0) % (2 * capacity) >= capacity
-    y = jnp.where(
-        second,
-        jnp.dot(x, w_ref[1], preferred_element_type=f32),
-        jnp.dot(x, w_ref[0], preferred_element_type=f32),
-    )
-    place = lax.broadcasted_iota(jnp.int32, (size, tokens), 0)
-    token = (place % tokens // 8) * 8 + place // tokens * 4 + place % 4
-    mine = (place % 8 // 4) == chip % 2
-    column = lax.broadcasted_iota(jnp.int32, (size, tokens), 1)
-    own = jnp.dot(
-        ((token == column) & mine).astype(f32).astype(bf16), state_ref[...], preferred_element_type=f32
-    )
+
+    table = got_ref[0, slots + rest :].astype(f32)
+    for y in range(1, sides):
+        table = table + got_ref[y, slots + rest :].astype(f32)
+    table = jnp.concatenate([table[k * 8 : (k + 1) * 8] for k in range(sides)], axis=1)
+    code = table.astype(jnp.int32)
     slot = lax.broadcasted_iota(jnp.int32, (slots, size), 0) + 1
-    for j in range(pairs):
-        table = got_ref[2 * j, part + rest :].astype(f32) + got_ref[2 * j + 1, part + rest :].astype(f32)
-        table = jnp.concatenate([table[:8], table[8:]], axis=1)
-        code = table.astype(jnp.int32)
-        hit_a = slot == code[0:1, :]
-        hit_b = slot == code[1:2, :]
-        weight_a = table[2:3, :] + table[3:4, :] + table[4:5, :]
-        weight_b = table[5:6, :] + table[6:7, :] + table[7:8, :]
-        weight = jnp.where(hit_a, weight_a, 0.0) + jnp.where(hit_b, weight_b, 0.0)
-        weight = jnp.sum(weight, axis=1, keepdims=True)
-        rows = (y[j * slots : (j + 1) * slots] * weight).astype(bf16)
-        select = (hit_a | hit_b).astype(f32).astype(bf16)
-        found = lax.dot_general(select, rows, (((0,), (0,)), ((), ())), preferred_element_type=f32)
-        mine = jnp.where(j == chip // 2, own, 0.0)
-        found = found + jnp.concatenate(
-            [jnp.where(half == 0, mine, 0.0), jnp.where(half == 0, 0.0, mine)], axis=1
-        )
-        low, high = found[:tokens], found[tokens:]
-        keep = jnp.where(half == 0, low, high).astype(bf16)
-        send = jnp.where(half == 0, high, low).astype(bf16)
-        keep_ref[:, j * 8 : (j + 1) * 8, :] = keep.reshape(chips, 8, width)
-        send_ref[:, j * 8 : (j + 1) * 8, :] = send.reshape(chips, 8, width)
+    hit_a = slot == code[0:1, :]
+    hit_b = slot == code[1:2, :]
+    weight_a = table[2:3, :] + table[3:4, :] + table[4:5, :]
+    weight_b = table[5:6, :] + table[6:7, :] + table[7:8, :]
+    weight = jnp.where(hit_a, weight_a, 0.0) + jnp.where(hit_b, weight_b, 0.0)
+    weight = jnp.sum(weight, axis=1, keepdims=True)
+    select = (hit_a | hit_b).astype(f32).T.astype(bf16)
+
+    second = lax.broadcasted_iota(jnp.int32, (slots, 1), 0) % (2 * capacity) >= capacity
+    for k in range(sides):
+        block = lax.rem(far + sides - k, sides)
+        for m in range(2):
+            for y in range(sides):
+                w_ref[m, y * 128 : (y + 1) * 128] = w_refs[k][m][y * 192 : y * 192 + 128]
+                start = sides * 128 + y * 64
+                w_ref[m, start : start + 64] = w_refs[k][m][y * 192 + 128 : (y + 1) * 192]
+        result = jnp.where(
+            second,
+            jnp.dot(x, w_ref[1], preferred_element_type=f32),
+            jnp.dot(x, w_ref[0], preferred_element_type=f32),
+        )
+        found = jnp.dot(select, (result * weight).astype(bf16), preferred_element_type=f32)
+        start = pl.multiple_of(block * width, width)
+        out_ref[:, :, :, pl.ds(start, width)] = found.astype(bf16).reshape(sides, -1, 16, width)
 
 
 def local(
@@ -302,6 +355,8 @@
     hidden_units = w_down.shape[1]
     capacity = 5 * rows * top_k // (4 * members * n_exp)
     swap = [(i, i ^ 1) for i in range(n_exp)]
+    near = [[4 * p + i for i in range(4)] for p in range(n_chip // 2)]
+    far = [[4 * p + i for p in range(n_chip // 2)] for i in range(4)]
     chips = [[2 * z + c for z in range(n_chip)] for c in range(2)]
     sides = math.isqrt(n_seq)
     along_x = [[sides * y + x for x in range(sides)] for y in range(sides)]
@@ -314,13 +369,28 @@
         return (sides * y + x) * n_exp + 2 * (sides * a + b) + c
 
     swap_x = [(flat(y, b, a, x, c), flat(y, x, a, b, c)) for y, x, a, b, c in spots()]
-    swap_y = [(flat(y, x, a, b, c), flat(a, x, y, b, c)) for y, x, a, b, c in spots()]
 
     def over_chips(value):
         return lax.all_to_all(value, "exp", 0, 0, tiled=True, axis_index_groups=chips)
 
-    def over_seq(value, groups=None):
+    def over_seq(value, groups):
         return lax.all_to_all(value, "seq", 0, 0, tiled=True, axis_index_groups=groups)
+
+    def sum_near(value):
+        value = lax.all_to_all(value, "exp", 0, 0, tiled=True, axis_index_groups=near)
+        return jnp.sum(value.astype(f32), axis=0).astype(bf16)
+
+    def over_far(value):
+        return lax.all_to_all(value, "exp", 0, 0, tiled=True, axis_index_groups=far)
+
+    shift_y, shift_x = {}, {}
+    for k in (1, -1):
+        shift_y[k] = [
+            (sides * y + x, sides * ((y + k) % sides) + x) for y in range(sides) for x in range(sides)
+        ]
+        shift_x[k] = [
+            (sides * y + x, sides * y + (x + k) % sides) for y in range(sides) for x in range(sides)
+        ]
 
     with jax.named_scope("turn_residual"):
         packed = jnp.concatenate([residual, expert_ids.T.astype(bf16)], axis=0)
@@ -335,24 +405,6 @@
         q = lax.all_gather(
             queries.transpose(1, 0, 2), "seq", axis=0, tiled=True, axis_index_groups=along_x
         )
-
-    with jax.named_scope("tables"):
-        lines = []
-        weights = []
-        for member in range(2):
-            chosen = expert_ids == exp_index * 2 + member
-            taken = jnp.sum(chosen.astype(jnp.int32), axis=1)
-            slot = jnp.cumsum(taken) - taken
-            code = slot + member * capacity + (seq_index % 2) * 2 * capacity + 1
-            lines.append(jnp.where(taken > 0, code, 0).astype(f32))
-            weight = jnp.sum(jnp.where(chosen, gates, 0.0), axis=1)
-            first = lax.reduce_precision(weight, 8, 7)
-            second = lax.reduce_precision(weight - first, 8, 7)
-            weights += [first, second, weight - first - second]
-        table = jnp.stack(lines + weights).reshape(8, n_chip, 2, 1, 4).transpose(0, 2, 1, 3, 4)
-        spot = (jnp.arange(2) == seq_index % 2).astype(f32).reshape(1, 1, 1, 2, 1)
-        extra = (table * spot).reshape(8, 2 * rows).astype(bf16)
-        extra = jnp.concatenate([extra[:, :rows], extra[:, rows:]], axis=0)
 
     with jax.named_scope("attention"):
         cached = cache.shape[0]
@@ -387,21 +439,20 @@
             name="project",
         )
         paired = (keep.astype(f32) + lax.ppermute(send, "exp", swap).astype(f32)).astype(bf16)
-        weights = lax.optimization_barrier((w_gate_up, paired))[0]
-        weights = weights.reshape(members, feature_block, 2, sides, -1, 64)
-        weights = weights.transpose(3, 0, 1, 4, 2, 5).reshape(sides, members, feature_block, -1)
-        blocks = []
-        for k in range(sides):
-            block = lax.dynamic_index_in_dim(weights, (seq_index // sides + k) % sides, 0, False)
-            if k:
-                ring = [
-                    (sides * y + x, sides * ((y + k) % sides) + x)
-                    for y in range(sides)
-                    for x in range(sides)
-                ]
-                block = lax.ppermute(block, "seq", ring)
-            blocks.append(block)
-        gathered, blocks = lax.optimization_barrier((over_chips(paired), blocks))
+        weights, w_out, paired = lax.optimization_barrier((w_gate_up, w_down, paired))
+        piece = (members, feature_block, gate_columns // sides)
+        longer = (members + 1,) + piece[1:]
+        w_own, w_next, w_prev = run(
+            split_columns,
+            [shape(piece), shape(longer), shape(longer)],
+            weights,
+            place=place,
+            scratch=[pltpu.VMEM((sides,) + piece, bf16)],
+            name="split_columns",
+        )
+        near_y = (lax.ppermute(w_next, "seq", shift_y[1]), lax.ppermute(w_prev, "seq", shift_y[-1]))
+        near_x = (lax.ppermute(w_out, "seq", shift_x[1]), lax.ppermute(w_out, "seq", shift_x[-1]))
+        gathered, near_y, near_x = lax.optimization_barrier((over_chips(paired), near_y, near_x))
         own_state = run(
             add_state,
             shape(turned.shape),
@@ -413,62 +464,96 @@
 
     with jax.named_scope("gate_up"):
         slots = 2 * capacity
+        size = slots + 8
         outgoing = run(
             functools.partial(dispatch, capacity=capacity),
-            shape((n_chip * slots, feature_block)),
+            shape((n_chip, size, feature_block)),
             own_state,
             other_state,
             place=place,
             name="dispatch",
         )
-        incoming = over_chips(outgoing.reshape(n_chip, slots, feature_block))
-        incoming = incoming.reshape(1, sides, sides * slots, feature_block)
+        incoming = over_chips(outgoing)
+        far_y = (
+            lax.ppermute(near_y[0][members], "seq", shift_y[1]),
+            lax.ppermute(near_y[1][members], "seq", shift_y[-1]),
+        )
+        far_x = (
+            lax.ppermute(near_x[0][0], "seq", shift_x[1]),
+            lax.ppermute(near_x[1][1], "seq", shift_x[-1]),
+        )
+        incoming, far_x, far_y = lax.optimization_barrier((incoming, far_x, far_y))
+        incoming = incoming.reshape(sides, sides, size, feature_block)
+        state = incoming[:, :, slots:]
+        incoming = incoming[:, :, :slots].reshape(1, sides, sides * slots, feature_block)
         incoming = over_seq(jnp.broadcast_to(incoming, (sides,) + incoming.shape[1:]), along_y)
-        state = lax.ppermute(own_state[:rows], ("seq", "exp"), swap_y)
         gain = lax.dynamic_index_in_dim(
             norm_gain.reshape(sides, sides, 1, feature_block), seq_index % sides, 1, False
         )
-        width = blocks[0].shape[-1] + 128
+        width = piece[-1] + 128
         partial = run(
             functools.partial(gate_up, capacity=capacity),
-            shape((n_seq * slots, width)),
+            shape((sides, sides, size, width)),
             incoming,
+            state,
             gain,
-            *blocks,
+            w_own,
+            *near_y,
+            *far_y,
             place=place,
             name="gate_up",
         )
-        sums = over_seq(partial.reshape(sides, sides * slots, width), along_x)
+    with jax.named_scope("tables"):
+        expert_ids, gates, partial = lax.optimization_barrier((expert_ids, gates, partial))
+        lines = []
+        weights = []
+        for member in range(2):
+            chosen = expert_ids == exp_index * 2 + member
+            taken = jnp.sum(chosen.astype(jnp.int32), axis=1)
+            slot = jnp.cumsum(taken) - taken
+            code = slot + member * capacity + (seq_index // sides) * 2 * capacity + 1
+            lines.append(jnp.where(taken > 0, code, 0).astype(f32))
+            weight = jnp.sum(jnp.where(chosen, gates, 0.0), axis=1)
+            first = lax.reduce_precision(weight, 8, 7)
+            second = lax.reduce_precision(weight - first, 8, 7)
+            weights += [first, second, weight - first - second]
+        table = jnp.stack(lines + weights).reshape(8, n_chip // 2, 2, 2, 1, 4)
+        spot = (jnp.arange(sides) == seq_index // sides).astype(f32).reshape(1, 1, 1, 1, sides, 1)
+        table = (table * spot).transpose(2, 3, 0, 1, 4, 5)
+        extra = table.reshape(4 * 8, rows).astype(bf16)
 
     with jax.named_scope("down"):
         quarter = sides * slots
-        active = run(
+        sums = over_seq(partial, along_x)
+        active, state = run(
             functools.partial(activate, features=features),
-            shape((n_seq, quarter + quarter // 2 + extra.shape[0], 128)),
+            [shape((sides, quarter + quarter // 2 + extra.shape[0], 128)), shape((8, features), f32)],
             sums,
             extra,
             name="activate",
         )
-        line = shape((n_chip, n_seq * 4, feature_block))
-        keep, send = run(
+        line = 4 * sides
+        partial = run(
             functools.partial(combine, capacity=capacity),
-            [line, line],
-            over_seq(active),
+            shape((4, n_chip // 2, line, sides * feature_block)),
+            over_seq(active, along_y),
             w_down,
-            state,
+            *near_x,
+            *far_x,
             place=place,
             scratch=[
-                pltpu.VMEM((n_seq * slots, hidden_units), bf16),
+                pltpu.VMEM((quarter, hidden_units), bf16),
                 pltpu.VMEM((members, hidden_units, feature_block), bf16),
             ],
             name="combine",
         )
 
     with jax.named_scope("output"):
-        paired = (keep.astype(f32) + lax.ppermute(send, "exp", swap).astype(f32)).astype(bf16)
-        mixed = jnp.sum(over_chips(paired).astype(f32), axis=0).astype(bf16)
-        mixed = over_seq(mixed.reshape(n_seq, 4, feature_block))
-        return mixed.transpose(1, 0, 2).reshape(4, features)
+        gathered = over_far(sum_near(partial))
+        mixed = jnp.sum(gathered.astype(f32), axis=0).astype(bf16)
+        mixed = over_seq(mixed.reshape(sides, 4, sides * feature_block), along_y)
+        mixed = mixed.transpose(1, 0, 2).reshape(4, features)
+        return (state[:4] + mixed.astype(f32)).astype(bf16)
 
 
 def solution(mesh):

time: 272 us -> 265 us (0.974)
  the two profiles are of different devices: /device:TPU:32 before, /device:TPU:2 now
where the time goes in v3:
time: 265 us; the launch traced here: 263 us
  blocking collectives  97.4 us (37%)
  starting transfers between devices  80.9 us (31%)
  waiting for transfers between devices  36.2 us (14%)
  Pallas kernels  27 us (10%)
  local copies, waits for them, and re-layouts  16.5 us (6%)
  other arithmetic  4.92 us (2%)
    all_to_all x1, blocking collectives, over_far(): return lax.all_to_all(value, 'exp', 0, 0, tiled=True, axis_index_groups=far)  31.6 us
    pallas_call x8, Pallas kernels, run(): pl.pallas_call(body, out_shape=out_shape, in_specs=[smem] * len(placed) +...  27 us
    all_to_all x2, starting transfers between devices, over_chips(): lax.all_to_all(value, 'exp', 0, 0, tiled=True, axis_index_groups=chips)  23.3 us
    all_to_all x4, starting transfers between devices, over_seq(): lax.all_to_all(value, 'seq', 0, 0, tiled=True, axis_index_groups=groups)  23.3 us
    all_to_all x2, blocking collectives, over_seq(): lax.all_to_all(value, 'seq', 0, 0, tiled=True, axis_index_groups=groups)  18.7 us
    all_to_all x1, blocking collectives, sum_near(): lax.all_to_all(value, 'exp', 0, 0, tiled=True, axis_index_groups=near)  18.3 us
    all_to_all x4, waiting for transfers between devices, over_seq(): lax.all_to_all(value, 'seq', 0, 0, tiled=True, axis_index_groups=groups)  16.3 us
    all_gather x1, blocking collectives, local(): lax.all_gather(queries.transpose(1, 0, 2), 'seq', axis=0, tiled=True, axi...  14.8 us
  transfers between devices with their start and end apart: 17, of which 9 were waited for; matrix products, arithmetic and copies ran while one was open for 3% of the time, Pallas kernels for 1%

profile of v3, /device:TPU:2, one launch (start us, length us, event | category | flops | bytes accessed | tf_op | source)
XLA Modules:
  0.0 263.3 jit_solution(174392787027006251)
XLA Ops:
  2.2 4.5 %all-to-all-start = ((bf16[4,2,384,128]{3,2,1,0:T(8,128)(2,1)}), bf16[4,2,384,128]{3,2,1,0:T(8,128)(2,1)S(1)}, u32[]{:S(2)}, u32[]{:S(2)}) async-start(bf16[4,2,384,128]{3,2,1,0:T(8,128)(2,1)} %broadcast_in_dim.21), calls=%async_computation | async-start | bytes 1572864 | tf_op jit(solution)/shard_map/key_values/all_to_all | solution.py:377
  6.7 14.8 %all_gather.6.q_ref = bf16[8,128,128]{2,1,0:T(8,128)(2,1)} all-gather(bf16[2,128,128]{2,1,0:T(8,128)(2,1)S(1)} %bitcast.42), channel_id=1, replica_groups={{0,32,64,96},{128,160,192,224},{256,288,320,352},{384,416,448,480},{1,3..., dimensions={0}, use_global_device_ids=true | all-gather | bytes 327680 | tf_op jit(solution)/shard_map/key_values/all_gather | solution.py:405
  23.0 5.4 %attend.1 = bf16[4,1056,128]{2,1,0:T(8,128)(2,1)} custom-call(s32[3]{0:T(128)} %pad_add_fusion.place_ref, bf16[8,128,128]{2,1,0:T(8,128)(2,1)} %all_gather.6.q_ref, bf16[4,2,384,128]{3,2,1,0:T(8,128)(2,1)} %copy-done.10), custom_call_target="tpu_custom_call" | custom-call | flops 805306368 | bytes 786432 | tf_op jit(solution)/shard_map/attention/attend/pallas_call | solution.py:24
  28.4 7.1 %all-to-all-start.1 = ((bf16[4,1056,128]{2,1,0:T(8,128)(2,1)}), bf16[4,1056,128]{2,1,0:T(8,128)(2,1)S(1)}, u32[]{:S(2)}, u32[]{:S(2)}) async-start(bf16[4,1056,128]{2,1,0:T(8,128)(2,1)} %attend.1), calls=%async_computation.1 | async-start | bytes 2162688 | tf_op jit(solution)/shard_map/projection/all_to_all | solution.py:377
  35.6 14.0 %all_gather.7.w_ref = bf16[1024,256]{1,0:T(8,128)(2,1)} all-gather(bf16[256,256]{1,0:T(8,128)(2,1)S(1)} %copy-done.14), channel_id=1, replica_groups={{0,128,256,384},{32,160,288,416},{64,192,320,448},{96,224,352,480},{1,1..., dimensions={0}, use_global_device_ids=true | all-gather | bytes 655360 | tf_op jit(solution)/shard_map/attention/all_gather | solution.py:423
  50.6 3.6 %project.1 = (bf16[16,128,128]{2,1,0:T(8,128)(2,1)}, bf16[16,128,128]{2,1,0:T(8,128)(2,1)}) custom-call(s32[3]{0:T(128)} %pad_add_fusion.place_ref, bf16[4,1056,128]{2,1,0:T(8,128)(2,1)} %copy-done.2, bf16[1024,256]{1,0:T(8,128)(2,1)} %all_gather.7.w_ref), custom_call_target="tpu_custom_call" | custom-call | tf_op jit(solution)/shard_map/projection/project/pallas_call | solution.py:24
  60.1 11.6 %all-to-all-start.2 = ((bf16[16,128,128]{2,1,0:T(8,128)(2,1)}), bf16[16,128,128]{2,1,0:T(8,128)(2,1)S(1)}, u32[]{:S(2)}, u32[]{:S(2)}) async-start(bf16[16,128,128]{2,1,0:T(8,128)(2,1)} %add_convert_fusion), calls=%async_computation.2 | async-start | bytes 1048576 | tf_op jit(solution)/shard_map/projection/all_to_all | solution.py:374
  73.7 3.9 %collective-permute-start.3 = (bf16[2,768,256]{2,1,0:T(8,128)(2,1)}, bf16[2,768,256]{2,1,0:T(8,128)(2,1)S(1)}, u32[]{:S(2)}, u32[]{:S(2)}) collective-permute-start(bf16[2,768,256]{2,1,0:T(8,128)(2,1)} %own_ref.1), channel_id=1, source_target_pairs={{0,32},{32,64},{64,96},{96,0},{128,160},{160,192},{192,224},{224,1... | collective-permute-start | bytes 2359304 | tf_op jit(solution)/shard_map/projection/ppermute | solution.py:454
  83.9 4.1 %collective-permute-start.2 = (bf16[3,256,384]{2,1,0:T(8,128)(2,1)}, bf16[3,256,384]{2,1,0:T(8,128)(2,1)S(1)}, u32[]{:S(2)}, u32[]{:S(2)}) collective-permute-start(bf16[3,256,384]{2,1,0:T(8,128)(2,1)} %get-tuple-element.35), channel_id=1, source_target_pairs={{0,384},{32,416},{64,448},{96,480},{128,0},{160,32},{192,64},{224,... | collective-permute-start | bytes 1769480 | tf_op jit(solution)/shard_map/projection/ppermute | solution.py:453
  88.1 4.5 %collective-permute-start.5 = (bf16[136,128]{1,0:T(8,128)(2,1)S(1)}, bf16[136,128]{1,0:T(8,128)(2,1)S(1)}, u32[]{:S(2)}, u32[]{:S(2)}) collective-permute-start(bf16[136,128]{1,0:T(8,128)(2,1)S(1)} %pad_maximum_fusion), channel_id=1, source_target_pairs={{0,0},{1,1},{32,2},{33,3},{64,4},{65,5},{96,6},{97,7},{8,8},{9,9},... | collective-permute-start | bytes 104456 | tf_op jit(solution)/shard_map/turn_residual/ppermute | solution.py:397
  92.6 6.2 %collective-permute-done.1.prev_ref = bf16[3,256,384]{2,1,0:T(8,128)(2,1)S(1)} collective-permute-done((bf16[3,256,384]{2,1,0:T(8,128)(2,1)}, bf16[3,256,384]{2,1,0:T(8,128)(2,1)S(1)}, u32[]{:S(2)}, u32[]{:S(2)}) %collective-permute-start.1) | collective-permute-done | bytes 589856 | tf_op jit(solution)/shard_map/projection/ppermute | solution.py:453
  110.1 11.7 %all-to-all-start.3 = ((bf16[16,48,256]{2,1,0:T(8,128)(2,1)}), bf16[16,48,256]{2,1,0:T(8,128)(2,1)S(1)}, u32[]{:S(2)}, u32[]{:S(2)}) async-start(bf16[16,48,256]{2,1,0:T(8,128)(2,1)} %dispatch.1), calls=%async_computation.3 | async-start | bytes 786432 | tf_op jit(solution)/shard_map/gate_up/all_to_all | solution.py:374
  128.8 5.3 %collective-permute-start.10 = (bf16[256,384]{1,0:T(8,128)(2,1)S(1)}, bf16[256,384]{1,0:T(8,128)(2,1)S(1)}, u32[]{:S(2)}, u32[]{:S(2)}) collective-permute-start(bf16[256,384]{1,0:T(8,128)(2,1)S(1)} %slice_bitcast_fusion.2), channel_id=1, source_target_pairs={{0,384},{32,416},{64,448},{96,480},{128,0},{160,32},{192,64},{224,... | collective-permute-start | bytes 589832 | tf_op jit(solution)/shard_map/gate_up/ppermute | solution.py:479
  137.7 5.3 %collective-permute-done.9.opp_ref = bf16[256,384]{1,0:T(8,128)(2,1)S(1)} collective-permute-done((bf16[256,384]{1,0:T(8,128)(2,1)S(1)}, bf16[256,384]{1,0:T(8,128)(2,1)S(1)}, u32[]{:S(2)}, u32[]{:S(2)}) %collective-permute-start.9) | collective-permute-done | bytes 196640 | tf_op jit(solution)/shard_map/gate_up/ppermute | solution.py:478
  147.5 4.7 %all-to-all-start.4 = ((bf16[4,4,160,256]{3,2,1,0:T(8,128)(2,1)}), bf16[4,4,160,256]{3,2,1,0:T(8,128)(2,1)S(1)}, u32[]{:S(2)}, u32[]{:S(2)}) async-start(bf16[4,4,160,256]{3,2,1,0:T(8,128)(2,1)} %broadcast_in_dim.23), calls=%async_computation.4 | async-start | bytes 2621440 | tf_op jit(solution)/shard_map/gate_up/all_to_all | solution.py:377
  154.4 11.3 %all-to-all-done.4.x_ref = bf16[4,4,160,256]{3,2,1,0:T(8,128)(2,1)S(1)} async-done(((bf16[4,4,160,256]{3,2,1,0:T(8,128)(2,1)}), bf16[4,4,160,256]{3,2,1,0:T(8,128)(2,1)S(1)}, u32[]{:S(2)}, u32[]{:S(2)}) %all-to-all-start.4) | async-done | bytes 1310752 | tf_op jit(solution)/shard_map/gate_up/all_to_all | solution.py:377
  166.8 4.3 %gate_up.1 = bf16[4,4,48,512]{3,2,1,0:T(8,128)(2,1)} custom-call(s32[3]{0:T(128)} %pad_add_fusion.place_ref, bf16[4,4,160,256]{3,2,1,0:T(8,128)(2,1)} %copy-done.1, bf16[4,4,8,256]{3,2,1,0:T(8,128)(2,1)} %slice.29.state_ref, f32[4,1,256]{2,1,0:T(1,128)} %dynamic-slice_bitcast_fusion.gain_ref, bf16[2,256,384]{2,1,0:T(8,128)(2,1)} %get-tuple-element.43.own_ref, ...), custom_call_target="tpu_custom_call" | custom-call | tf_op jit(solution)/shard_map/gate_up/gate_up/pallas_call | solution.py:24
  171.1 7.1 %all-to-all-start.5 = ((bf16[4,4,48,512]{3,2,1,0:T(8,128)(2,1)}), bf16[4,4,48,512]{3,2,1,0:T(8,128)(2,1)S(1)}, u32[]{:S(2)}, u32[]{:S(2)}) async-start(bf16[4,4,48,512]{3,2,1,0:T(8,128)(2,1)} %gate_up.1), calls=%async_computation.5 | async-start | bytes 1572864 | tf_op jit(solution)/shard_map/down/all_to_all | solution.py:377
  181.3 5.0 %all-to-all-done.5.got_ref = bf16[4,4,48,512]{3,2,1,0:T(8,128)(2,1)S(1)} async-done(((bf16[4,4,48,512]{3,2,1,0:T(8,128)(2,1)}), bf16[4,4,48,512]{3,2,1,0:T(8,128)(2,1)S(1)}, u32[]{:S(2)}, u32[]{:S(2)}) %all-to-all-start.5) | async-done | bytes 786464 | tf_op jit(solution)/shard_map/down/all_to_all | solution.py:377
  189.3 10.9 %all_to_all.50.got_ref = bf16[4,272,128]{2,1,0:T(8,128)(2,1)} all-to-all(bf16[4,272,128]{2,1,0:T(8,128)(2,1)} %get-tuple-element.50), channel_id=1, replica_groups={{0,128,256,384},{32,160,288,416},{64,192,320,448},{96,224,352,480},{1,1..., dimensions={0} | all-to-all | bytes 557056 | tf_op jit(solution)/shard_map/down/all_to_all | solution.py:377
  200.2 4.5 %combine.1 = bf16[4,8,16,1024]{3,2,1,0:T(8,128)(2,1)} custom-call(s32[3]{0:T(128)} %pad_add_fusion.place_ref, bf16[4,272,128]{2,1,0:T(8,128)(2,1)} %all_to_all.50.got_ref, bf16[2,768,256]{2,1,0:T(8,128)(2,1)} %own_ref.1, bf16[2,768,256]{2,1,0:T(8,128)(2,1)} %copy-done.6, bf16[2,768,256]{2,1,0:T(8,128)(2,1)} %copy-done.5, ...), custom_call_target="tpu_custom_call" | custom-call | tf_op jit(solution)/shard_map/down/combine/pallas_call | solution.py:24
  204.7 18.3 %all_to_all.51 = bf16[4,8,16,1024]{3,2,1,0:T(8,128)(2,1)S(1)} all-to-all(bf16[4,8,16,1024]{3,2,1,0:T(8,128)(2,1)} %combine.1), channel_id=1, replica_groups={{0,1,2,3},{4,5,6,7},{8,9,10,11},{12,13,14,15},{16,17,18,19},{20,21,22,2..., dimensions={0} | all-to-all | bytes 2097152 | tf_op jit(solution)/shard_map/output/all_to_all | solution.py:380
  223.2 31.6 %all_to_all.52 = bf16[8,16,1024]{2,1,0:T(8,128)(2,1)S(1)} all-to-all(bf16[8,16,1024]{2,1,0:T(8,128)(2,1)S(1)} %reduce_sum.76), channel_id=1, replica_groups={{0,4,8,12,16,20,24,28},{1,5,9,13,17,21,25,29},{2,6,10,14,18,22,26,30},{..., dimensions={0} | all-to-all | bytes 524288 | tf_op jit(solution)/shard_map/output/all_to_all | solution.py:384
  254.9 7.8 %all_to_all.53 = bf16[4,4,1024]{2,1,0:T(4,128)(2,1)S(1)} all-to-all(bf16[4,4,1024]{2,1,0:T(4,128)(2,1)S(1)} %reshape.212), channel_id=1, replica_groups={{0,128,256,384},{32,160,288,416},{64,192,320,448},{96,224,352,480},{1,1..., dimensions={0} | all-to-all | bytes 65536 | tf_op jit(solution)/shard_map/output/all_to_all | solution.py:377
  (125 shorter events, 55.5 us)
Async XLA Ops:
  2.2 19.9 %all-to-all-start = ((bf16[4,2,384,128]{3,2,1,0:T(8,128)(2,1)}), bf16[4,2,384,128]{3,2,1,0:T(8,128)(2,1)S(1)}, u32[]{:S(2)}, u32[]{:S(2)}) async-start(bf16[4,2,384,128]{3,2,1,0:T(8,128)(2,1)} %broadcast_in_dim.21), calls=%async_computation | async-start | bytes 1572864 | tf_op jit(solution)/shard_map/key_values/all_to_all | solution.py:377
  28.4 7.1 %copy-start.14 = (bf16[256,256]{1,0:T(8,128)(2,1)S(1)}, bf16[256,256]{1,0:T(8,128)(2,1)}, u32[]{:S(2)}) copy-start(bf16[256,256]{1,0:T(8,128)(2,1)} %param.13) | copy-start | bytes 393220
  28.4 21.2 %all-to-all-start.1 = ((bf16[4,1056,128]{2,1,0:T(8,128)(2,1)}), bf16[4,1056,128]{2,1,0:T(8,128)(2,1)S(1)}, u32[]{:S(2)}, u32[]{:S(2)}) async-start(bf16[4,1056,128]{2,1,0:T(8,128)(2,1)} %attend.1), calls=%async_computation.1 | async-start | bytes 2162688 | tf_op jit(solution)/shard_map/projection/all_to_all | solution.py:377
  54.2 4.0 %collective-permute-start = (bf16[16,128,128]{2,1,0:T(8,128)(2,1)}, bf16[16,128,128]{2,1,0:T(8,128)(2,1)S(1)}, u32[]{:S(2)}, u32[]{:S(2)}) collective-permute-start(bf16[16,128,128]{2,1,0:T(8,128)(2,1)} %get-tuple-element.31), channel_id=1, source_target_pairs={{0,1},{1,0},{2,3},{3,2},{4,5},{5,4},{6,7},{7,6},{8,9},{9,8},{10,11... | collective-permute-start | bytes 1572872 | tf_op jit(solution)/shard_map/projection/ppermute | solution.py:441
  60.1 27.9 %copy-start.20 = (s32[128,8]{0,1:T(8,128)S(1)}, s32[128,8]{0,1:T(8,128)}, u32[]{:S(2)}) copy-start(s32[128,8]{0,1:T(8,128)} %param.16) | copy-start | bytes 12292
  60.1 27.9 %copy-start.19 = (bf16[128,128]{1,0:T(8,128)(2,1)S(1)}, bf16[128,128]{1,0:T(8,128)(2,1)}, u32[]{:S(2)}) copy-start(bf16[128,128]{1,0:T(8,128)(2,1)} %param.14) | copy-start | bytes 98308
  60.1 41.0 %all-to-all-start.2 = ((bf16[16,128,128]{2,1,0:T(8,128)(2,1)}), bf16[16,128,128]{2,1,0:T(8,128)(2,1)S(1)}, u32[]{:S(2)}, u32[]{:S(2)}) async-start(bf16[16,128,128]{2,1,0:T(8,128)(2,1)} %add_convert_fusion), calls=%async_computation.2 | async-start | bytes 1048576 | tf_op jit(solution)/shard_map/projection/all_to_all | solution.py:374
  71.8 28.5 %collective-permute-start.4 = (bf16[2,768,256]{2,1,0:T(8,128)(2,1)}, bf16[2,768,256]{2,1,0:T(8,128)(2,1)S(1)}, u32[]{:S(2)}, u32[]{:S(2)}) collective-permute-start(bf16[2,768,256]{2,1,0:T(8,128)(2,1)} %own_ref.1), channel_id=1, source_target_pairs={{0,96},{32,0},{64,32},{96,64},{128,224},{160,128},{192,160},{224,1... | collective-permute-start | bytes 2359304 | tf_op jit(solution)/shard_map/projection/ppermute | solution.py:454
  73.7 27.4 %collective-permute-start.3 = (bf16[2,768,256]{2,1,0:T(8,128)(2,1)}, bf16[2,768,256]{2,1,0:T(8,128)(2,1)S(1)}, u32[]{:S(2)}, u32[]{:S(2)}) collective-permute-start(bf16[2,768,256]{2,1,0:T(8,128)(2,1)} %own_ref.1), channel_id=1, source_target_pairs={{0,32},{32,64},{64,96},{96,0},{128,160},{160,192},{192,224},{224,1... | collective-permute-start | bytes 2359304 | tf_op jit(solution)/shard_map/projection/ppermute | solution.py:454
  81.0 17.8 %collective-permute-start.1 = (bf16[3,256,384]{2,1,0:T(8,128)(2,1)}, bf16[3,256,384]{2,1,0:T(8,128)(2,1)S(1)}, u32[]{:S(2)}, u32[]{:S(2)}) collective-permute-start(bf16[3,256,384]{2,1,0:T(8,128)(2,1)} %get-tuple-element.34), channel_id=1, source_target_pairs={{0,128},{32,160},{64,192},{96,224},{128,256},{160,288},{192,320},{... | collective-permute-start | bytes 1769480 | tf_op jit(solution)/shard_map/projection/ppermute | solution.py:453
  83.9 16.4 %collective-permute-start.2 = (bf16[3,256,384]{2,1,0:T(8,128)(2,1)}, bf16[3,256,384]{2,1,0:T(8,128)(2,1)S(1)}, u32[]{:S(2)}, u32[]{:S(2)}) collective-permute-start(bf16[3,256,384]{2,1,0:T(8,128)(2,1)} %get-tuple-element.35), channel_id=1, source_target_pairs={{0,384},{32,416},{64,448},{96,480},{128,0},{160,32},{192,64},{224,... | collective-permute-start | bytes 1769480 | tf_op jit(solution)/shard_map/projection/ppermute | solution.py:453
  88.1 13.1 %collective-permute-start.5 = (bf16[136,128]{1,0:T(8,128)(2,1)S(1)}, bf16[136,128]{1,0:T(8,128)(2,1)S(1)}, u32[]{:S(2)}, u32[]{:S(2)}) collective-permute-start(bf16[136,128]{1,0:T(8,128)(2,1)S(1)} %pad_maximum_fusion), channel_id=1, source_target_pairs={{0,0},{1,1},{32,2},{33,3},{64,4},{65,5},{96,6},{97,7},{8,8},{9,9},... | collective-permute-start | bytes 104456 | tf_op jit(solution)/shard_map/turn_residual/ppermute | solution.py:397
  98.8 48.6 %copy-start.8 = (bf16[3,256,384]{2,1,0:T(8,128)(2,1)}, bf16[3,256,384]{2,1,0:T(8,128)(2,1)S(1)}, u32[]{:S(2)}) copy-start(bf16[3,256,384]{2,1,0:T(8,128)(2,1)S(1)} %collective-permute-done.1.prev_ref) | copy-start | bytes 1769476
  101.1 46.3 %copy-start.5 = (bf16[2,768,256]{2,1,0:T(8,128)(2,1)}, bf16[2,768,256]{2,1,0:T(8,128)(2,1)S(1)}, u32[]{:S(2)}) copy-start(bf16[2,768,256]{2,1,0:T(8,128)(2,1)S(1)} %collective-permute-done.4.next_ref) | copy-start | bytes 2359300
  101.1 46.3 %copy-start.6 = (bf16[2,768,256]{2,1,0:T(8,128)(2,1)}, bf16[2,768,256]{2,1,0:T(8,128)(2,1)S(1)}, u32[]{:S(2)}) copy-start(bf16[2,768,256]{2,1,0:T(8,128)(2,1)S(1)} %collective-permute-done.3.prev_ref) | copy-start | bytes 2359300
  104.3 3.3 %collective-permute-start.6 = (bf16[136,128]{1,0:T(8,128)(2,1)}, bf16[136,128]{1,0:T(8,128)(2,1)S(1)}, u32[]{:S(2)}, u32[]{:S(2)}) collective-permute-start(bf16[136,128]{1,0:T(8,128)(2,1)} %add_state.1.own_ref), channel_id=1, source_target_pairs={{0,1},{1,0},{2,3},{3,2},{4,5},{5,4},{6,7},{7,6},{8,9},{9,8},{10,11... | collective-permute-start | bytes 104456 | tf_op jit(solution)/shard_map/projection/ppermute | solution.py:463
  110.1 36.1 %all-to-all-start.3 = ((bf16[16,48,256]{2,1,0:T(8,128)(2,1)}), bf16[16,48,256]{2,1,0:T(8,128)(2,1)S(1)}, u32[]{:S(2)}, u32[]{:S(2)}) async-start(bf16[16,48,256]{2,1,0:T(8,128)(2,1)} %dispatch.1), calls=%async_computation.3 | async-start | bytes 786432 | tf_op jit(solution)/shard_map/gate_up/all_to_all | solution.py:374
  121.9 21.1 %collective-permute-start.8 = (bf16[768,256]{1,0:T(8,128)(2,1)S(1)}, bf16[768,256]{1,0:T(8,128)(2,1)S(1)}, u32[]{:S(2)}, u32[]{:S(2)}) collective-permute-start(bf16[768,256]{1,0:T(8,128)(2,1)S(1)} %slice_bitcast_fusion), channel_id=1, source_target_pairs={{0,96},{32,0},{64,32},{96,64},{128,224},{160,128},{192,160},{224,1... | collective-permute-start | bytes 1179656 | tf_op jit(solution)/shard_map/gate_up/ppermute | solution.py:483
  125.4 19.1 %collective-permute-start.7 = (bf16[768,256]{1,0:T(8,128)(2,1)S(1)}, bf16[768,256]{1,0:T(8,128)(2,1)}, u32[]{:S(2)}, u32[]{:S(2)}) collective-permute-start(bf16[768,256]{1,0:T(8,128)(2,1)S(1)} %slice_bitcast_fusion.1), channel_id=1, source_target_pairs={{0,32},{32,64},{64,96},{96,0},{128,160},{160,192},{192,224},{224,1... | collective-permute-start | bytes 1179656 | tf_op jit(solution)/shard_map/gate_up/ppermute | solution.py:482
  128.8 8.9 %collective-permute-start.10 = (bf16[256,384]{1,0:T(8,128)(2,1)S(1)}, bf16[256,384]{1,0:T(8,128)(2,1)S(1)}, u32[]{:S(2)}, u32[]{:S(2)}) collective-permute-start(bf16[256,384]{1,0:T(8,128)(2,1)S(1)} %slice_bitcast_fusion.2), channel_id=1, source_target_pairs={{0,384},{32,416},{64,448},{96,480},{128,0},{160,32},{192,64},{224,... | collective-permute-start | bytes 589832 | tf_op jit(solution)/shard_map/gate_up/ppermute | solution.py:479
  134.1 9.0 %collective-permute-start.9 = (bf16[256,384]{1,0:T(8,128)(2,1)S(1)}, bf16[256,384]{1,0:T(8,128)(2,1)S(1)}, u32[]{:S(2)}, u32[]{:S(2)}) collective-permute-start(bf16[256,384]{1,0:T(8,128)(2,1)S(1)} %slice_bitcast_fusion.3), channel_id=1, source_target_pairs={{0,128},{32,160},{64,192},{96,224},{128,256},{160,288},{192,320},{... | collective-permute-start | bytes 589832 | tf_op jit(solution)/shard_map/gate_up/ppermute | solution.py:478
  147.5 18.3 %all-to-all-start.4 = ((bf16[4,4,160,256]{3,2,1,0:T(8,128)(2,1)}), bf16[4,4,160,256]{3,2,1,0:T(8,128)(2,1)S(1)}, u32[]{:S(2)}, u32[]{:S(2)}) async-start(bf16[4,4,160,256]{3,2,1,0:T(8,128)(2,1)} %broadcast_in_dim.23), calls=%async_computation.4 | async-start | bytes 2621440 | tf_op jit(solution)/shard_map/gate_up/all_to_all | solution.py:377
  171.1 15.1 %all-to-all-start.5 = ((bf16[4,4,48,512]{3,2,1,0:T(8,128)(2,1)}), bf16[4,4,48,512]{3,2,1,0:T(8,128)(2,1)S(1)}, u32[]{:S(2)}, u32[]{:S(2)}) async-start(bf16[4,4,48,512]{3,2,1,0:T(8,128)(2,1)} %gate_up.1), calls=%async_computation.5 | async-start | bytes 1572864 | tf_op jit(solution)/shard_map/down/all_to_all | solution.py:377
  223.0 39.7 %copy-start.18 = (f32[8,4096]{1,0:T(8,128)S(1)}, f32[8,4096]{1,0:T(8,128)}, u32[]{:S(2)}) copy-start(f32[8,4096]{1,0:T(8,128)} %get-tuple-element.49) | copy-start | bytes 393220
  (16 other events, 33.2 us)

commit v4 on v3

--- a/solution.py
+++ b/solution.py
@@ -12,22 +12,24 @@
 QUERY_HEADS = 64
 KEY_VALUE_HEADS = 4
 FLOOR = -1e30
-VMEM_BYTES = 56 * 1024 * 1024
 f32 = jnp.float32
 bf16 = jnp.bfloat16
 
 
-def run(body, out_shape, *operands, place=None, flops=0, moved=0, scratch=(), name=None):
+def run(body, out_shape, *operands, place=None, left=(), room=16, flops=0, moved=0, scratch=(), name=None):
     vmem = pl.BlockSpec(memory_space=pltpu.VMEM)
+    spaces = [
+        pl.BlockSpec(memory_space=pl.ANY) if i in left else vmem for i in range(len(operands))
+    ]
     smem = pl.BlockSpec(memory_space=pltpu.SMEM)
     placed = [] if place is None else [place]
     return pl.pallas_call(
         body,
         out_shape=out_shape,
-        in_specs=[smem] * len(placed) + [vmem] * len(operands),
+        in_specs=[smem] * len(placed) + spaces,
         out_specs=jax.tree.map(lambda _: vmem, out_shape),
         scratch_shapes=list(scratch),
-        compiler_params=pltpu.CompilerParams(vmem_limit_bytes=VMEM_BYTES),
+        compiler_params=pltpu.CompilerParams(vmem_limit_bytes=room * 1024 * 1024),
         cost_estimate=pl.CostEstimate(flops=flops, bytes_accessed=moved, transcendentals=0),
         name=name,
     )(*placed, *operands)
@@ -44,11 +46,8 @@
     near, far = seq_index // sides, seq_index % sides
     heads = blocks // sides
     total = heads * rows
-    wide = sides * span
-    lane = lax.broadcasted_iota(jnp.int32, (1, wide), 1)
-    within = lane % span
-    pos = ((lane // span) * sides + far) * rows + within - cached
-    pos = jnp.where(within < cached, -1, pos)
+    lane = lax.broadcasted_iota(jnp.int32, (1, rows), 1)
+    pos = [(part * sides + far) * rows + lane for part in range(sides)]
     token = lax.broadcasted_iota(jnp.int32, (total, 1), 0) % rows
     column = lax.broadcasted_iota(jnp.int32, (rows, 128), 1)
     factor = scale * math.log2(math.e)
@@ -58,14 +57,16 @@
         query_pos = (near * sides + b) * rows + token
         top = jnp.full((total, 128), FLOOR, f32)
         for part in range(sides):
-            cut = slice(part * span, (part + 1) * span)
             s = lax.dot_general(
                 q, kv_ref[part, 0], (((1,), (1,)), ((), ())), preferred_element_type=f32
             )
-            s = jnp.where(pos[:, cut] <= query_pos, s, FLOOR)
-            s_ref[b % 2, :, cut] = s
-            for k in range(span // 128):
+            fresh = jnp.where(pos[part] <= query_pos, s[:, cached:], FLOOR)
+            s_ref[b % 2, :, part * span : part * span + cached] = s[:, :cached]
+            s_ref[b % 2, :, part * span + cached : (part + 1) * span] = fresh
+            for k in range(cached // 128):
                 top = jnp.maximum(top, s[:, k * 128 : (k + 1) * 128])
+            for k in range(rows // 128):
+                top = jnp.maximum(top, fresh[:, k * 128 : (k + 1) * 128])
         top = jnp.max(top, axis=1, keepdims=True)
         acc = jnp.zeros((total, width), f32)
         sums = jnp.zeros((total, 128), f32)
@@ -169,7 +170,10 @@
     out_ref[...] = rows.astype(bf16).reshape(out_ref.shape)
 
 
-def split_columns(place_ref, w_ref, own_ref, next_ref, prev_ref, all_ref):
+def split_columns(place_ref, w_in_ref, own_ref, next_ref, prev_ref, all_ref, w_ref, sem):
+    copy = pltpu.make_async_copy(w_in_ref, w_ref, sem)
+    copy.start()
+    copy.wait()
     sides = all_ref.shape[0]
     near = place_ref[0] // sides
     members, depth, columns = w_ref.shape
@@ -193,26 +197,31 @@
         ref[2] = all_ref[far, m]
 
 
-def gate_up(place_ref, x_ref, state_ref, gain_ref, own_ref, prev_ref, next_ref, opp_ref, opp2_ref, out_ref, *, capacity):
-    w_refs = (
-        (own_ref.at[0], own_ref.at[1]),
-        (prev_ref.at[0], prev_ref.at[1]),
-        (opp_ref, opp2_ref),
-        (next_ref.at[0], next_ref.at[1]),
+def gate_up(place_ref, x_ref, state_ref, gain_ref, own_ref, prev_ref, next_ref, opp_ref, opp2_ref, out_ref, scaled_ref, weight_ref, sems, *, capacity):
+    sides, _, slots, depth = x_ref.shape
+    parts = (
+        (own_ref, weight_ref.at[:, 0:depth]),
+        (prev_ref.at[0:2], weight_ref.at[:, depth : 2 * depth]),
+        (opp_ref, weight_ref.at[0, 2 * depth : 3 * depth]),
+        (opp2_ref, weight_ref.at[1, 2 * depth : 3 * depth]),
+        (next_ref.at[0:2], weight_ref.at[:, 3 * depth : 4 * depth]),
     )
-    sides, _, slots, depth = x_ref.shape
+    copies = [pltpu.make_async_copy(a, b, sems.at[k]) for k, (a, b) in enumerate(parts)]
+    for copy in copies:
+        copy.start()
     near = place_ref[0] // sides
     total = sides * slots
     columns = own_ref.shape[-1]
-    sums = [jnp.zeros((total, columns), f32)] * 2
     squares = jnp.zeros((total, 1), f32)
     for k in range(sides):
         block = lax.rem(near + sides - k, sides)
         x = x_ref[:, block].reshape(total, depth).astype(f32)
         squares = squares + jnp.sum(x * x, axis=1, keepdims=True)
-        scaled = (x * gain_ref[block]).astype(bf16)
-        for m in range(2):
-            sums[m] = sums[m] + jnp.dot(scaled, w_refs[k][m][...], preferred_element_type=f32)
+        scaled_ref[:, k * depth : (k + 1) * depth] = (x * gain_ref[block]).astype(bf16)
+    for copy in copies:
+        copy.wait()
+    scaled = scaled_ref[...]
+    sums = [jnp.dot(scaled, weight_ref[m], preferred_element_type=f32) for m in range(2)]
     second = lax.broadcasted_iota(jnp.int32, (total, 1), 0) % (2 * capacity) >= capacity
     partial = jnp.where(second, sums[1], sums[0])
     high = squares.astype(bf16).astype(f32)
@@ -438,8 +447,8 @@
             place=place,
             name="project",
         )
+        weights, w_out, send = lax.optimization_barrier((w_gate_up, w_down, send))
         paired = (keep.astype(f32) + lax.ppermute(send, "exp", swap).astype(f32)).astype(bf16)
-        weights, w_out, paired = lax.optimization_barrier((w_gate_up, w_down, paired))
         piece = (members, feature_block, gate_columns // sides)
         longer = (members + 1,) + piece[1:]
         w_own, w_next, w_prev = run(
@@ -447,7 +456,12 @@
             [shape(piece), shape(longer), shape(longer)],
             weights,
             place=place,
-            scratch=[pltpu.VMEM((sides,) + piece, bf16)],
+            left=(0,),
+            scratch=[
+                pltpu.VMEM((sides,) + piece, bf16),
+                pltpu.VMEM(w_gate_up.shape, bf16),
+                pltpu.SemaphoreType.DMA(()),
+            ],
             name="split_columns",
         )
         near_y = (lax.ppermute(w_next, "seq", shift_y[1]), lax.ppermute(w_prev, "seq", shift_y[-1]))
@@ -501,6 +515,13 @@
             *near_y,
             *far_y,
             place=place,
+            left=range(3, 8),
+            room=56,
+            scratch=[
+                pltpu.VMEM((n_seq * slots, sides * feature_block), bf16),
+                pltpu.VMEM((members, sides * feature_block, piece[-1]), bf16),
+                pltpu.SemaphoreType.DMA((5,)),
+            ],
             name="gate_up",
         )
     with jax.named_scope("tables"):

time: 265 us -> 247 us (0.932)
  Pallas kernels: 27 us -> 17.8 us
  blocking collectives: 97.4 us -> 93.3 us
  waiting for transfers between devices: 36.2 us -> 33.4 us
    pallas_call x8, Pallas kernels: 27 us -> 17.8 us  [run(): pl.pallas_call(body, out_shape=out_shape, in_specs=[smem] * len(placed) +...]
    mul x6, local copies, waits for them, and re-layouts: 0.83 us -> 4.64 us  [local(): table = (table * spot).transpose(2, 3, 0, 1, 4, 5)]
    unnamed x49 -> x39, local copies, waits for them, and re-layouts: 8.33 us -> 4.53 us
  transfers between devices with their start and end apart: 17 -> 17, of which waited for: 9 -> 9; matrix products, arithmetic and copies ran while one was open for 3% -> 4% of each run, Pallas kernels for 1% -> 1%
where the time goes in v4:
time: 247 us; the launch traced here: 245 us
  blocking collectives  93.3 us (38%)
  starting transfers between devices  80.9 us (33%)
  waiting for transfers between devices  33.4 us (14%)
  Pallas kernels  17.8 us (7%)
  local copies, waits for them, and re-layouts  16.6 us (7%)
  other arithmetic  2.68 us (1%)
    all_to_all x1, blocking collectives, over_far(): return lax.all_to_all(value, 'exp', 0, 0, tiled=True, axis_index_groups=far)  31.7 us
    all_to_all x2, starting transfers between devices, over_chips(): lax.all_to_all(value, 'exp', 0, 0, tiled=True, axis_index_groups=chips)  23.5 us
    all_to_all x4, starting transfers between devices, over_seq(): lax.all_to_all(value, 'seq', 0, 0, tiled=True, axis_index_groups=groups)  23.1 us
    pallas_call x8, Pallas kernels, run(): pl.pallas_call(body, out_shape=out_shape, in_specs=[smem] * len(placed) +...  17.8 us
    all_to_all x1, blocking collectives, sum_near(): lax.all_to_all(value, 'exp', 0, 0, tiled=True, axis_index_groups=near)  17.1 us
    all_to_all x2, blocking collectives, over_seq(): lax.all_to_all(value, 'seq', 0, 0, tiled=True, axis_index_groups=groups)  16.9 us
    all_to_all x4, waiting for transfers between devices, over_seq(): lax.all_to_all(value, 'seq', 0, 0, tiled=True, axis_index_groups=groups)  14.3 us
    all_gather x1, blocking collectives, local(): lax.all_gather(queries.transpose(1, 0, 2), 'seq', axis=0, tiled=True, axi...  14 us
  transfers between devices with their start and end apart: 17, of which 9 were waited for; matrix products, arithmetic and copies ran while one was open for 4% of the time, Pallas kernels for 1%

profile of v4, /device:TPU:2, one launch (start us, length us, event | category | flops | bytes accessed | tf_op | source)
XLA Modules:
  0.0 245.2 jit_solution(12778563826631797429)
XLA Ops:
  2.2 4.5 %all-to-all-start = ((bf16[4,2,384,128]{3,2,1,0:T(8,128)(2,1)}), bf16[4,2,384,128]{3,2,1,0:T(8,128)(2,1)S(1)}, u32[]{:S(2)}, u32[]{:S(2)}) async-start(bf16[4,2,384,128]{3,2,1,0:T(8,128)(2,1)} %broadcast_in_dim.21), calls=%async_computation | async-start | bytes 1572864 | tf_op jit(solution)/shard_map/key_values/all_to_all | solution.py:386
  6.7 14.0 %all_gather.6.q_ref = bf16[8,128,128]{2,1,0:T(8,128)(2,1)S(1)} all-gather(bf16[2,128,128]{2,1,0:T(8,128)(2,1)S(1)} %bitcast.42), channel_id=1, replica_groups={{0,32,64,96},{128,160,192,224},{256,288,320,352},{384,416,448,480},{1,3..., dimensions={0}, use_global_device_ids=true | all-gather | bytes 327680 | tf_op jit(solution)/shard_map/key_values/all_gather | solution.py:414
  20.8 4.4 %attend.1 = bf16[4,1056,128]{2,1,0:T(8,128)(2,1)} custom-call(s32[3]{0:T(128)S(1)} %pad_add_fusion.place_ref, bf16[8,128,128]{2,1,0:T(8,128)(2,1)S(1)} %all_gather.6.q_ref, bf16[4,2,384,128]{3,2,1,0:T(8,128)(2,1)S(1)} %all-to-all-done.kv_ref), custom_call_target="tpu_custom_call" | custom-call | flops 805306368 | bytes 786432 | tf_op jit(solution)/shard_map/attention/attend/pallas_call | solution.py:26
  25.2 6.8 %all-to-all-start.1 = ((bf16[4,1056,128]{2,1,0:T(8,128)(2,1)}), bf16[4,1056,128]{2,1,0:T(8,128)(2,1)S(1)}, u32[]{:S(2)}, u32[]{:S(2)}) async-start(bf16[4,1056,128]{2,1,0:T(8,128)(2,1)} %attend.1), calls=%async_computation.1 | async-start | bytes 2162688 | tf_op jit(solution)/shard_map/projection/all_to_all | solution.py:386
  32.1 13.6 %all_gather.7.w_ref = bf16[1024,256]{1,0:T(8,128)(2,1)S(1)} all-gather(bf16[256,256]{1,0:T(8,128)(2,1)S(1)} %copy-done.12), channel_id=1, replica_groups={{0,128,256,384},{32,160,288,416},{64,192,320,448},{96,224,352,480},{1,1..., dimensions={0}, use_global_device_ids=true | all-gather | bytes 655360 | tf_op jit(solution)/shard_map/attention/all_gather | solution.py:432
  52.2 11.7 %all-to-all-start.2 = ((bf16[16,128,128]{2,1,0:T(8,128)(2,1)}), bf16[16,128,128]{2,1,0:T(8,128)(2,1)S(1)}, u32[]{:S(2)}, u32[]{:S(2)}) async-start(bf16[16,128,128]{2,1,0:T(8,128)(2,1)} %add_convert_fusion), calls=%async_computation.2 | async-start | bytes 1048576 | tf_op jit(solution)/shard_map/projection/all_to_all | solution.py:383
  66.4 3.4 %collective-permute-start.3 = (bf16[2,768,256]{2,1,0:T(8,128)(2,1)}, bf16[2,768,256]{2,1,0:T(8,128)(2,1)S(1)}, u32[]{:S(2)}, u32[]{:S(2)}) collective-permute-start(bf16[2,768,256]{2,1,0:T(8,128)(2,1)} %own_ref.1), channel_id=1, source_target_pairs={{0,32},{32,64},{64,96},{96,0},{128,160},{160,192},{192,224},{224,1... | collective-permute-start | bytes 2359304 | tf_op jit(solution)/shard_map/projection/ppermute | solution.py:468
  73.4 3.0 %collective-permute-start.1 = (bf16[3,256,384]{2,1,0:T(8,128)(2,1)S(1)}, bf16[3,256,384]{2,1,0:T(8,128)(2,1)S(1)}, u32[]{:S(2)}, u32[]{:S(2)}) collective-permute-start(bf16[3,256,384]{2,1,0:T(8,128)(2,1)S(1)} %get-tuple-element.34), channel_id=1, source_target_pairs={{0,128},{32,160},{64,192},{96,224},{128,256},{160,288},{192,320},{... | collective-permute-start | bytes 1769480 | tf_op jit(solution)/shard_map/projection/ppermute | solution.py:467
  76.4 4.1 %collective-permute-start.2 = (bf16[3,256,384]{2,1,0:T(8,128)(2,1)S(1)}, bf16[3,256,384]{2,1,0:T(8,128)(2,1)S(1)}, u32[]{:S(2)}, u32[]{:S(2)}) collective-permute-start(bf16[3,256,384]{2,1,0:T(8,128)(2,1)S(1)} %get-tuple-element.35), channel_id=1, source_target_pairs={{0,384},{32,416},{64,448},{96,480},{128,0},{160,32},{192,64},{224,... | collective-permute-start | bytes 1769480 | tf_op jit(solution)/shard_map/projection/ppermute | solution.py:467
  80.5 4.6 %collective-permute-start.5 = (bf16[136,128]{1,0:T(8,128)(2,1)S(1)}, bf16[136,128]{1,0:T(8,128)(2,1)S(1)}, u32[]{:S(2)}, u32[]{:S(2)}) collective-permute-start(bf16[136,128]{1,0:T(8,128)(2,1)S(1)} %pad_maximum_fusion), channel_id=1, source_target_pairs={{0,0},{1,1},{32,2},{33,3},{64,4},{65,5},{96,6},{97,7},{8,8},{9,9},... | collective-permute-start | bytes 104456 | tf_op jit(solution)/shard_map/turn_residual/ppermute | solution.py:406
  85.1 6.0 %collective-permute-done.1.prev_ref = bf16[3,256,384]{2,1,0:T(8,128)(2,1)S(1)} collective-permute-done((bf16[3,256,384]{2,1,0:T(8,128)(2,1)S(1)}, bf16[3,256,384]{2,1,0:T(8,128)(2,1)S(1)}, u32[]{:S(2)}, u32[]{:S(2)}) %collective-permute-start.1) | collective-permute-done | bytes 589856 | tf_op jit(solution)/shard_map/projection/ppermute | solution.py:467
  98.2 11.7 %all-to-all-start.3 = ((bf16[16,48,256]{2,1,0:T(8,128)(2,1)}), bf16[16,48,256]{2,1,0:T(8,128)(2,1)S(1)}, u32[]{:S(2)}, u32[]{:S(2)}) async-start(bf16[16,48,256]{2,1,0:T(8,128)(2,1)} %dispatch.1), calls=%async_computation.3 | async-start | bytes 786432 | tf_op jit(solution)/shard_map/gate_up/all_to_all | solution.py:383
  110.0 3.4 %collective-permute-start.8 = (bf16[768,256]{1,0:T(8,128)(2,1)S(1)}, bf16[768,256]{1,0:T(8,128)(2,1)S(1)}, u32[]{:S(2)}, u32[]{:S(2)}) collective-permute-start(bf16[768,256]{1,0:T(8,128)(2,1)S(1)} %slice_bitcast_fusion), channel_id=1, source_target_pairs={{0,96},{32,0},{64,32},{96,64},{128,224},{160,128},{192,160},{224,1... | collective-permute-start | bytes 1179656 | tf_op jit(solution)/shard_map/gate_up/ppermute | solution.py:497
  117.8 5.3 %collective-permute-start.10 = (bf16[256,384]{1,0:T(8,128)(2,1)S(1)}, bf16[256,384]{1,0:T(8,128)(2,1)S(1)}, u32[]{:S(2)}, u32[]{:S(2)}) collective-permute-start(bf16[256,384]{1,0:T(8,128)(2,1)S(1)} %slice_bitcast_fusion.2), channel_id=1, source_target_pairs={{0,384},{32,416},{64,448},{96,480},{128,0},{160,32},{192,64},{224,... | collective-permute-start | bytes 589832 | tf_op jit(solution)/shard_map/gate_up/ppermute | solution.py:493
  126.7 5.3 %collective-permute-done.9.opp_ref = bf16[256,384]{1,0:T(8,128)(2,1)S(1)} collective-permute-done((bf16[256,384]{1,0:T(8,128)(2,1)S(1)}, bf16[256,384]{1,0:T(8,128)(2,1)S(1)}, u32[]{:S(2)}, u32[]{:S(2)}) %collective-permute-start.9) | collective-permute-done | bytes 196640 | tf_op jit(solution)/shard_map/gate_up/ppermute | solution.py:492
  135.5 4.8 %all-to-all-start.4 = ((bf16[4,4,160,256]{3,2,1,0:T(8,128)(2,1)}), bf16[4,4,160,256]{3,2,1,0:T(8,128)(2,1)}, u32[]{:S(2)}, u32[]{:S(2)}) async-start(bf16[4,4,160,256]{3,2,1,0:T(8,128)(2,1)} %broadcast_in_dim.23), calls=%async_computation.4 | async-start | bytes 2621440 | tf_op jit(solution)/shard_map/gate_up/all_to_all | solution.py:386
  141.8 13.2 %all-to-all-done.4.x_ref = bf16[4,4,160,256]{3,2,1,0:T(8,128)(2,1)} async-done(((bf16[4,4,160,256]{3,2,1,0:T(8,128)(2,1)}), bf16[4,4,160,256]{3,2,1,0:T(8,128)(2,1)}, u32[]{:S(2)}, u32[]{:S(2)}) %all-to-all-start.4) | async-done | bytes 1310752 | tf_op jit(solution)/shard_map/gate_up/all_to_all | solution.py:386
  155.0 5.4 %gate_up.1 = bf16[4,4,48,512]{3,2,1,0:T(8,128)(2,1)} custom-call(s32[3]{0:T(128)} %copy-done.5, bf16[4,4,160,256]{3,2,1,0:T(8,128)(2,1)} %all-to-all-done.4.x_ref, bf16[4,4,8,256]{3,2,1,0:T(8,128)(2,1)} %slice.29.state_ref, f32[4,1,256]{2,1,0:T(1,128)} %dynamic-slice_bitcast_fusion.gain_ref, bf16[2,256,384]{2,1,0:T(8,128)(2,1)} %copy-done.4, ...), custom_call_target="tpu_custom_call" | custom-call | tf_op jit(solution)/shard_map/gate_up/gate_up/pallas_call | solution.py:26
  160.4 7.0 %all-to-all-start.5 = ((bf16[4,4,48,512]{3,2,1,0:T(8,128)(2,1)}), bf16[4,4,48,512]{3,2,1,0:T(8,128)(2,1)S(1)}, u32[]{:S(2)}, u32[]{:S(2)}) async-start(bf16[4,4,48,512]{3,2,1,0:T(8,128)(2,1)} %gate_up.1), calls=%async_computation.5 | async-start | bytes 1572864 | tf_op jit(solution)/shard_map/down/all_to_all | solution.py:386
  175.8 9.1 %all_to_all.50.got_ref = bf16[4,272,128]{2,1,0:T(8,128)(2,1)S(1)} all-to-all(bf16[4,272,128]{2,1,0:T(8,128)(2,1)S(1)} %get-tuple-element.50), channel_id=1, replica_groups={{0,128,256,384},{32,160,288,416},{64,192,320,448},{96,224,352,480},{1,1..., dimensions={0} | all-to-all | bytes 557056 | tf_op jit(solution)/shard_map/down/all_to_all | solution.py:386
  184.9 2.7 %combine.1 = bf16[4,8,16,1024]{3,2,1,0:T(8,128)(2,1)S(1)} custom-call(s32[3]{0:T(128)S(1)} %copy-done.6, bf16[4,272,128]{2,1,0:T(8,128)(2,1)S(1)} %all_to_all.50.got_ref, bf16[2,768,256]{2,1,0:T(8,128)(2,1)} %own_ref.1, bf16[2,768,256]{2,1,0:T(8,128)(2,1)S(1)} %collective-permute-done.3.prev_ref, bf16[2,768,256]{2,1,0:T(8,128)(2,1)S(1)} %collective-permute-done.4.next_ref, ...), custom_call_target="tpu_custom_call" | custom-call | tf_op jit(solution)/shard_map/down/combine/pallas_call | solution.py:26
  187.6 17.1 %all_to_all.51 = bf16[4,8,16,1024]{3,2,1,0:T(8,128)(2,1)S(1)} all-to-all(bf16[4,8,16,1024]{3,2,1,0:T(8,128)(2,1)S(1)} %combine.1), channel_id=1, replica_groups={{0,1,2,3},{4,5,6,7},{8,9,10,11},{12,13,14,15},{16,17,18,19},{20,21,22,2..., dimensions={0} | all-to-all | bytes 2097152 | tf_op jit(solution)/shard_map/output/all_to_all | solution.py:389
  204.9 31.7 %all_to_all.52 = bf16[8,16,1024]{2,1,0:T(8,128)(2,1)S(1)} all-to-all(bf16[8,16,1024]{2,1,0:T(8,128)(2,1)S(1)} %reduce_sum.76), channel_id=1, replica_groups={{0,4,8,12,16,20,24,28},{1,5,9,13,17,21,25,29},{2,6,10,14,18,22,26,30},{..., dimensions={0} | all-to-all | bytes 524288 | tf_op jit(solution)/shard_map/output/all_to_all | solution.py:393
  236.7 7.8 %all_to_all.53 = bf16[4,4,1024]{2,1,0:T(4,128)(2,1)S(1)} all-to-all(bf16[4,4,1024]{2,1,0:T(4,128)(2,1)S(1)} %reshape.212), channel_id=1, replica_groups={{0,128,256,384},{32,160,288,416},{64,192,320,448},{96,224,352,480},{1,1..., dimensions={0} | all-to-all | bytes 65536 | tf_op jit(solution)/shard_map/output/all_to_all | solution.py:386
  (115 shorter events, 44.2 us)
Async XLA Ops:
  2.2 18.6 %all-to-all-start = ((bf16[4,2,384,128]{3,2,1,0:T(8,128)(2,1)}), bf16[4,2,384,128]{3,2,1,0:T(8,128)(2,1)S(1)}, u32[]{:S(2)}, u32[]{:S(2)}) async-start(bf16[4,2,384,128]{3,2,1,0:T(8,128)(2,1)} %broadcast_in_dim.21), calls=%async_computation | async-start | bytes 1572864 | tf_op jit(solution)/shard_map/key_values/all_to_all | solution.py:386
  20.8 75.7 %copy-start.5 = (s32[3]{0:T(128)}, s32[3]{0:T(128)S(1)}, u32[]{:S(2)}) copy-start(s32[3]{0:T(128)S(1)} %pad_add_fusion.place_ref) | copy-start | bytes 40
  25.2 20.4 %all-to-all-start.1 = ((bf16[4,1056,128]{2,1,0:T(8,128)(2,1)}), bf16[4,1056,128]{2,1,0:T(8,128)(2,1)S(1)}, u32[]{:S(2)}, u32[]{:S(2)}) async-start(bf16[4,1056,128]{2,1,0:T(8,128)(2,1)} %attend.1), calls=%async_computation.1 | async-start | bytes 2162688 | tf_op jit(solution)/shard_map/projection/all_to_all | solution.py:386
  47.4 3.8 %collective-permute-start = (bf16[16,128,128]{2,1,0:T(8,128)(2,1)S(1)}, bf16[16,128,128]{2,1,0:T(8,128)(2,1)S(1)}, u32[]{:S(2)}, u32[]{:S(2)}) collective-permute-start(bf16[16,128,128]{2,1,0:T(8,128)(2,1)S(1)} %get-tuple-element.32), channel_id=1, source_target_pairs={{0,1},{1,0},{2,3},{3,2},{4,5},{5,4},{6,7},{7,6},{8,9},{9,8},{10,11... | collective-permute-start | bytes 1572872 | tf_op jit(solution)/shard_map/projection/ppermute | solution.py:451
  52.2 28.3 %copy-start.15 = (s32[128,8]{0,1:T(8,128)S(1)}, s32[128,8]{0,1:T(8,128)}, u32[]{:S(2)}) copy-start(s32[128,8]{0,1:T(8,128)} %param.16) | copy-start | bytes 12292
  52.2 28.3 %copy-start.14 = (bf16[128,128]{1,0:T(8,128)(2,1)S(1)}, bf16[128,128]{1,0:T(8,128)(2,1)}, u32[]{:S(2)}) copy-start(bf16[128,128]{1,0:T(8,128)(2,1)} %param.14) | copy-start | bytes 98308
  52.2 41.2 %all-to-all-start.2 = ((bf16[16,128,128]{2,1,0:T(8,128)(2,1)}), bf16[16,128,128]{2,1,0:T(8,128)(2,1)S(1)}, u32[]{:S(2)}, u32[]{:S(2)}) async-start(bf16[16,128,128]{2,1,0:T(8,128)(2,1)} %add_convert_fusion), calls=%async_computation.2 | async-start | bytes 1048576 | tf_op jit(solution)/shard_map/projection/all_to_all | solution.py:383
  63.9 28.6 %collective-permute-start.4 = (bf16[2,768,256]{2,1,0:T(8,128)(2,1)}, bf16[2,768,256]{2,1,0:T(8,128)(2,1)S(1)}, u32[]{:S(2)}, u32[]{:S(2)}) collective-permute-start(bf16[2,768,256]{2,1,0:T(8,128)(2,1)} %own_ref.1), channel_id=1, source_target_pairs={{0,96},{32,0},{64,32},{96,64},{128,224},{160,128},{192,160},{224,1... | collective-permute-start | bytes 2359304 | tf_op jit(solution)/shard_map/projection/ppermute | solution.py:468
  66.4 27.0 %collective-permute-start.3 = (bf16[2,768,256]{2,1,0:T(8,128)(2,1)}, bf16[2,768,256]{2,1,0:T(8,128)(2,1)S(1)}, u32[]{:S(2)}, u32[]{:S(2)}) collective-permute-start(bf16[2,768,256]{2,1,0:T(8,128)(2,1)} %own_ref.1), channel_id=1, source_target_pairs={{0,32},{32,64},{64,96},{96,0},{128,160},{160,192},{192,224},{224,1... | collective-permute-start | bytes 2359304 | tf_op jit(solution)/shard_map/projection/ppermute | solution.py:468
  73.4 17.6 %collective-permute-start.1 = (bf16[3,256,384]{2,1,0:T(8,128)(2,1)S(1)}, bf16[3,256,384]{2,1,0:T(8,128)(2,1)S(1)}, u32[]{:S(2)}, u32[]{:S(2)}) collective-permute-start(bf16[3,256,384]{2,1,0:T(8,128)(2,1)S(1)} %get-tuple-element.34), channel_id=1, source_target_pairs={{0,128},{32,160},{64,192},{96,224},{128,256},{160,288},{192,320},{... | collective-permute-start | bytes 1769480 | tf_op jit(solution)/shard_map/projection/ppermute | solution.py:467
  76.4 16.1 %collective-permute-start.2 = (bf16[3,256,384]{2,1,0:T(8,128)(2,1)S(1)}, bf16[3,256,384]{2,1,0:T(8,128)(2,1)S(1)}, u32[]{:S(2)}, u32[]{:S(2)}) collective-permute-start(bf16[3,256,384]{2,1,0:T(8,128)(2,1)S(1)} %get-tuple-element.35), channel_id=1, source_target_pairs={{0,384},{32,416},{64,448},{96,480},{128,0},{160,32},{192,64},{224,... | collective-permute-start | bytes 1769480 | tf_op jit(solution)/shard_map/projection/ppermute | solution.py:467
  80.5 12.9 %collective-permute-start.5 = (bf16[136,128]{1,0:T(8,128)(2,1)S(1)}, bf16[136,128]{1,0:T(8,128)(2,1)S(1)}, u32[]{:S(2)}, u32[]{:S(2)}) collective-permute-start(bf16[136,128]{1,0:T(8,128)(2,1)S(1)} %pad_maximum_fusion), channel_id=1, source_target_pairs={{0,0},{1,1},{32,2},{33,3},{64,4},{65,5},{96,6},{97,7},{8,8},{9,9},... | collective-permute-start | bytes 104456 | tf_op jit(solution)/shard_map/turn_residual/ppermute | solution.py:406
  93.4 3.1 %collective-permute-start.6 = (bf16[136,128]{1,0:T(8,128)(2,1)S(1)}, bf16[136,128]{1,0:T(8,128)(2,1)S(1)}, u32[]{:S(2)}, u32[]{:S(2)}) collective-permute-start(bf16[136,128]{1,0:T(8,128)(2,1)S(1)} %add_state.1.own_ref), channel_id=1, source_target_pairs={{0,1},{1,0},{2,3},{3,2},{4,5},{5,4},{6,7},{7,6},{8,9},{9,8},{10,11... | collective-permute-start | bytes 104456 | tf_op jit(solution)/shard_map/projection/ppermute | solution.py:477
  98.2 36.1 %all-to-all-start.3 = ((bf16[16,48,256]{2,1,0:T(8,128)(2,1)}), bf16[16,48,256]{2,1,0:T(8,128)(2,1)S(1)}, u32[]{:S(2)}, u32[]{:S(2)}) async-start(bf16[16,48,256]{2,1,0:T(8,128)(2,1)} %dispatch.1), calls=%async_computation.3 | async-start | bytes 786432 | tf_op jit(solution)/shard_map/gate_up/all_to_all | solution.py:383
  110.0 22.0 %collective-permute-start.8 = (bf16[768,256]{1,0:T(8,128)(2,1)S(1)}, bf16[768,256]{1,0:T(8,128)(2,1)S(1)}, u32[]{:S(2)}, u32[]{:S(2)}) collective-permute-start(bf16[768,256]{1,0:T(8,128)(2,1)S(1)} %slice_bitcast_fusion), channel_id=1, source_target_pairs={{0,96},{32,0},{64,32},{96,64},{128,224},{160,128},{192,160},{224,1... | collective-permute-start | bytes 1179656 | tf_op jit(solution)/shard_map/gate_up/ppermute | solution.py:497
  113.5 19.3 %collective-permute-start.7 = (bf16[768,256]{1,0:T(8,128)(2,1)S(1)}, bf16[768,256]{1,0:T(8,128)(2,1)S(1)}, u32[]{:S(2)}, u32[]{:S(2)}) collective-permute-start(bf16[768,256]{1,0:T(8,128)(2,1)S(1)} %slice_bitcast_fusion.1), channel_id=1, source_target_pairs={{0,32},{32,64},{64,96},{96,0},{128,160},{160,192},{192,224},{224,1... | collective-permute-start | bytes 1179656 | tf_op jit(solution)/shard_map/gate_up/ppermute | solution.py:496
  117.8 8.9 %collective-permute-start.10 = (bf16[256,384]{1,0:T(8,128)(2,1)S(1)}, bf16[256,384]{1,0:T(8,128)(2,1)S(1)}, u32[]{:S(2)}, u32[]{:S(2)}) collective-permute-start(bf16[256,384]{1,0:T(8,128)(2,1)S(1)} %slice_bitcast_fusion.2), channel_id=1, source_target_pairs={{0,384},{32,416},{64,448},{96,480},{128,0},{160,32},{192,64},{224,... | collective-permute-start | bytes 589832 | tf_op jit(solution)/shard_map/gate_up/ppermute | solution.py:493
  123.1 9.0 %collective-permute-start.9 = (bf16[256,384]{1,0:T(8,128)(2,1)S(1)}, bf16[256,384]{1,0:T(8,128)(2,1)S(1)}, u32[]{:S(2)}, u32[]{:S(2)}) collective-permute-start(bf16[256,384]{1,0:T(8,128)(2,1)S(1)} %slice_bitcast_fusion.3), channel_id=1, source_target_pairs={{0,128},{32,160},{64,192},{96,224},{128,256},{160,288},{192,320},{... | collective-permute-start | bytes 589832 | tf_op jit(solution)/shard_map/gate_up/ppermute | solution.py:492
  126.7 8.8 %copy-start.9 = (bf16[256,384]{1,0:T(8,128)(2,1)}, bf16[256,384]{1,0:T(8,128)(2,1)S(1)}, u32[]{:S(2)}) copy-start(bf16[256,384]{1,0:T(8,128)(2,1)S(1)} %collective-permute-done.10.opp2_ref) | copy-start | bytes 589828
  135.5 19.4 %all-to-all-start.4 = ((bf16[4,4,160,256]{3,2,1,0:T(8,128)(2,1)}), bf16[4,4,160,256]{3,2,1,0:T(8,128)(2,1)}, u32[]{:S(2)}, u32[]{:S(2)}) async-start(bf16[4,4,160,256]{3,2,1,0:T(8,128)(2,1)} %broadcast_in_dim.23), calls=%async_computation.4 | async-start | bytes 2621440 | tf_op jit(solution)/shard_map/gate_up/all_to_all | solution.py:386
  160.3 7.0 %copy-start.17 = (f32[128,8]{0,1:T(8,128)S(1)}, f32[128,8]{0,1:T(8,128)}, u32[]{:S(2)}) copy-start(f32[128,8]{0,1:T(8,128)} %param.17) | copy-start | bytes 12292
  160.4 15.0 %all-to-all-start.5 = ((bf16[4,4,48,512]{3,2,1,0:T(8,128)(2,1)}), bf16[4,4,48,512]{3,2,1,0:T(8,128)(2,1)S(1)}, u32[]{:S(2)}, u32[]{:S(2)}) async-start(bf16[4,4,48,512]{3,2,1,0:T(8,128)(2,1)} %gate_up.1), calls=%async_computation.5 | async-start | bytes 1572864 | tf_op jit(solution)/shard_map/down/all_to_all | solution.py:386
  168.8 16.1 %copy-start.6 = (s32[3]{0:T(128)S(1)}, s32[3]{0:T(128)}, u32[]{:S(2)}) copy-start(s32[3]{0:T(128)} %copy-done.5) | copy-start | bytes 40
  175.4 9.5 %copy-start.3 = (bf16[768,256]{1,0:T(8,128)(2,1)S(1)}, bf16[768,256]{1,0:T(8,128)(2,1)}, u32[]{:S(2)}) copy-start(bf16[768,256]{1,0:T(8,128)(2,1)} %copy-done.2) | copy-start | bytes 1179652
  (11 other events, 27.0 us)

commit v5 on v4

--- a/solution.py
+++ b/solution.py
@@ -280,7 +280,8 @@
     next_ref,
     opp_ref,
     opp2_ref,
-    out_ref,
+    keep_ref,
+    send_ref,
     x_ref,
     w_ref,
     *,
@@ -337,7 +338,13 @@
         )
         found = jnp.dot(select, (result * weight).astype(bf16), preferred_element_type=f32)
         start = pl.multiple_of(block * width, width)
-        out_ref[:, :, :, pl.ds(start, width)] = found.astype(bf16).reshape(sides, -1, 16, width)
+        found = found.reshape(sides, -1, 16, width)
+        for p in range(2):
+            low, high = found[2 * p], found[2 * p + 1]
+            keep = jnp.where(place_ref[1] == 0, low, high).astype(bf16)
+            send = jnp.where(place_ref[1] == 0, high, low).astype(bf16)
+            keep_ref[:, p, :, pl.ds(start, width)] = keep
+            send_ref[:, p, :, pl.ds(start, width)] = send
 
 
 def local(
@@ -554,9 +561,10 @@
             name="activate",
         )
         line = 4 * sides
-        partial = run(
+        part = shape((n_chip // 2, 2, line, sides * feature_block))
+        keep, send = run(
             functools.partial(combine, capacity=capacity),
-            shape((4, n_chip // 2, line, sides * feature_block)),
+            [part, part],
             over_seq(active, along_y),
             w_down,
             *near_x,
@@ -570,7 +578,8 @@
         )
 
     with jax.named_scope("output"):
-        gathered = over_far(sum_near(partial))
+        paired = (keep.astype(f32) + lax.ppermute(send, "exp", swap).astype(f32)).astype(bf16)
+        gathered = over_chips(paired.reshape(n_chip, line, sides * feature_block))
         mixed = jnp.sum(gathered.astype(f32), axis=0).astype(bf16)
         mixed = over_seq(mixed.reshape(sides, 4, sides * feature_block), along_y)
         mixed = mixed.transpose(1, 0, 2).reshape(4, features)

time: 247 us -> 243 us (0.984)
  the two profiles are of different devices: /device:TPU:2 before, /device:TPU:32 now
where the time goes in v5:
time: 243 us; the launch traced here: 242 us
  blocking collectives  84.3 us (35%)
  starting transfers between devices  80 us (33%)
  waiting for transfers between devices  39.8 us (16%)
  Pallas kernels  17.8 us (7%)
  local copies, waits for them, and re-layouts  16.5 us (7%)
  other arithmetic  2.72 us (1%)
    all_to_all x1, blocking collectives, over_chips(): lax.all_to_all(value, 'exp', 0, 0, tiled=True, axis_index_groups=chips)  41 us
    all_to_all x2, starting transfers between devices, over_chips(): lax.all_to_all(value, 'exp', 0, 0, tiled=True, axis_index_groups=chips)  27.4 us
    all_to_all x4, waiting for transfers between devices, over_seq(): lax.all_to_all(value, 'seq', 0, 0, tiled=True, axis_index_groups=groups)  18.1 us
    pallas_call x8, Pallas kernels, run(): pl.pallas_call(body, out_shape=out_shape, in_specs=[smem] * len(placed) +...  17.8 us
    all_to_all x4, starting transfers between devices, over_seq(): lax.all_to_all(value, 'seq', 0, 0, tiled=True, axis_index_groups=groups)  17 us
    all_to_all x2, blocking collectives, over_seq(): lax.all_to_all(value, 'seq', 0, 0, tiled=True, axis_index_groups=groups)  16.9 us
    all_gather x1, blocking collectives, local(): lax.all_gather(lax.optimization_barrier((out_proj, kv))[0], 'seq', axis=0...  13.8 us
    all_gather x1, blocking collectives, local(): lax.all_gather(queries.transpose(1, 0, 2), 'seq', axis=0, tiled=True, axi...  12.6 us
  transfers between devices with their start and end apart: 18, of which 10 were waited for; matrix products, arithmetic and copies ran while one was open for 4% of the time, Pallas kernels for 1%

profile of v5, /device:TPU:32, one launch (start us, length us, event | category | flops | bytes accessed | tf_op | source)
XLA Modules:
  0.0 241.6 jit_solution(3176623218620240417)
XLA Ops:
  2.2 4.5 %all-to-all-start = ((bf16[4,2,384,128]{3,2,1,0:T(8,128)(2,1)}), bf16[4,2,384,128]{3,2,1,0:T(8,128)(2,1)S(1)}, u32[]{:S(2)}, u32[]{:S(2)}) async-start(bf16[4,2,384,128]{3,2,1,0:T(8,128)(2,1)} %broadcast_in_dim.21), calls=%async_computation | async-start | bytes 1572864 | tf_op jit(solution)/shard_map/key_values/all_to_all | solution.py:393
  6.7 12.6 %all_gather.6.q_ref = bf16[8,128,128]{2,1,0:T(8,128)(2,1)S(1)} all-gather(bf16[2,128,128]{2,1,0:T(8,128)(2,1)S(1)} %bitcast.44), channel_id=1, replica_groups={{0,32,64,96},{128,160,192,224},{256,288,320,352},{384,416,448,480},{1,3..., dimensions={0}, use_global_device_ids=true | all-gather | bytes 327680 | tf_op jit(solution)/shard_map/key_values/all_gather | solution.py:421
  19.4 4.4 %attend.1 = bf16[4,1056,128]{2,1,0:T(8,128)(2,1)} custom-call(s32[3]{0:T(128)S(1)} %pad_add_fusion.place_ref, bf16[8,128,128]{2,1,0:T(8,128)(2,1)S(1)} %all_gather.6.q_ref, bf16[4,2,384,128]{3,2,1,0:T(8,128)(2,1)S(1)} %all-to-all-done.kv_ref), custom_call_target="tpu_custom_call" | custom-call | flops 805306368 | bytes 786432 | tf_op jit(solution)/shard_map/attention/attend/pallas_call | solution.py:26
  23.8 4.0 %all-to-all-start.1 = ((bf16[4,1056,128]{2,1,0:T(8,128)(2,1)}), bf16[4,1056,128]{2,1,0:T(8,128)(2,1)S(1)}, u32[]{:S(2)}, u32[]{:S(2)}) async-start(bf16[4,1056,128]{2,1,0:T(8,128)(2,1)} %attend.1), calls=%async_computation.1 | async-start | bytes 2162688 | tf_op jit(solution)/shard_map/projection/all_to_all | solution.py:393
  27.8 13.8 %all_gather.7.w_ref = bf16[1024,256]{1,0:T(8,128)(2,1)S(1)} all-gather(bf16[256,256]{1,0:T(8,128)(2,1)S(1)} %copy-done.12), channel_id=1, replica_groups={{0,128,256,384},{32,160,288,416},{64,192,320,448},{96,224,352,480},{1,1..., dimensions={0}, use_global_device_ids=true | all-gather | bytes 655360 | tf_op jit(solution)/shard_map/attention/all_gather | solution.py:439
  48.6 15.3 %all-to-all-start.2 = ((bf16[16,128,128]{2,1,0:T(8,128)(2,1)}), bf16[16,128,128]{2,1,0:T(8,128)(2,1)S(1)}, u32[]{:S(2)}, u32[]{:S(2)}) async-start(bf16[16,128,128]{2,1,0:T(8,128)(2,1)} %add_convert_fusion.1), calls=%async_computation.2 | async-start | bytes 1048576 | tf_op jit(solution)/shard_map/projection/all_to_all | solution.py:390
  63.9 4.6 %collective-permute-start.4 = (bf16[2,768,256]{2,1,0:T(8,128)(2,1)}, bf16[2,768,256]{2,1,0:T(8,128)(2,1)S(1)}, u32[]{:S(2)}, u32[]{:S(2)}) collective-permute-start(bf16[2,768,256]{2,1,0:T(8,128)(2,1)} %own_ref.1), channel_id=1, source_target_pairs={{0,96},{32,0},{64,32},{96,64},{128,224},{160,128},{192,160},{224,1... | collective-permute-start | bytes 2359304 | tf_op jit(solution)/shard_map/projection/ppermute | solution.py:475
  74.1 2.9 %collective-permute-start.1 = (bf16[3,256,384]{2,1,0:T(8,128)(2,1)S(1)}, bf16[3,256,384]{2,1,0:T(8,128)(2,1)S(1)}, u32[]{:S(2)}, u32[]{:S(2)}) collective-permute-start(bf16[3,256,384]{2,1,0:T(8,128)(2,1)S(1)} %get-tuple-element.36), channel_id=1, source_target_pairs={{0,128},{32,160},{64,192},{96,224},{128,256},{160,288},{192,320},{... | collective-permute-start | bytes 1769480 | tf_op jit(solution)/shard_map/projection/ppermute | solution.py:474
  77.0 4.1 %collective-permute-start.2 = (bf16[3,256,384]{2,1,0:T(8,128)(2,1)S(1)}, bf16[3,256,384]{2,1,0:T(8,128)(2,1)S(1)}, u32[]{:S(2)}, u32[]{:S(2)}) collective-permute-start(bf16[3,256,384]{2,1,0:T(8,128)(2,1)S(1)} %get-tuple-element.37), channel_id=1, source_target_pairs={{0,384},{32,416},{64,448},{96,480},{128,0},{160,32},{192,64},{224,... | collective-permute-start | bytes 1769480 | tf_op jit(solution)/shard_map/projection/ppermute | solution.py:474
  81.2 2.2 collective-permute-start.5
  83.4 8.3 %collective-permute-done.1.prev_ref = bf16[3,256,384]{2,1,0:T(8,128)(2,1)S(1)} collective-permute-done((bf16[3,256,384]{2,1,0:T(8,128)(2,1)S(1)}, bf16[3,256,384]{2,1,0:T(8,128)(2,1)S(1)}, u32[]{:S(2)}, u32[]{:S(2)}) %collective-permute-start.1) | collective-permute-done | bytes 589856 | tf_op jit(solution)/shard_map/projection/ppermute | solution.py:474
  98.9 12.0 %all-to-all-start.3 = ((bf16[16,48,256]{2,1,0:T(8,128)(2,1)}), bf16[16,48,256]{2,1,0:T(8,128)(2,1)S(1)}, u32[]{:S(2)}, u32[]{:S(2)}) async-start(bf16[16,48,256]{2,1,0:T(8,128)(2,1)} %dispatch.1), calls=%async_computation.3 | async-start | bytes 786432 | tf_op jit(solution)/shard_map/gate_up/all_to_all | solution.py:390
  111.0 4.9 %collective-permute-start.8 = (bf16[768,256]{1,0:T(8,128)(2,1)S(1)}, bf16[768,256]{1,0:T(8,128)(2,1)S(1)}, u32[]{:S(2)}, u32[]{:S(2)}) collective-permute-start(bf16[768,256]{1,0:T(8,128)(2,1)S(1)} %slice_bitcast_fusion), channel_id=1, source_target_pairs={{0,96},{32,0},{64,32},{96,64},{128,224},{160,128},{192,160},{224,1... | collective-permute-start | bytes 1179656 | tf_op jit(solution)/shard_map/gate_up/ppermute | solution.py:504
  119.7 5.3 %collective-permute-start.10 = (bf16[256,384]{1,0:T(8,128)(2,1)S(1)}, bf16[256,384]{1,0:T(8,128)(2,1)S(1)}, u32[]{:S(2)}, u32[]{:S(2)}) collective-permute-start(bf16[256,384]{1,0:T(8,128)(2,1)S(1)} %slice_bitcast_fusion.2), channel_id=1, source_target_pairs={{0,384},{32,416},{64,448},{96,480},{128,0},{160,32},{192,64},{224,... | collective-permute-start | bytes 589832 | tf_op jit(solution)/shard_map/gate_up/ppermute | solution.py:500
  128.7 5.3 %collective-permute-done.9.opp_ref = bf16[256,384]{1,0:T(8,128)(2,1)S(1)} collective-permute-done((bf16[256,384]{1,0:T(8,128)(2,1)S(1)}, bf16[256,384]{1,0:T(8,128)(2,1)S(1)}, u32[]{:S(2)}, u32[]{:S(2)}) %collective-permute-start.9) | collective-permute-done | bytes 196640 | tf_op jit(solution)/shard_map/gate_up/ppermute | solution.py:499
  135.9 4.4 %all-to-all-start.4 = ((bf16[4,4,160,256]{3,2,1,0:T(8,128)(2,1)}), bf16[4,4,160,256]{3,2,1,0:T(8,128)(2,1)}, u32[]{:S(2)}, u32[]{:S(2)}) async-start(bf16[4,4,160,256]{3,2,1,0:T(8,128)(2,1)} %broadcast_in_dim.23), calls=%async_computation.4 | async-start | bytes 2621440 | tf_op jit(solution)/shard_map/gate_up/all_to_all | solution.py:393
  141.8 15.0 %all-to-all-done.4.x_ref = bf16[4,4,160,256]{3,2,1,0:T(8,128)(2,1)} async-done(((bf16[4,4,160,256]{3,2,1,0:T(8,128)(2,1)}), bf16[4,4,160,256]{3,2,1,0:T(8,128)(2,1)}, u32[]{:S(2)}, u32[]{:S(2)}) %all-to-all-start.4) | async-done | bytes 1310752 | tf_op jit(solution)/shard_map/gate_up/all_to_all | solution.py:393
  156.9 5.3 %gate_up.1 = bf16[4,4,48,512]{3,2,1,0:T(8,128)(2,1)} custom-call(s32[3]{0:T(128)} %copy-done.5, bf16[4,4,160,256]{3,2,1,0:T(8,128)(2,1)} %all-to-all-done.4.x_ref, bf16[4,4,8,256]{3,2,1,0:T(8,128)(2,1)} %slice.29.state_ref, f32[4,1,256]{2,1,0:T(1,128)} %dynamic-slice_bitcast_fusion.gain_ref, bf16[2,256,384]{2,1,0:T(8,128)(2,1)} %copy-done.2, ...), custom_call_target="tpu_custom_call" | custom-call | tf_op jit(solution)/shard_map/gate_up/gate_up/pallas_call | solution.py:26
  162.2 4.1 %all-to-all-start.5 = ((bf16[4,4,48,512]{3,2,1,0:T(8,128)(2,1)}), bf16[4,4,48,512]{3,2,1,0:T(8,128)(2,1)S(1)}, u32[]{:S(2)}, u32[]{:S(2)}) async-start(bf16[4,4,48,512]{3,2,1,0:T(8,128)(2,1)} %gate_up.1), calls=%async_computation.5 | async-start | bytes 1572864 | tf_op jit(solution)/shard_map/down/all_to_all | solution.py:393
  173.3 2.6 %all-to-all-done.5.got_ref = bf16[4,4,48,512]{3,2,1,0:T(8,128)(2,1)S(1)} async-done(((bf16[4,4,48,512]{3,2,1,0:T(8,128)(2,1)}), bf16[4,4,48,512]{3,2,1,0:T(8,128)(2,1)S(1)}, u32[]{:S(2)}, u32[]{:S(2)}) %all-to-all-start.5) | async-done | bytes 786464 | tf_op jit(solution)/shard_map/down/all_to_all | solution.py:393
  176.2 9.1 %all_to_all.45.got_ref = bf16[4,272,128]{2,1,0:T(8,128)(2,1)S(1)} all-to-all(bf16[4,272,128]{2,1,0:T(8,128)(2,1)S(1)} %get-tuple-element.52), channel_id=1, replica_groups={{0,128,256,384},{32,160,288,416},{64,192,320,448},{96,224,352,480},{1,1..., dimensions={0} | all-to-all | bytes 557056 | tf_op jit(solution)/shard_map/down/all_to_all | solution.py:393
  185.3 2.7 %combine.1 = (bf16[8,2,16,1024]{3,2,1,0:T(8,128)(2,1)S(1)}, bf16[8,2,16,1024]{3,2,1,0:T(8,128)(2,1)S(1)}) custom-call(s32[3]{0:T(128)S(1)} %copy-done.6, bf16[4,272,128]{2,1,0:T(8,128)(2,1)S(1)} %all_to_all.45.got_ref, bf16[2,768,256]{2,1,0:T(8,128)(2,1)} %own_ref.1, bf16[2,768,256]{2,1,0:T(8,128)(2,1)S(1)} %collective-permute-done.3.prev_ref, ...), custom_call_target="tpu_custom_call" | custom-call | tf_op jit(solution)/shard_map/down/combine/pallas_call | solution.py:26
  192.1 41.0 %all_to_all.46 = bf16[16,16,1024]{2,1,0:T(8,128)(2,1)S(1)} all-to-all(bf16[16,16,1024]{2,1,0:T(8,128)(2,1)S(1)} %bitcast.39), channel_id=1, replica_groups={{0,2,4,6,8,10,12,14,16,18,20,22,24,26,28,30},{1,3,5,7,9,11,13,15,17,19,..., dimensions={0} | all-to-all | bytes 1048576 | tf_op jit(solution)/shard_map/output/all_to_all | solution.py:390
  233.1 7.8 %all_to_all.47 = bf16[4,4,1024]{2,1,0:T(4,128)(2,1)S(1)} all-to-all(bf16[4,4,1024]{2,1,0:T(4,128)(2,1)S(1)} %reshape.216), channel_id=1, replica_groups={{0,128,256,384},{32,160,288,416},{64,192,320,448},{96,224,352,480},{1,1..., dimensions={0} | all-to-all | bytes 65536 | tf_op jit(solution)/shard_map/output/all_to_all | solution.py:393
  (116 shorter events, 44.5 us)
Async XLA Ops:
  2.2 17.2 %all-to-all-start = ((bf16[4,2,384,128]{3,2,1,0:T(8,128)(2,1)}), bf16[4,2,384,128]{3,2,1,0:T(8,128)(2,1)S(1)}, u32[]{:S(2)}, u32[]{:S(2)}) async-start(bf16[4,2,384,128]{3,2,1,0:T(8,128)(2,1)} %broadcast_in_dim.21), calls=%async_computation | async-start | bytes 1572864 | tf_op jit(solution)/shard_map/key_values/all_to_all | solution.py:393
  19.4 77.8 %copy-start.5 = (s32[3]{0:T(128)}, s32[3]{0:T(128)S(1)}, u32[]{:S(2)}) copy-start(s32[3]{0:T(128)S(1)} %pad_add_fusion.place_ref) | copy-start | bytes 40
  23.8 18.2 %all-to-all-start.1 = ((bf16[4,1056,128]{2,1,0:T(8,128)(2,1)}), bf16[4,1056,128]{2,1,0:T(8,128)(2,1)S(1)}, u32[]{:S(2)}, u32[]{:S(2)}) async-start(bf16[4,1056,128]{2,1,0:T(8,128)(2,1)} %attend.1), calls=%async_computation.1 | async-start | bytes 2162688 | tf_op jit(solution)/shard_map/projection/all_to_all | solution.py:393
  43.8 3.8 %collective-permute-start = (bf16[16,128,128]{2,1,0:T(8,128)(2,1)S(1)}, bf16[16,128,128]{2,1,0:T(8,128)(2,1)S(1)}, u32[]{:S(2)}, u32[]{:S(2)}) collective-permute-start(bf16[16,128,128]{2,1,0:T(8,128)(2,1)S(1)} %get-tuple-element.34), channel_id=1, source_target_pairs={{0,1},{1,0},{2,3},{3,2},{4,5},{5,4},{6,7},{7,6},{8,9},{9,8},{10,11... | collective-permute-start | bytes 1572872 | tf_op jit(solution)/shard_map/projection/ppermute | solution.py:458
  48.6 32.6 %copy-start.15 = (s32[128,8]{0,1:T(8,128)S(1)}, s32[128,8]{0,1:T(8,128)}, u32[]{:S(2)}) copy-start(s32[128,8]{0,1:T(8,128)} %param.16) | copy-start | bytes 12292
  48.6 32.6 %copy-start.14 = (bf16[128,128]{1,0:T(8,128)(2,1)S(1)}, bf16[128,128]{1,0:T(8,128)(2,1)}, u32[]{:S(2)}) copy-start(bf16[128,128]{1,0:T(8,128)(2,1)} %param.14) | copy-start | bytes 98308
  48.6 45.4 %all-to-all-start.2 = ((bf16[16,128,128]{2,1,0:T(8,128)(2,1)}), bf16[16,128,128]{2,1,0:T(8,128)(2,1)S(1)}, u32[]{:S(2)}, u32[]{:S(2)}) async-start(bf16[16,128,128]{2,1,0:T(8,128)(2,1)} %add_convert_fusion.1), calls=%async_computation.2 | async-start | bytes 1048576 | tf_op jit(solution)/shard_map/projection/all_to_all | solution.py:390
  63.9 29.3 %collective-permute-start.4 = (bf16[2,768,256]{2,1,0:T(8,128)(2,1)}, bf16[2,768,256]{2,1,0:T(8,128)(2,1)S(1)}, u32[]{:S(2)}, u32[]{:S(2)}) collective-permute-start(bf16[2,768,256]{2,1,0:T(8,128)(2,1)} %own_ref.1), channel_id=1, source_target_pairs={{0,96},{32,0},{64,32},{96,64},{128,224},{160,128},{192,160},{224,1... | collective-permute-start | bytes 2359304 | tf_op jit(solution)/shard_map/projection/ppermute | solution.py:475
  68.6 25.4 %collective-permute-start.3 = (bf16[2,768,256]{2,1,0:T(8,128)(2,1)}, bf16[2,768,256]{2,1,0:T(8,128)(2,1)S(1)}, u32[]{:S(2)}, u32[]{:S(2)}) collective-permute-start(bf16[2,768,256]{2,1,0:T(8,128)(2,1)} %own_ref.1), channel_id=1, source_target_pairs={{0,32},{32,64},{64,96},{96,0},{128,160},{160,192},{192,224},{224,1... | collective-permute-start | bytes 2359304 | tf_op jit(solution)/shard_map/projection/ppermute | solution.py:475
  74.1 17.6 %collective-permute-start.1 = (bf16[3,256,384]{2,1,0:T(8,128)(2,1)S(1)}, bf16[3,256,384]{2,1,0:T(8,128)(2,1)S(1)}, u32[]{:S(2)}, u32[]{:S(2)}) collective-permute-start(bf16[3,256,384]{2,1,0:T(8,128)(2,1)S(1)} %get-tuple-element.36), channel_id=1, source_target_pairs={{0,128},{32,160},{64,192},{96,224},{128,256},{160,288},{192,320},{... | collective-permute-start | bytes 1769480 | tf_op jit(solution)/shard_map/projection/ppermute | solution.py:474
  77.0 16.1 %collective-permute-start.2 = (bf16[3,256,384]{2,1,0:T(8,128)(2,1)S(1)}, bf16[3,256,384]{2,1,0:T(8,128)(2,1)S(1)}, u32[]{:S(2)}, u32[]{:S(2)}) collective-permute-start(bf16[3,256,384]{2,1,0:T(8,128)(2,1)S(1)} %get-tuple-element.37), channel_id=1, source_target_pairs={{0,384},{32,416},{64,448},{96,480},{128,0},{160,32},{192,64},{224,... | collective-permute-start | bytes 1769480 | tf_op jit(solution)/shard_map/projection/ppermute | solution.py:474
  81.2 12.8 %collective-permute-start.5 = (bf16[136,128]{1,0:T(8,128)(2,1)S(1)}, bf16[136,128]{1,0:T(8,128)(2,1)S(1)}, u32[]{:S(2)}, u32[]{:S(2)}) collective-permute-start(bf16[136,128]{1,0:T(8,128)(2,1)S(1)} %pad_maximum_fusion), channel_id=1, source_target_pairs={{0,0},{1,1},{32,2},{33,3},{64,4},{65,5},{96,6},{97,7},{8,8},{9,9},... | collective-permute-start | bytes 104456 | tf_op jit(solution)/shard_map/turn_residual/ppermute | solution.py:413
  94.1 3.1 %collective-permute-start.6 = (bf16[136,128]{1,0:T(8,128)(2,1)S(1)}, bf16[136,128]{1,0:T(8,128)(2,1)S(1)}, u32[]{:S(2)}, u32[]{:S(2)}) collective-permute-start(bf16[136,128]{1,0:T(8,128)(2,1)S(1)} %add_state.1.own_ref), channel_id=1, source_target_pairs={{0,1},{1,0},{2,3},{3,2},{4,5},{5,4},{6,7},{7,6},{8,9},{9,8},{10,11... | collective-permute-start | bytes 104456 | tf_op jit(solution)/shard_map/projection/ppermute | solution.py:484
  98.9 35.8 %all-to-all-start.3 = ((bf16[16,48,256]{2,1,0:T(8,128)(2,1)}), bf16[16,48,256]{2,1,0:T(8,128)(2,1)S(1)}, u32[]{:S(2)}, u32[]{:S(2)}) async-start(bf16[16,48,256]{2,1,0:T(8,128)(2,1)} %dispatch.1), calls=%async_computation.3 | async-start | bytes 786432 | tf_op jit(solution)/shard_map/gate_up/all_to_all | solution.py:390
  111.0 23.0 %collective-permute-start.8 = (bf16[768,256]{1,0:T(8,128)(2,1)S(1)}, bf16[768,256]{1,0:T(8,128)(2,1)S(1)}, u32[]{:S(2)}, u32[]{:S(2)}) collective-permute-start(bf16[768,256]{1,0:T(8,128)(2,1)S(1)} %slice_bitcast_fusion), channel_id=1, source_target_pairs={{0,96},{32,0},{64,32},{96,64},{128,224},{160,128},{192,160},{224,1... | collective-permute-start | bytes 1179656 | tf_op jit(solution)/shard_map/gate_up/ppermute | solution.py:504
  115.9 18.8 %collective-permute-start.7 = (bf16[768,256]{1,0:T(8,128)(2,1)S(1)}, bf16[768,256]{1,0:T(8,128)(2,1)S(1)}, u32[]{:S(2)}, u32[]{:S(2)}) collective-permute-start(bf16[768,256]{1,0:T(8,128)(2,1)S(1)} %slice_bitcast_fusion.1), channel_id=1, source_target_pairs={{0,32},{32,64},{64,96},{96,0},{128,160},{160,192},{192,224},{224,1... | collective-permute-start | bytes 1179656 | tf_op jit(solution)/shard_map/gate_up/ppermute | solution.py:503
  119.7 9.0 %collective-permute-start.10 = (bf16[256,384]{1,0:T(8,128)(2,1)S(1)}, bf16[256,384]{1,0:T(8,128)(2,1)S(1)}, u32[]{:S(2)}, u32[]{:S(2)}) collective-permute-start(bf16[256,384]{1,0:T(8,128)(2,1)S(1)} %slice_bitcast_fusion.2), channel_id=1, source_target_pairs={{0,384},{32,416},{64,448},{96,480},{128,0},{160,32},{192,64},{224,... | collective-permute-start | bytes 589832 | tf_op jit(solution)/shard_map/gate_up/ppermute | solution.py:500
  125.0 9.0 %collective-permute-start.9 = (bf16[256,384]{1,0:T(8,128)(2,1)S(1)}, bf16[256,384]{1,0:T(8,128)(2,1)S(1)}, u32[]{:S(2)}, u32[]{:S(2)}) collective-permute-start(bf16[256,384]{1,0:T(8,128)(2,1)S(1)} %slice_bitcast_fusion.3), channel_id=1, source_target_pairs={{0,128},{32,160},{64,192},{96,224},{128,256},{160,288},{192,320},{... | collective-permute-start | bytes 589832 | tf_op jit(solution)/shard_map/gate_up/ppermute | solution.py:499
  128.7 7.2 %copy-start.9 = (bf16[256,384]{1,0:T(8,128)(2,1)}, bf16[256,384]{1,0:T(8,128)(2,1)S(1)}, u32[]{:S(2)}) copy-start(bf16[256,384]{1,0:T(8,128)(2,1)S(1)} %collective-permute-done.10.opp2_ref) | copy-start | bytes 589828
  135.9 21.0 %all-to-all-start.4 = ((bf16[4,4,160,256]{3,2,1,0:T(8,128)(2,1)}), bf16[4,4,160,256]{3,2,1,0:T(8,128)(2,1)}, u32[]{:S(2)}, u32[]{:S(2)}) async-start(bf16[4,4,160,256]{3,2,1,0:T(8,128)(2,1)} %broadcast_in_dim.23), calls=%async_computation.4 | async-start | bytes 2621440 | tf_op jit(solution)/shard_map/gate_up/all_to_all | solution.py:393
  162.2 13.6 %all-to-all-start.5 = ((bf16[4,4,48,512]{3,2,1,0:T(8,128)(2,1)}), bf16[4,4,48,512]{3,2,1,0:T(8,128)(2,1)S(1)}, u32[]{:S(2)}, u32[]{:S(2)}) async-start(bf16[4,4,48,512]{3,2,1,0:T(8,128)(2,1)} %gate_up.1), calls=%async_computation.5 | async-start | bytes 1572864 | tf_op jit(solution)/shard_map/down/all_to_all | solution.py:393
  167.8 17.5 %copy-start.6 = (s32[3]{0:T(128)S(1)}, s32[3]{0:T(128)}, u32[]{:S(2)}) copy-start(s32[3]{0:T(128)} %copy-done.5) | copy-start | bytes 40
  175.9 9.5 %copy-start.4 = (bf16[768,256]{1,0:T(8,128)(2,1)S(1)}, bf16[768,256]{1,0:T(8,128)(2,1)}, u32[]{:S(2)}) copy-start(bf16[768,256]{1,0:T(8,128)(2,1)} %copy-done.3) | copy-start | bytes 1179652
  188.1 3.8 %collective-permute-start.11 = (bf16[8,2,16,1024]{3,2,1,0:T(8,128)(2,1)S(1)}, bf16[8,2,16,1024]{3,2,1,0:T(8,128)(2,1)S(1)}, u32[]{:S(2)}, u32[]{:S(2)}) collective-permute-start(bf16[8,2,16,1024]{3,2,1,0:T(8,128)(2,1)S(1)} %get-tuple-element.56), channel_id=1, source_target_pairs={{0,1},{1,0},{2,3},{3,2},{4,5},{5,4},{6,7},{7,6},{8,9},{9,8},{10,11... | collective-permute-start | bytes 1572872 | tf_op jit(solution)/shard_map/output/ppermute | solution.py:581
  (12 other events, 26.3 us)
